TPU v7x, 32 devices: a whole 2x2x4 slice. The times are simulated.
32 devices in a mesh: groups: 2 (over x), wide: 16 (over z, y, core).
Axes of the slice: x: 2, y: 2, z: 4, core: 2. Of those that a mesh axis runs over, the one named last changes fastest.
Arguments:
- pair: bfloat16 [512, 256, 128], P(('groups', 'wide')), parts along dimension 0, may hold values from -6 to 6
- residue_mask: int32 [512], P('groups'), parts along dimension 0, may hold values from 0 to 1, as said below
- input_gain: float32 [128], replicated, may hold values from 0.25 to 1.75
- left_gate: bfloat16 [128, 128], replicated, may hold values from -0.5 to 0.5
- left_value: bfloat16 [128, 128], replicated, may hold values from -0.5 to 0.5
- right_gate: bfloat16 [128, 128], replicated, may hold values from -0.5 to 0.5
- right_value: bfloat16 [128, 128], replicated, may hold values from -0.5 to 0.5
- middle_gain: float32 [128], replicated, may hold values from 0.25 to 1.75
- output_gate: bfloat16 [128, 128], replicated, may hold values from -0.5 to 0.5
- output_value: bfloat16 [128, 128], replicated, may hold values from -0.5 to 0.5
Outputs:
- pair_next: bfloat16 [512, 256, 128], P('groups', 'wide'), parts along dimension 0
There are 2 independent parts, one for each index of `groups`. A program takes and returns all parts, laid end to end along the dimension named above; an argument that names none is the same for every part. Nothing has to cross between parts.
Inputs may be any that keep to these rules, and one draw needn't show every extreme that they name: `residue_mask`: 1 on a leading run of residues of length 128 or more and 0 after it; the last residue is always 0.
All inputs are finite; a program needn't handle non-finite values.
Results may differ from a plain program's by a relative error of at most 0.0035.
Values may be sent and summed in bfloat16 or wider, within the bound.
No kernel may reach another device: no remote copies, remote signals or barrier semaphores. Data moves between devices by JAX's collectives and lax.ppermute only.
A program may use at most 64 MiB of HBM per device.

v0:
```python
import jax
import jax.numpy as jnp
from jax import lax
from jax.sharding import PartitionSpec as P


def layer_norm(values, gain, axis):
    mean_value = jnp.mean(values, axis=axis, keepdims=True)
    centred = values - mean_value
    variance = jnp.mean(centred * centred, axis=axis, keepdims=True)
    return centred * lax.rsqrt(variance + 1e-05) * gain


def edge_side(normed, gate_weight, value_weight, pair_mask):
    gated = jnp.einsum("ikc,ch->hik", normed, gate_weight, preferred_element_type=jnp.float32)
    valued = jnp.einsum("ikc,ch->hik", normed, value_weight, preferred_element_type=jnp.float32)
    return (jax.nn.sigmoid(gated) * valued * pair_mask[None, :, :]).astype(jnp.bfloat16)


def finish_update(triangle_back, normed, base_pair, middle_gain, output_gate, output_value):
    middle = layer_norm(triangle_back.astype(jnp.float32), middle_gain[:, None, None], 0).astype(
        jnp.bfloat16
    )
    projected = jnp.einsum("hij,hc->ijc", middle, output_value, preferred_element_type=jnp.float32)
    gating = jax.nn.sigmoid(
        jnp.einsum("ijc,cd->ijd", normed, output_gate, preferred_element_type=jnp.float32)
    )
    return (base_pair.astype(jnp.float32) + gating * projected).astype(jnp.bfloat16)


def shards(
    pair,
    residue_mask,
    input_gain,
    left_gate,
    left_value,
    right_gate,
    right_value,
    middle_gain,
    output_gate,
    output_value,
):
    row_count = pair.shape[0]
    row_start = lax.axis_index("wide") * row_count
    chain_mask = residue_mask.astype(jnp.float32)
    own_mask = lax.dynamic_slice_in_dim(chain_mask, row_start, row_count, 0)
    pair_mask = own_mask[:, None] * chain_mask[None, :]
    normed = layer_norm(pair.astype(jnp.float32), input_gain, 2).astype(jnp.bfloat16)
    left_edges = edge_side(normed, left_gate, left_value, pair_mask)
    right_edges = edge_side(normed, right_gate, right_value, pair_mask)
    left_full, right_full = (
        lax.all_to_all(left_edges, "wide", split_axis=0, concat_axis=1, tiled=True),
        lax.all_to_all(right_edges, "wide", split_axis=0, concat_axis=1, tiled=True),
    )
    triangle = jnp.einsum(
        "cik,cjk->cij", left_full, right_full, preferred_element_type=jnp.float32
    ).astype(jnp.bfloat16)
    triangle_rows = lax.all_to_all(triangle, "wide", split_axis=1, concat_axis=0, tiled=True)
    updated_rows = finish_update(
        triangle_rows, normed, pair, middle_gain, output_gate, output_value
    )
    return lax.all_to_all(updated_rows, "wide", split_axis=1, concat_axis=0, tiled=True)


def solution(mesh):
    in_specs = (
        P(("groups", "wide"), None, None),
        P("groups"),
        P(),
        P(),
        P(),
        P(),
        P(),
        P(),
        P(),
        P(),
    )
    out_specs = P("groups", "wide", None)
    return jax.shard_map(shards, mesh=mesh, in_specs=in_specs, out_specs=out_specs, check_vma=False)
```

profile of v0, /device:TPU:0, one launch (start us, length us, event | category | flops | bytes accessed | tf_op | source)
XLA Modules:
  0.0 141.2 jit_solution(17950312006780872993)
XLA Ops:
  0.0 0.8 convert_element_type.45
  0.8 1.6 %convert_reduce_fusion = f32[16,256]{1,0:T(8,128)S(1)} fusion(bf16[16,256,128]{2,1,0:T(8,128)(2,1)} %param.10), kind=kLoop, calls=%fused_computation.2 | loop fusion | flops 1044480 | bytes 1064960 | tf_op jit(solution)/shard_map/reduce_sum | solution.py:8
  2.4 2.3 %fusion.2 = f32[16,256]{1,0:T(8,128)S(1)} fusion(bf16[16,256,128]{2,1,0:T(8,128)(2,1)} %param.10, f32[16,256]{1,0:T(8,128)S(1)} %broadcast_multiply_fusion.2), kind=kLoop, calls=%fused_computation.5 | loop fusion | flops 2093056 | bytes 1081344 | tf_op jit(solution)/shard_map/reduce_sum | solution.py:10
  4.9 1.5 %fusion.15 = f32[16,256,128]{2,1,0:T(8,128)S(1)} fusion(bf16[128,128]{1,0:T(8,128)(2,1)S(1)} %copy-done, bf16[16,256,128]{2,1,0:T(8,128)(2,1)S(1)} %copy-done.1, f32[128]{0:T(128)S(1)} %copy-done.5, f32[16,256]{1,0:T(8,128)S(1)} %get-tuple-element.7, f32[16,256]{1,0:T(8,128)S(1)} %broadcast_multiply_fusion.2), kind=kOutput, calls=%fused_computation.24 | convolution fusion | flops 136839168 | bytes 3211776 | tf_op jit(solution)/shard_map/ikc,ch->hik/dot_general | solution.py:15
  6.4 2.1 %fusion.10 = bf16[128,16,256]{0,2,1:T(8,128)(2,1)S(1)} fusion(f32[16,256,128]{2,1,0:T(8,128)S(1)} %fusion.15, f32[16,256]{1,0:T(8,128)S(1)} %get-tuple-element.8, bf16[128,128]{1,0:T(8,128)(2,1)S(1)} %copy-done.7, bf16[16,256,128]{2,1,0:T(8,128)(2,1)S(1)} %copy-done.1, f32[128]{0:T(128)S(1)} %copy-done.5, f32[16,256]{1,0:T(8,128)S(1)} %get-tuple-element.7, ...), kind=kOutput, calls=%fused_computation.19 | convolution fusion | flops 139984896 | bytes 4276736 | tf_op jit(solution)/shard_map/ikc,ch->hik/dot_general | solution.py:16
  8.5 1.7 %copy.32 = bf16[128,16,256]{2,1,0:T(8,128)(2,1)} copy(bf16[128,16,256]{0,2,1:T(8,128)(2,1)S(1)} %fusion.10) | data formatting | bytes 2097152 | tf_op jit(solution)/shard_map/convert_element_type | solution.py:17
  10.2 7.4 %all-to-all-start.1 = ((bf16[128,16,256]{2,1,0:T(8,128)(2,1)}), bf16[128,16,256]{2,1,0:T(8,128)(2,1)S(1)}, u32[]{:S(2)}, u32[]{:S(2)}) async-start(bf16[128,16,256]{2,1,0:T(8,128)(2,1)} %copy.32), calls=%async_computation.1 | async-start | bytes 2097152 | tf_op jit(solution)/shard_map/all_to_all | solution.py:53
  17.6 1.5 %fusion.18 = f32[16,256,128]{2,1,0:T(8,128)S(1)} fusion(bf16[128,128]{1,0:T(8,128)(2,1)S(1)} %copy-done.3, bf16[16,256,128]{2,1,0:T(8,128)(2,1)S(1)} %copy-done.1, f32[128]{0:T(128)S(1)} %copy-done.5, f32[16,256]{1,0:T(8,128)S(1)} %get-tuple-element.7, f32[16,256]{1,0:T(8,128)S(1)} %broadcast_multiply_fusion.2), kind=kOutput, calls=%fused_computation.27 | convolution fusion | flops 136839168 | bytes 3211776 | tf_op jit(solution)/shard_map/ikc,ch->hik/dot_general | solution.py:15
  19.1 2.1 %fusion.9 = bf16[128,16,256]{0,2,1:T(8,128)(2,1)S(1)} fusion(f32[16,256,128]{2,1,0:T(8,128)S(1)} %fusion.18, f32[16,256]{1,0:T(8,128)S(1)} %get-tuple-element.8, bf16[128,128]{1,0:T(8,128)(2,1)S(1)} %copy-done.8, bf16[16,256,128]{2,1,0:T(8,128)(2,1)S(1)} %copy-done.1, f32[128]{0:T(128)S(1)} %copy-done.5, f32[16,256]{1,0:T(8,128)S(1)} %get-tuple-element.7, ...), kind=kOutput, calls=%fused_computation.18 | convolution fusion | flops 139984896 | bytes 4276736 | tf_op jit(solution)/shard_map/ikc,ch->hik/dot_general | solution.py:16
  21.2 1.7 %copy.30 = bf16[128,16,256]{2,1,0:T(8,128)(2,1)} copy(bf16[128,16,256]{0,2,1:T(8,128)(2,1)S(1)} %fusion.9) | data formatting | bytes 2097152 | tf_op jit(solution)/shard_map/convert_element_type | solution.py:17
  22.8 17.7 %all-to-all-done.1 = bf16[128,16,256]{2,1,0:T(8,128)(2,1)S(1)} async-done(((bf16[128,16,256]{2,1,0:T(8,128)(2,1)}), bf16[128,16,256]{2,1,0:T(8,128)(2,1)S(1)}, u32[]{:S(2)}, u32[]{:S(2)}) %all-to-all-start.1) | async-done | bytes 1048608 | tf_op jit(solution)/shard_map/all_to_all | solution.py:53
  40.5 6.9 %all-to-all-start = ((bf16[128,16,256]{2,1,0:T(8,128)(2,1)}), bf16[128,16,256]{2,1,0:T(8,128)(2,1)}, u32[]{:S(2)}, u32[]{:S(2)}) async-start(bf16[128,16,256]{2,1,0:T(8,128)(2,1)} %copy.30), calls=%async_computation | async-start | bytes 2097152 | tf_op jit(solution)/shard_map/all_to_all | solution.py:52
  47.5 22.9 %all-to-all-done = bf16[128,16,256]{2,1,0:T(8,128)(2,1)} async-done(((bf16[128,16,256]{2,1,0:T(8,128)(2,1)}), bf16[128,16,256]{2,1,0:T(8,128)(2,1)}, u32[]{:S(2)}, u32[]{:S(2)}) %all-to-all-start) | async-done | bytes 1048608 | tf_op jit(solution)/shard_map/all_to_all | solution.py:52
  70.4 1.3 copy.31
  71.7 0.5 convolution_convert_fusion
  72.2 1.6 %copy.34 = bf16[8,256,256]{2,0,1:T(8,128)(2,1)} copy(bf16[8,256,256]{2,1,0:T(8,128)(2,1)S(1)} %convolution_convert_fusion) | data formatting | bytes 2097152 | tf_op jit(solution)/shard_map/convert_element_type | solution.py:57
  73.8 6.9 %all-to-all-start.2 = ((bf16[8,256,256]{2,0,1:T(8,128)(2,1)}), bf16[8,256,256]{2,0,1:T(8,128)(2,1)S(1)}, u32[]{:S(2)}, u32[]{:S(2)}) async-start(bf16[8,256,256]{2,0,1:T(8,128)(2,1)} %copy.34), calls=%async_computation.2 | async-start | bytes 2097152 | tf_op jit(solution)/shard_map/all_to_all | solution.py:58
  80.7 2.5 %fusion.20 = f32[16,256,128]{2,1,0:T(8,128)} fusion(bf16[128,128]{1,0:T(8,128)(2,1)S(1)} %copy-done.4, bf16[16,256,128]{2,1,0:T(8,128)(2,1)S(1)} %copy-done.1, f32[128]{0:T(128)S(1)} %copy-done.5, f32[16,256]{1,0:T(8,128)S(1)} %get-tuple-element.7, f32[16,256]{1,0:T(8,128)S(1)} %broadcast_multiply_fusion.2), kind=kOutput, calls=%fused_computation.29 | convolution fusion | flops 136839168 | bytes 3211776 | tf_op jit(solution)/shard_map/ijc,cd->ijd/dot_general | solution.py:26
  83.2 20.4 %all-to-all-done.2 = bf16[8,256,256]{2,0,1:T(8,128)(2,1)S(1)} async-done(((bf16[8,256,256]{2,0,1:T(8,128)(2,1)}), bf16[8,256,256]{2,0,1:T(8,128)(2,1)S(1)}, u32[]{:S(2)}, u32[]{:S(2)}) %all-to-all-start.2) | async-done | bytes 1048608 | tf_op jit(solution)/shard_map/all_to_all | solution.py:58
  105.4 1.3 copy-done.2
  106.7 1.0 fusion.5
  107.7 0.7 copy.38
  108.4 31.5 %all_to_all.63 = bf16[16,256,128]{2,0,1:T(8,128)(2,1)S(1)} all-to-all(bf16[16,256,128]{2,0,1:T(8,128)(2,1)S(1)} %copy.38), channel_id=1, replica_groups=mesh['groups'=2,'wide'=16] {'wide'}, dimensions={1} | all-to-all | bytes 2097152 | tf_op jit(solution)/shard_map/all_to_all | solution.py:62
  139.9 1.2 copy.39
  (30 shorter events, 2.0 us)
Async XLA Ops:
  0.0 4.9 %copy-start = (bf16[128,128]{1,0:T(8,128)(2,1)S(1)}, bf16[128,128]{1,0:T(8,128)(2,1)}, u32[]{:S(2)}) copy-start(bf16[128,128]{1,0:T(8,128)(2,1)} %param.15) | copy-start | bytes 98308
  0.0 4.9 %copy-start.1 = (bf16[16,256,128]{2,1,0:T(8,128)(2,1)S(1)}, bf16[16,256,128]{2,1,0:T(8,128)(2,1)}, u32[]{:S(2)}) copy-start(bf16[16,256,128]{2,1,0:T(8,128)(2,1)} %param.10) | copy-start | bytes 3145732
  0.0 4.9 %copy-start.5 = (f32[128]{0:T(128)S(1)}, f32[128]{0:T(128)}, u32[]{:S(2)}) copy-start(f32[128]{0:T(128)} %param.12) | copy-start | bytes 1540
  2.4 4.0 %copy-start.7 = (bf16[128,128]{1,0:T(8,128)(2,1)S(1)}, bf16[128,128]{1,0:T(8,128)(2,1)}, u32[]{:S(2)}) copy-start(bf16[128,128]{1,0:T(8,128)(2,1)} %param.16) | copy-start | bytes 98308
  8.4 9.1 %copy-start.3 = (bf16[128,128]{1,0:T(8,128)(2,1)S(1)}, bf16[128,128]{1,0:T(8,128)(2,1)}, u32[]{:S(2)}) copy-start(bf16[128,128]{1,0:T(8,128)(2,1)} %param.13) | copy-start | bytes 98308
  10.2 30.3 %all-to-all-start.1 = ((bf16[128,16,256]{2,1,0:T(8,128)(2,1)}), bf16[128,16,256]{2,1,0:T(8,128)(2,1)S(1)}, u32[]{:S(2)}, u32[]{:S(2)}) async-start(bf16[128,16,256]{2,1,0:T(8,128)(2,1)} %copy.32), calls=%async_computation.1 | async-start | bytes 2097152 | tf_op jit(solution)/shard_map/all_to_all | solution.py:53
  17.6 1.5 %copy-start.8 = (bf16[128,128]{1,0:T(8,128)(2,1)S(1)}, bf16[128,128]{1,0:T(8,128)(2,1)}, u32[]{:S(2)}) copy-start(bf16[128,128]{1,0:T(8,128)(2,1)} %param.14) | copy-start | bytes 98308
  40.5 29.9 %all-to-all-start = ((bf16[128,16,256]{2,1,0:T(8,128)(2,1)}), bf16[128,16,256]{2,1,0:T(8,128)(2,1)}, u32[]{:S(2)}, u32[]{:S(2)}) async-start(bf16[128,16,256]{2,1,0:T(8,128)(2,1)} %copy.30), calls=%async_computation | async-start | bytes 2097152 | tf_op jit(solution)/shard_map/all_to_all | solution.py:52
  72.2 8.4 %copy-start.4 = (bf16[128,128]{1,0:T(8,128)(2,1)S(1)}, bf16[128,128]{1,0:T(8,128)(2,1)}, u32[]{:S(2)}) copy-start(bf16[128,128]{1,0:T(8,128)(2,1)} %param.18) | copy-start | bytes 98308
  73.8 29.8 %all-to-all-start.2 = ((bf16[8,256,256]{2,0,1:T(8,128)(2,1)}), bf16[8,256,256]{2,0,1:T(8,128)(2,1)S(1)}, u32[]{:S(2)}, u32[]{:S(2)}) async-start(bf16[8,256,256]{2,0,1:T(8,128)(2,1)} %copy.34), calls=%async_computation.2 | async-start | bytes 2097152 | tf_op jit(solution)/shard_map/all_to_all | solution.py:58
  104.5 0.7 copy-start.6
  105.1 1.6 %copy-start.2 = (f32[16,256,128]{2,1,0:T(8,128)S(1)}, f32[16,256,128]{2,1,0:T(8,128)}, u32[]{:S(2)}) copy-start(f32[16,256,128]{2,1,0:T(8,128)} %fusion.20) | copy-start | bytes 6291460
  105.1 1.6 %copy-start.9 = (bf16[128,128]{1,0:T(8,128)(2,1)S(1)}, bf16[128,128]{1,0:T(8,128)(2,1)}, u32[]{:S(2)}) copy-start(bf16[128,128]{1,0:T(8,128)(2,1)} %param.19) | copy-start | bytes 98308
where the time goes:
time: 142 us; the launch traced here: 141 us
  waiting for transfers between devices  61 us (43%)
  blocking collectives  31.5 us (22%)
  starting transfers between devices  21.2 us (15%)
  matrix products  11.1 us (8%)
  local copies, waits for them, and re-layouts  10.3 us (7%)
  other arithmetic  5.87 us (4%)
    all_to_all x1, blocking collectives, shards(): lax.all_to_all(updated_rows, 'wide', split_axis=1, concat_axis=0, tiled=T...  31.5 us
    all_to_all x1, waiting for transfers between devices, shards(): lax.all_to_all(left_edges, 'wide', split_axis=0, concat_axis=1, tiled=True)  22.9 us
    all_to_all x1, waiting for transfers between devices, shards(): lax.all_to_all(triangle, 'wide', split_axis=1, concat_axis=0, tiled=True)  20.4 us
    all_to_all x1, waiting for transfers between devices, shards(): lax.all_to_all(right_edges, 'wide', split_axis=0, concat_axis=1, tiled=True)  17.7 us
    all_to_all x1, starting transfers between devices, shards(): lax.all_to_all(right_edges, 'wide', split_axis=0, concat_axis=1, tiled=True)  7.39 us
    all_to_all x1, starting transfers between devices, shards(): lax.all_to_all(left_edges, 'wide', split_axis=0, concat_axis=1, tiled=True)  6.92 us
    all_to_all x1, starting transfers between devices, shards(): lax.all_to_all(triangle, 'wide', split_axis=1, concat_axis=0, tiled=True)  6.86 us
    dot_general x2, matrix products, edge_side(): jnp.einsum('ikc,ch->hik', normed, value_weight, preferred_element_type=jn...  4.12 us
  transfers between devices with their start and end apart: 3, of which 3 were waited for; matrix products, arithmetic and copies ran while one was open for 6% of the time, Pallas kernels for 0%

commit v1 on v0

v1 whole, which is shorter than its diff:
```python
import jax
import jax.numpy as jnp
from jax import lax
from jax.sharding import PartitionSpec as P


def layer_norm(values, gain, axis):
    mean_value = jnp.mean(values, axis=axis, keepdims=True)
    centred = values - mean_value
    variance = jnp.mean(centred * centred, axis=axis, keepdims=True)
    return centred * lax.rsqrt(variance + 1e-05) * gain


def swap(values, mask, count):
    return lax.ppermute(values, "wide", [(d, d ^ mask) for d in range(count)])


def edge_side(normed, gate_weight, value_weight, pair_mask):
    gated = jnp.einsum("ikc,ch->hik", normed, gate_weight, preferred_element_type=jnp.float32)
    valued = jnp.einsum("ikc,ch->hik", normed, value_weight, preferred_element_type=jnp.float32)
    return (jax.nn.sigmoid(gated) * valued * pair_mask[None, :, :]).astype(jnp.bfloat16)


def gather(own, bits, count):
    units = {0: own}
    for bit in bits:
        for mask in list(units):
            units[mask | bit] = swap(units[mask], bit, count)
    return units


def make_shards(count):
    bits = [1 << b for b in range(count.bit_length() - 1)]
    right_bits = bits[0::2][::-1]
    left_bits = bits[1::2][::-1]

    def shards(
        pair,
        residue_mask,
        input_gain,
        left_gate,
        left_value,
        right_gate,
        right_value,
        middle_gain,
        output_gate,
        output_value,
    ):
        rows = pair.shape[0]
        me = lax.axis_index("wide")
        chain_mask = residue_mask.astype(jnp.float32)

        def mask_of(unit):
            own_mask = lax.dynamic_slice_in_dim(chain_mask, (me ^ unit) * rows, rows, 0)
            return own_mask[:, None] * chain_mask[None, :]

        def norm(values):
            return layer_norm(values.astype(jnp.float32), input_gain, 2).astype(jnp.bfloat16)

        left_rows = gather(pair, left_bits, count)
        own_normed = norm(pair)
        right_own = edge_side(own_normed, right_gate, right_value, mask_of(0))
        right_units = gather(right_own, right_bits, count)
        right_order = list(right_units)
        right_edges = jnp.concatenate([right_units[m] for m in right_order], axis=1)

        result = {}
        for unit, raw in left_rows.items():
            normed = own_normed if unit == 0 else norm(raw)
            left = edge_side(normed, left_gate, left_value, mask_of(unit))
            triangle = jnp.einsum(
                "hik,hjk->hij", left, right_edges, preferred_element_type=jnp.float32
            ).astype(jnp.bfloat16)
            middle = layer_norm(
                triangle.astype(jnp.float32), middle_gain[:, None, None], 0
            ).astype(jnp.bfloat16)
            projected = jnp.einsum(
                "hij,hc->ijc", middle, output_value, preferred_element_type=jnp.float32
            )
            columns = lambda v: jnp.concatenate(
                [lax.dynamic_slice_in_dim(v, (me ^ m) * rows, rows, 1) for m in right_order], axis=1
            )
            gating = jax.nn.sigmoid(
                jnp.einsum("ijc,cd->ijd", columns(normed), output_gate, preferred_element_type=jnp.float32)
            )
            out = (columns(raw).astype(jnp.float32) + gating * projected).astype(jnp.bfloat16)
            for at, m in enumerate(right_order):
                block = out[:, at * rows : (at + 1) * rows]
                result[unit | m] = block if m == 0 else swap(block, m, count)
        stacked = jnp.stack([result[m] for m in range(count)])
        picked = stacked[me ^ jnp.arange(count)]
        return picked.reshape(count * rows, rows, pair.shape[2])

    return shards


def solution(mesh):
    in_specs = (P(("groups", "wide"), None, None), P("groups")) + (P(),) * 8
    out_specs = P("groups", "wide", None)
    return jax.shard_map(
        make_shards(mesh.shape["wide"]), mesh=mesh, in_specs=in_specs, out_specs=out_specs, check_vma=False
    )
```

time: 142 us -> 171 us (1.20)
  blocking collectives: 31.5 us -> 0 us
  waiting for transfers between devices: 61 us -> 84.4 us
  local copies, waits for them, and re-layouts: 10.3 us -> 26.9 us
  other arithmetic: 5.87 us -> 22 us
  matrix products: 11.1 us -> 19.2 us
  starting transfers between devices: 21.2 us -> 16.7 us
    ppermute x0 -> x18, waiting for transfers between devices: none -> 84.4 us  [swap(): return lax.ppermute(values, 'wide', [(d, d ^ mask) for d in range(count)])]
    all_to_all x3 -> x0, waiting for transfers between devices: 61 us -> none  [the longest x1 22.9 us: shards(): lax.all_to_all(left_edges, 'wide', split_axis=0, concat_axis=1, tiled=True)]
    all_to_all x1 -> x0, blocking collectives: 31.5 us -> none  [shards(): lax.all_to_all(updated_rows, 'wide', split_axis=1, concat_axis=0, tiled=T...]
    all_to_all x3 -> x0, starting transfers between devices: 21.2 us -> none  [the longest x1 7.39 us: shards(): lax.all_to_all(right_edges, 'wide', split_axis=0, concat_axis=1, tiled=True)]
    ppermute x0 -> x18, starting transfers between devices: none -> 16.7 us  [swap(): return lax.ppermute(values, 'wide', [(d, d ^ mask) for d in range(count)])]
    convert_element_type x1 -> x2, other arithmetic: 0.28 us -> 8.54 us  [the longest x1 7.83 us: norm(): layer_norm(values.astype(jnp.float32), input_gain, 2).astype(jnp.bfloat16)]
    concatenate x0 -> x1, local copies, waits for them, and re-layouts: none -> 6.96 us  [shards(): right_edges = jnp.concatenate([right_units[m] for m in right_order], axis=1)]
    dynamic_slice x1 -> x7, local copies, waits for them, and re-layouts: 0.08 us -> 6.58 us  [the longest x6 6.49 us: shards(): lax.dynamic_slice_in_dim(v, (me ^ m) * rows, rows, 1)]
  transfers between devices with their start and end apart: 3 -> 18, of which waited for: 3 -> 9; matrix products, arithmetic and copies ran while one was open for 6% -> 19% of each run, Pallas kernels for 0% -> 0%
where the time goes in v1:
time: 171 us; the launch traced here: 170 us
  waiting for transfers between devices  84.4 us (49%)
  local copies, waits for them, and re-layouts  26.9 us (16%)
  other arithmetic  22 us (13%)
  matrix products  19.2 us (11%)
  starting transfers between devices  16.7 us (10%)
    ppermute x18, waiting for transfers between devices, swap(): return lax.ppermute(values, 'wide', [(d, d ^ mask) for d in range(count)])  84.4 us
    ppermute x18, starting transfers between devices, swap(): return lax.ppermute(values, 'wide', [(d, d ^ mask) for d in range(count)])  16.7 us
    convert_element_type x4, local copies, waits for them, and re-layouts, edge_side(): (jax.nn.sigmoid(gated) * valued * pair_mask[None, :, :]).astype(jnp.bfloa...  9.87 us
    convert_element_type x1, other arithmetic, norm(): layer_norm(values.astype(jnp.float32), input_gain, 2).astype(jnp.bfloat16)  7.83 us
    dot_general x5, matrix products, edge_side(): jnp.einsum('ikc,ch->hik', normed, value_weight, preferred_element_type=jn...  7.54 us
    dot_general x4, matrix products, shards(): jnp.einsum('hik,hjk->hij', left, right_edges, preferred_element_type=jnp....  7.13 us
    concatenate x1, local copies, waits for them, and re-layouts, shards(): right_edges = jnp.concatenate([right_units[m] for m in right_order], axis=1)  6.96 us
    dynamic_slice x6, local copies, waits for them, and re-layouts, shards(): lax.dynamic_slice_in_dim(v, (me ^ m) * rows, rows, 1)  6.49 us
  transfers between devices with their start and end apart: 18, of which 9 were waited for; matrix products, arithmetic and copies ran while one was open for 19% of the time, Pallas kernels for 0%

profile of v1, /device:TPU:0, one launch (start us, length us, event | category | flops | bytes accessed | tf_op | source)
XLA Modules:
  0.0 169.8 jit_solution(17413837807497003188)
XLA Ops:
  0.0 4.0 %collective-permute-start.10 = (bf16[16,256,128]{2,1,0:T(8,128)(2,1)}, bf16[16,256,128]{2,1,0:T(8,128)(2,1)S(1)}, u32[]{:S(2)}, u32[]{:S(2)}) collective-permute-start(bf16[16,256,128]{2,1,0:T(8,128)(2,1)} %param.10), channel_id=1, source_target_pairs={{0,8},{1,9},{2,10},{3,11},{4,12},{5,13},{6,14},{7,15},{8,0},{9,1},... | collective-permute-start | bytes 3145736 | tf_op jit(solution)/shard_map/ppermute | solution.py:15
  7.9 1.6 constant_dynamic-slice_fusion.31
  11.0 38.9 %collective-permute-done.10 = bf16[16,256,128]{2,1,0:T(8,128)(2,1)S(1)} collective-permute-done((bf16[16,256,128]{2,1,0:T(8,128)(2,1)}, bf16[16,256,128]{2,1,0:T(8,128)(2,1)S(1)}, u32[]{:S(2)}, u32[]{:S(2)}) %collective-permute-start.10) | collective-permute-done | bytes 1048608 | tf_op jit(solution)/shard_map/ppermute | solution.py:15
  56.3 17.9 %collective-permute-done.12 = bf16[16,256,128]{2,1,0:T(8,128)(2,1)S(1)} collective-permute-done((bf16[16,256,128]{2,1,0:T(8,128)(2,1)S(1)}, bf16[16,256,128]{2,1,0:T(8,128)(2,1)S(1)}, u32[]{:S(2)}, u32[]{:S(2)}) %collective-permute-start.12) | collective-permute-done | bytes 1048608 | tf_op jit(solution)/shard_map/ppermute | solution.py:15
  76.0 7.8 %fusion.10 = (bf16[16,256,128]{2,1,0:T(8,128)(2,1)S(1)}, bf16[16,256,128]{2,1,0:T(8,128)(2,1)}, bf16[16,256,128]{2,1,0:T(8,128)(2,1)}, bf16[16,256,128]{2,1,0:T(8,128)(2,1)S(1)}) fusion(bf16[16,256,128]{2,1,0:T(8,128)(2,1)S(1)} %collective-permute-done.12, f32[16,256]{1,0:T(8,128)S(1)} %add_rsqrt_fusion, f32[16,256]{1,0:T(8,128)S(1)} %broadcast_multiply_fusion.4, ...), kind=kLoop, calls=%fused_computation.20 | loop fusion | flops 10485760 | bytes 8520192 | tf_op jit(solution)/shard_map/convert_element_type | solution.py:58
  84.6 1.7 fusion.21
  89.1 1.7 %copy.20 = bf16[128,16,256]{2,1,0:T(8,128)(2,1)} copy(bf16[128,16,256]{0,2,1:T(8,128)(2,1)S(1)} %fusion.24) | data formatting | bytes 2097152 | tf_op jit(solution)/shard_map/convert_element_type | solution.py:21
  91.3 1.7 fusion.22
  92.9 2.8 %copy.14 = bf16[128,16,256]{2,1,0:T(8,128)(2,1)} copy(bf16[128,16,256]{0,2,1:T(8,128)(2,1)} %fusion.22) | data formatting | bytes 2097152 | tf_op jit(solution)/shard_map/convert_element_type | solution.py:21
  96.1 1.7 fusion.23
  97.8 2.7 %copy.17 = bf16[128,16,256]{2,1,0:T(8,128)(2,1)} copy(bf16[128,16,256]{0,2,1:T(8,128)(2,1)} %fusion.23) | data formatting | bytes 2097152 | tf_op jit(solution)/shard_map/convert_element_type | solution.py:21
  100.8 11.3 %collective-permute-done = bf16[128,16,256]{0,2,1:T(8,128)(2,1)} collective-permute-done((bf16[128,16,256]{0,2,1:T(8,128)(2,1)}, bf16[128,16,256]{0,2,1:T(8,128)(2,1)}, u32[]{:S(2)}, u32[]{:S(2)}) %collective-permute-start) | collective-permute-done | bytes 1048608 | tf_op jit(solution)/shard_map/ppermute | solution.py:15
  112.1 1.6 fusion.20
  113.8 2.7 %copy.11 = bf16[128,16,256]{2,1,0:T(8,128)(2,1)} copy(bf16[128,16,256]{0,2,1:T(8,128)(2,1)} %fusion.20) | data formatting | bytes 2097152 | tf_op jit(solution)/shard_map/convert_element_type | solution.py:21
  116.5 1.7 constant_dynamic-slice_fusion.7
  120.2 3.9 %pad_maximum_fusion = bf16[128,64,256]{0,2,1:T(8,128)(2,1)} fusion(bf16[128,16,256]{0,2,1:T(8,128)(2,1)} %collective-permute-done.2, bf16[128,16,256]{0,2,1:T(8,128)(2,1)} %collective-permute-done.1, bf16[128,16,256]{0,2,1:T(8,128)(2,1)} %collective-permute-done, bf16[128,16,256]{0,2,1:T(8,128)(2,1)} %fusion.21), kind=kLoop, calls=%fused_computation.1 | loop fusion | flops 6291456 | bytes 8388608 | tf_op jit(solution)/shard_map/concatenate | solution.py:65
  124.1 7.0 %copy.12 = bf16[128,64,256]{2,1,0:T(8,128)(2,1)} copy(bf16[128,64,256]{0,2,1:T(8,128)(2,1)} %pad_maximum_fusion) | data formatting | bytes 8388608 | tf_op jit(solution)/shard_map/concatenate | solution.py:65
  131.1 3.5 %convert_reduce_fusion.4 = (f32[16,64]{1,0:T(8,128)S(1)}, bf16[128,16,64]{2,1,0:T(8,128)(2,1)S(1)}) fusion(bf16[128,16,256]{2,1,0:T(8,128)(2,1)S(1)} %copy-done.9, bf16[128,64,256]{2,1,0:T(8,128)(2,1)} %copy.12), kind=kOutput, calls=%fused_computation.41 | convolution fusion | flops 67501056 | bytes 5509120 | tf_op jit(solution)/shard_map/hik,hjk->hij/dot_general | solution.py:71
  141.6 1.7 %collective-permute-start.17 = (bf16[16,16,128]{2,1,0:T(8,128)(2,1)S(1)}, bf16[16,16,128]{2,1,0:T(8,128)(2,1)S(1)}, u32[]{:S(2)}, u32[]{:S(2)}) collective-permute-start(bf16[16,16,128]{2,1,0:T(8,128)(2,1)S(1)} %get-tuple-element.37), channel_id=1, source_target_pairs={{0,5},{1,4},{2,7},{3,6},{4,1},{5,0},{6,3},{7,2},{8,13},{9,12},{10,... | collective-permute-start | bytes 196616 | tf_op jit(solution)/shard_map/ppermute | solution.py:15
  149.4 3.8 %collective-permute-done.6 = bf16[16,16,128]{2,1,0:T(8,128)(2,1)S(1)} collective-permute-done((bf16[16,16,128]{2,1,0:T(8,128)(2,1)S(1)}, bf16[16,16,128]{2,1,0:T(8,128)(2,1)S(1)}, u32[]{:S(2)}, u32[]{:S(2)}) %collective-permute-start.6) | collective-permute-done | bytes 65568 | tf_op jit(solution)/shard_map/ppermute | solution.py:15
  154.5 4.0 %collective-permute-done.8 = bf16[16,16,128]{2,1,0:T(8,128)(2,1)S(1)} collective-permute-done((bf16[16,16,128]{2,1,0:T(8,128)(2,1)S(1)}, bf16[16,16,128]{2,1,0:T(8,128)(2,1)S(1)}, u32[]{:S(2)}, u32[]{:S(2)}) %collective-permute-start.8) | collective-permute-done | bytes 65568 | tf_op jit(solution)/shard_map/ppermute | solution.py:15
  159.2 3.4 %collective-permute-done.9 = bf16[16,16,128]{2,1,0:T(8,128)(2,1)S(1)} collective-permute-done((bf16[16,16,128]{2,1,0:T(8,128)(2,1)S(1)}, bf16[16,16,128]{2,1,0:T(8,128)(2,1)S(1)}, u32[]{:S(2)}, u32[]{:S(2)}) %collective-permute-start.9) | collective-permute-done | bytes 65568 | tf_op jit(solution)/shard_map/ppermute | solution.py:15
  165.0 3.1 %collective-permute-done.14 = bf16[16,16,128]{2,1,0:T(8,128)(2,1)S(1)} collective-permute-done((bf16[16,16,128]{2,1,0:T(8,128)(2,1)S(1)}, bf16[16,16,128]{2,1,0:T(8,128)(2,1)S(1)}, u32[]{:S(2)}, u32[]{:S(2)}) %collective-permute-start.14) | collective-permute-done | bytes 65568 | tf_op jit(solution)/shard_map/ppermute | solution.py:15
  168.2 1.7 gather_fusion
  (176 shorter events, 37.3 us)
Async XLA Ops:
  0.0 87.8 %copy-start = (bf16[128,128]{1,0:T(8,128)(2,1)S(1)}, bf16[128,128]{1,0:T(8,128)(2,1)}, u32[]{:S(2)}) copy-start(bf16[128,128]{1,0:T(8,128)(2,1)} %param.13) | copy-start | bytes 98308
  0.0 9.5 %copy-start.2 = (bf16[16,256,128]{2,1,0:T(8,128)(2,1)S(1)}, bf16[16,256,128]{2,1,0:T(8,128)(2,1)}, u32[]{:S(2)}) copy-start(bf16[16,256,128]{2,1,0:T(8,128)(2,1)} %param.10) | copy-start | bytes 3145732
  0.0 49.9 %collective-permute-start.10 = (bf16[16,256,128]{2,1,0:T(8,128)(2,1)}, bf16[16,256,128]{2,1,0:T(8,128)(2,1)S(1)}, u32[]{:S(2)}, u32[]{:S(2)}) collective-permute-start(bf16[16,256,128]{2,1,0:T(8,128)(2,1)} %param.10), channel_id=1, source_target_pairs={{0,8},{1,9},{2,10},{3,11},{4,12},{5,13},{6,14},{7,15},{8,0},{9,1},... | collective-permute-start | bytes 3145736 | tf_op jit(solution)/shard_map/ppermute | solution.py:15
  4.0 48.5 %collective-permute-start.4 = (bf16[16,256,128]{2,1,0:T(8,128)(2,1)}, bf16[16,256,128]{2,1,0:T(8,128)(2,1)S(1)}, u32[]{:S(2)}, u32[]{:S(2)}) collective-permute-start(bf16[16,256,128]{2,1,0:T(8,128)(2,1)} %param.10), channel_id=1, source_target_pairs={{0,2},{1,3},{2,0},{3,1},{4,6},{5,7},{6,4},{7,5},{8,10},{9,11},{10,... | collective-permute-start | bytes 3145736 | tf_op jit(solution)/shard_map/ppermute | solution.py:15
  49.9 24.3 %collective-permute-start.12 = (bf16[16,256,128]{2,1,0:T(8,128)(2,1)S(1)}, bf16[16,256,128]{2,1,0:T(8,128)(2,1)S(1)}, u32[]{:S(2)}, u32[]{:S(2)}) collective-permute-start(bf16[16,256,128]{2,1,0:T(8,128)(2,1)S(1)} %collective-permute-done.10), channel_id=1, source_target_pairs={{0,2},{1,3},{2,0},{3,1},{4,6},{5,7},{6,4},{7,5},{8,10},{9,11},{10,... | collective-permute-start | bytes 3145736 | tf_op jit(solution)/shard_map/ppermute | solution.py:15
  52.6 22.0 %copy-start.3 = (bf16[16,256,128]{2,1,0:T(8,128)(2,1)}, bf16[16,256,128]{2,1,0:T(8,128)(2,1)S(1)}, u32[]{:S(2)}) copy-start(bf16[16,256,128]{2,1,0:T(8,128)(2,1)S(1)} %collective-permute-done.4) | copy-start | bytes 3145732
  53.7 22.3 %copy-start.33 = (f32[128]{0:T(128)S(1)}, f32[128]{0:T(128)}, u32[]{:S(2)}) copy-start(f32[128]{0:T(128)} %param.12) | copy-start | bytes 1540
  74.3 9.6 %copy-start.4 = (bf16[16,256,128]{2,1,0:T(8,128)(2,1)}, bf16[16,256,128]{2,1,0:T(8,128)(2,1)S(1)}, u32[]{:S(2)}) copy-start(bf16[16,256,128]{2,1,0:T(8,128)(2,1)S(1)} %collective-permute-done.12) | copy-start | bytes 3145732
  76.0 7.9 %copy-start.32 = (bf16[128,128]{1,0:T(8,128)(2,1)S(1)}, bf16[128,128]{1,0:T(8,128)(2,1)}, u32[]{:S(2)}) copy-start(bf16[128,128]{1,0:T(8,128)(2,1)} %param.15) | copy-start | bytes 98308
  86.3 33.9 %collective-permute-start.1 = (bf16[128,16,256]{0,2,1:T(8,128)(2,1)}, bf16[128,16,256]{0,2,1:T(8,128)(2,1)}, u32[]{:S(2)}, u32[]{:S(2)}) collective-permute-start(bf16[128,16,256]{0,2,1:T(8,128)(2,1)} %fusion.21), channel_id=1, source_target_pairs={{0,1},{1,0},{2,3},{3,2},{4,5},{5,4},{6,7},{7,6},{8,9},{9,8},{10,11... | collective-permute-start | bytes 3145736 | tf_op jit(solution)/shard_map/ppermute | solution.py:15
  86.3 25.9 %collective-permute-start = (bf16[128,16,256]{0,2,1:T(8,128)(2,1)}, bf16[128,16,256]{0,2,1:T(8,128)(2,1)}, u32[]{:S(2)}, u32[]{:S(2)}) collective-permute-start(bf16[128,16,256]{0,2,1:T(8,128)(2,1)} %fusion.21), channel_id=1, source_target_pairs={{0,4},{1,5},{2,6},{3,7},{4,0},{5,1},{6,2},{7,3},{8,12},{9,13},{10,... | collective-permute-start | bytes 3145736 | tf_op jit(solution)/shard_map/ppermute | solution.py:15
  112.1 8.1 %collective-permute-start.2 = (bf16[128,16,256]{0,2,1:T(8,128)(2,1)}, bf16[128,16,256]{0,2,1:T(8,128)(2,1)}, u32[]{:S(2)}, u32[]{:S(2)}) collective-permute-start(bf16[128,16,256]{0,2,1:T(8,128)(2,1)} %collective-permute-done), channel_id=1, source_target_pairs={{0,1},{1,0},{2,3},{3,2},{4,5},{5,4},{6,7},{7,6},{8,9},{9,8},{10,11... | collective-permute-start | bytes 3145736 | tf_op jit(solution)/shard_map/ppermute | solution.py:15
  141.6 26.6 %collective-permute-start.17 = (bf16[16,16,128]{2,1,0:T(8,128)(2,1)S(1)}, bf16[16,16,128]{2,1,0:T(8,128)(2,1)S(1)}, u32[]{:S(2)}, u32[]{:S(2)}) collective-permute-start(bf16[16,16,128]{2,1,0:T(8,128)(2,1)S(1)} %get-tuple-element.37), channel_id=1, source_target_pairs={{0,5},{1,4},{2,7},{3,6},{4,1},{5,0},{6,3},{7,2},{8,13},{9,12},{10,... | collective-permute-start | bytes 196616 | tf_op jit(solution)/shard_map/ppermute | solution.py:15
  143.3 24.8 %collective-permute-start.16 = (bf16[16,16,128]{2,1,0:T(8,128)(2,1)S(1)}, bf16[16,16,128]{2,1,0:T(8,128)(2,1)S(1)}, u32[]{:S(2)}, u32[]{:S(2)}) collective-permute-start(bf16[16,16,128]{2,1,0:T(8,128)(2,1)S(1)} %get-tuple-element.38), channel_id=1, source_target_pairs={{0,4},{1,5},{2,6},{3,7},{4,0},{5,1},{6,2},{7,3},{8,12},{9,13},{10,... | collective-permute-start | bytes 196616 | tf_op jit(solution)/shard_map/ppermute | solution.py:15
  143.8 21.2 %collective-permute-start.13 = (bf16[16,16,128]{2,1,0:T(8,128)(2,1)S(1)}, bf16[16,16,128]{2,1,0:T(8,128)(2,1)S(1)}, u32[]{:S(2)}, u32[]{:S(2)}) collective-permute-start(bf16[16,16,128]{2,1,0:T(8,128)(2,1)S(1)} %get-tuple-element.39), channel_id=1, source_target_pairs={{0,1},{1,0},{2,3},{3,2},{4,5},{5,4},{6,7},{7,6},{8,9},{9,8},{10,11... | collective-permute-start | bytes 196616 | tf_op jit(solution)/shard_map/ppermute | solution.py:15
  143.8 9.5 %collective-permute-start.7 = (bf16[16,16,128]{2,1,0:T(8,128)(2,1)S(1)}, bf16[16,16,128]{2,1,0:T(8,128)(2,1)S(1)}, u32[]{:S(2)}, u32[]{:S(2)}) collective-permute-start(bf16[16,16,128]{2,1,0:T(8,128)(2,1)S(1)} %get-tuple-element.46), channel_id=1, source_target_pairs={{0,5},{1,4},{2,7},{3,6},{4,1},{5,0},{6,3},{7,2},{8,13},{9,12},{10,... | collective-permute-start | bytes 196616 | tf_op jit(solution)/shard_map/ppermute | solution.py:15
  145.4 1.9 %collective-permute-start.3 = (bf16[16,16,128]{2,1,0:T(8,128)(2,1)S(1)}, bf16[16,16,128]{2,1,0:T(8,128)(2,1)S(1)}, u32[]{:S(2)}, u32[]{:S(2)}) collective-permute-start(bf16[16,16,128]{2,1,0:T(8,128)(2,1)S(1)} %get-tuple-element.48), channel_id=1, source_target_pairs={{0,1},{1,0},{2,3},{3,2},{4,5},{5,4},{6,7},{7,6},{8,9},{9,8},{10,11... | collective-permute-start | bytes 196616 | tf_op jit(solution)/shard_map/ppermute | solution.py:15
  147.4 1.5 collective-permute-start.5
  148.9 4.3 %collective-permute-start.6 = (bf16[16,16,128]{2,1,0:T(8,128)(2,1)S(1)}, bf16[16,16,128]{2,1,0:T(8,128)(2,1)S(1)}, u32[]{:S(2)}, u32[]{:S(2)}) collective-permute-start(bf16[16,16,128]{2,1,0:T(8,128)(2,1)S(1)} %get-tuple-element.47), channel_id=1, source_target_pairs={{0,4},{1,5},{2,6},{3,7},{4,0},{5,1},{6,2},{7,3},{8,12},{9,13},{10,... | collective-permute-start | bytes 196616 | tf_op jit(solution)/shard_map/ppermute | solution.py:15
  153.2 14.9 %collective-permute-start.15 = (bf16[16,16,128]{2,1,0:T(8,128)(2,1)S(1)}, bf16[16,16,128]{2,1,0:T(8,128)(2,1)S(1)}, u32[]{:S(2)}, u32[]{:S(2)}) collective-permute-start(bf16[16,16,128]{2,1,0:T(8,128)(2,1)S(1)} %get-tuple-element.40), channel_id=1, source_target_pairs={{0,5},{1,4},{2,7},{3,6},{4,1},{5,0},{6,3},{7,2},{8,13},{9,12},{10,... | collective-permute-start | bytes 196616 | tf_op jit(solution)/shard_map/ppermute | solution.py:15
  153.2 5.2 %collective-permute-start.8 = (bf16[16,16,128]{2,1,0:T(8,128)(2,1)S(1)}, bf16[16,16,128]{2,1,0:T(8,128)(2,1)S(1)}, u32[]{:S(2)}, u32[]{:S(2)}) collective-permute-start(bf16[16,16,128]{2,1,0:T(8,128)(2,1)S(1)} %get-tuple-element.44), channel_id=1, source_target_pairs={{0,4},{1,5},{2,6},{3,7},{4,0},{5,1},{6,2},{7,3},{8,12},{9,13},{10,... | collective-permute-start | bytes 196616 | tf_op jit(solution)/shard_map/ppermute | solution.py:15
  158.5 4.1 %collective-permute-start.9 = (bf16[16,16,128]{2,1,0:T(8,128)(2,1)S(1)}, bf16[16,16,128]{2,1,0:T(8,128)(2,1)S(1)}, u32[]{:S(2)}, u32[]{:S(2)}) collective-permute-start(bf16[16,16,128]{2,1,0:T(8,128)(2,1)S(1)} %get-tuple-element.43), channel_id=1, source_target_pairs={{0,5},{1,4},{2,7},{3,6},{4,1},{5,0},{6,3},{7,2},{8,13},{9,12},{10,... | collective-permute-start | bytes 196616 | tf_op jit(solution)/shard_map/ppermute | solution.py:15
  162.6 1.3 collective-permute-start.11
  163.8 4.3 %collective-permute-start.14 = (bf16[16,16,128]{2,1,0:T(8,128)(2,1)S(1)}, bf16[16,16,128]{2,1,0:T(8,128)(2,1)S(1)}, u32[]{:S(2)}, u32[]{:S(2)}) collective-permute-start(bf16[16,16,128]{2,1,0:T(8,128)(2,1)S(1)} %get-tuple-element.41), channel_id=1, source_target_pairs={{0,4},{1,5},{2,6},{3,7},{4,0},{5,1},{6,2},{7,3},{8,12},{9,13},{10,... | collective-permute-start | bytes 196616 | tf_op jit(solution)/shard_map/ppermute | solution.py:15
  (32 other events, 68.0 us)

commit v2 on v1

v2 whole, which is shorter than its diff:
```python
import functools

import jax
import jax.numpy as jnp
from jax import lax
from jax.experimental import pallas as pl
from jax.experimental.pallas import tpu as pltpu
from jax.sharding import PartitionSpec as P

LANES = 128
WIDE_TYPE = jnp.float32
NARROW = jnp.bfloat16
LAST_BY_LAST = (((1,), (1,)), ((), ()))
VMEM = pl.BlockSpec(memory_space=pltpu.VMEM)
SMEM = pl.BlockSpec(memory_space=pltpu.SMEM)
ANY = pl.BlockSpec(memory_space=pl.ANY)


SHORT = pl.CostEstimate(flops=1 << 20, bytes_accessed=1 << 10, transcendentals=0)
LONG = pl.CostEstimate(flops=1 << 35, bytes_accessed=1 << 10, transcendentals=0)


def sigmoid(values):
    return 0.5 * jnp.tanh(0.5 * values) + 0.5


def norm_rows(values, gain):
    values = values.astype(WIDE_TYPE)
    mean_value = jnp.mean(values, axis=1, keepdims=True)
    centred = values - mean_value
    variance = jnp.mean(centred * centred, axis=1, keepdims=True)
    return (centred * lax.rsqrt(variance + 1e-05) * gain).astype(NARROW)


def fill_edges(first, at, total, pair_ref, chain_ref, mask_ref, gain_ref, weight_refs, edges):
    rows, _, channels = pair_ref.shape
    hidden = weight_refs[0].shape[1]
    gain = jnp.broadcast_to(gain_ref[...], (channels, channels)).T[:, :1]
    weights = jnp.concatenate([ref[...].T for ref in weight_refs], axis=0)
    column_mask = mask_ref[...].astype(WIDE_TYPE)

    def one_row(i, carry):
        values = pair_ref[i].astype(WIDE_TYPE).T
        mean_value = jnp.mean(values, axis=0, keepdims=True)
        centred = values - mean_value
        variance = jnp.mean(centred * centred, axis=0, keepdims=True)
        normed = (centred * lax.rsqrt(variance + 1e-05) * gain).astype(NARROW)
        both = jnp.dot(weights, normed, preferred_element_type=WIDE_TYPE)
        row_mask = chain_ref[first + i].astype(WIDE_TYPE)
        masked = sigmoid(both[:hidden]) * both[hidden:] * (column_mask * row_mask)
        for part in range(len(edges)):
            edges[part][pl.ds(at + i, hidden, stride=total), :] = masked[
                :, part * LANES : (part + 1) * LANES
            ]
        return carry

    lax.fori_loop(0, rows, one_row, 0, unroll=8)


def read_edges(edges, start, size):
    return jnp.concatenate([part[pl.ds(start, size), :] for part in edges], axis=1).astype(NARROW)


def edge_kernel(unit, me_ref, chain_ref, pair_ref, mask_ref, gain_ref, gate_ref, value_ref, out_ref, *edges):
    rows = pair_ref.shape[0]
    first = (me_ref[0] ^ unit) * rows
    fill_edges(first, 0, rows, pair_ref, chain_ref, mask_ref, gain_ref, (gate_ref, value_ref), edges)

    def one_channel(h, carry):
        out_ref[h] = read_edges(edges, pl.multiple_of(h * rows, rows), rows)
        return carry

    lax.fori_loop(0, out_ref.shape[0], one_channel, 0, unroll=16)


def left_kernel(unit, offset, me_ref, chain_ref, pair_ref, mask_ref, gain_ref, gate_ref, value_ref, *edges):
    rows = pair_ref.shape[0]
    first = (me_ref[0] ^ unit) * offset[1] + offset[0]
    fill_edges(first, 0, rows, pair_ref, chain_ref, mask_ref, gain_ref, (gate_ref, value_ref), edges)


def triangle_kernel(
    count, order, me_ref, middle_gain_ref, gain_ref, output_gate_ref, output_value_ref, *rest
):
    units = len(order)
    right_refs, rest = rest[:units], rest[units:]
    pair_refs, rest = rest[:count], rest[count:]
    out_refs, triangle = rest[-1 - units : -1], rest[-1]
    parts = pair_refs[0].shape[1] // LANES
    left_refs = [rest[n * parts : (n + 1) * parts] for n in range(count)]
    me = me_ref[0]
    sizes = [ref.shape[0] for ref in pair_refs]
    rows = sum(sizes)
    hidden = output_value_ref.shape[0]
    width = right_refs[0].shape[1]
    span = units * width
    starts = [sum(sizes[:n]) for n in range(count)]

    def read_left(h):
        whole = [
            jnp.concatenate([ref[pl.ds(pl.multiple_of(h * size, size), size), :] for ref in refs], axis=1)
            for refs, size in zip(left_refs, sizes)
        ]
        return jnp.concatenate(whole, axis=0).astype(NARROW)

    def multiply(h, total):
        at = pl.multiple_of(h * rows, rows)
        left = read_left(h)
        right = jnp.concatenate([ref[h] for ref in right_refs], axis=0)
        product = lax.dot_general(left, right, LAST_BY_LAST, preferred_element_type=WIDE_TYPE)
        product = product.astype(NARROW).astype(WIDE_TYPE)
        triangle[pl.ds(at, rows), :span] = product
        return total + product

    zeros = jnp.zeros((rows, span), WIDE_TYPE)
    mean_value = lax.fori_loop(0, hidden, multiply, zeros, unroll=16) * (1.0 / hidden)

    def spread(h, total):
        centred = triangle[pl.ds(pl.multiple_of(h * rows, rows), rows), :span] - mean_value
        return total + centred * centred

    variance = lax.fori_loop(0, hidden, spread, zeros, unroll=16) * (1.0 / hidden)
    scale = lax.rsqrt(variance + 1e-05)

    def normalise(h, carry):
        at = pl.multiple_of(h * rows, rows)
        triangle[pl.ds(at, rows), :span] = (
            (triangle[pl.ds(at, rows), :span] - mean_value) * scale * middle_gain_ref[h]
        )
        return carry

    lax.fori_loop(0, hidden, normalise, 0, unroll=16)
    for n in range(count):

        def finish(i, carry):
            row = starts[n] + i
            middle = triangle[pl.ds(row, hidden, stride=rows), :].T[:span].astype(NARROW)
            projected = jnp.dot(middle, output_value_ref[...], preferred_element_type=WIDE_TYPE)
            base = jnp.concatenate(
                [
                    pair_refs[n][i, pl.ds(pl.multiple_of((me ^ unit) * width, width), width), :]
                    for unit in order
                ],
                axis=0,
            )
            normed = norm_rows(base, gain_ref[...])
            gating = sigmoid(jnp.dot(normed, output_gate_ref[...], preferred_element_type=WIDE_TYPE))
            updated = (base.astype(WIDE_TYPE) + gating * projected).astype(NARROW)
            for u in range(units):
                out_refs[u][row] = updated[u * width : (u + 1) * width]
            return carry

        lax.fori_loop(0, sizes[n], finish, 0, unroll=4)


def place_kernel(places, me_ref, *rest):
    count = len(places)
    in_refs, out_ref, sem = rest[:count], rest[count], rest[count + 1]
    me = me_ref[0]
    copies = []
    for n, place in enumerate(places):
        for unit, start, size, offset, width in place:
            copies.append(
                pltpu.make_async_copy(
                    in_refs[n].at[pl.ds(start, size)],
                    out_ref.at[pl.ds((me ^ unit) * width + offset, size)],
                    sem.at[len(copies)],
                )
            )
    for copy in copies:
        copy.start()
    for copy in copies:
        copy.wait()


def edge_scratch(rows, hidden, residues):
    return [pltpu.VMEM((hidden * rows, LANES), WIDE_TYPE)] * (residues // LANES)


def edge_call(unit, me, chain, pair, mask, gain, gate, value):
    rows, residues, _ = pair.shape
    hidden = gate.shape[1]
    return pl.pallas_call(
        functools.partial(edge_kernel, unit),
        out_shape=jax.ShapeDtypeStruct((hidden, rows, residues), NARROW),
        in_specs=[SMEM] * 2 + [VMEM] * 5,
        out_specs=VMEM,
        scratch_shapes=edge_scratch(rows, hidden, residues),
        compiler_params=pltpu.CompilerParams(vmem_limit_bytes=16 << 20),
        cost_estimate=pl.CostEstimate(flops=1 << 20, bytes_accessed=1 << 10, transcendentals=0),
        name="edges",
    )(me, chain, pair, mask, gain, gate, value)


def left_call(unit, offset, cost, me, chain, pair, mask, gain, gate, value):
    rows, residues, _ = pair.shape
    hidden = gate.shape[1]
    return pl.pallas_call(
        functools.partial(left_kernel, unit, offset),
        out_shape=[jax.ShapeDtypeStruct((hidden * rows, LANES), WIDE_TYPE)] * (residues // LANES),
        in_specs=[SMEM] * 2 + [VMEM] * 5,
        out_specs=[VMEM] * (residues // LANES),
        compiler_params=pltpu.CompilerParams(vmem_limit_bytes=16 << 20),
        cost_estimate=cost,
        name="left_edges",
    )(me, chain, pair, mask, gain, gate, value)


def triangle_call(order, me, middle_gain, gain, output_gate, output_value, right, pairs, lefts):
    _, _, channels = pairs[0].shape
    rows = sum(p.shape[0] for p in pairs)
    hidden = output_value.shape[0]
    width = right[0].shape[1]
    tensors = [gain, output_gate, output_value, *right, *pairs]
    for left in lefts:
        tensors += left
    return pl.pallas_call(
        functools.partial(triangle_kernel, len(pairs), order),
        out_shape=[jax.ShapeDtypeStruct((rows, width, channels), NARROW)] * len(order),
        in_specs=[SMEM] * 2 + [VMEM] * len(tensors),
        out_specs=[VMEM] * len(order),
        scratch_shapes=[pltpu.VMEM((hidden * rows, LANES), WIDE_TYPE)],
        compiler_params=pltpu.CompilerParams(vmem_limit_bytes=40 << 20),
        cost_estimate=pl.CostEstimate(flops=1 << 20, bytes_accessed=1 << 10, transcendentals=0),
        name="triangle",
    )(me, middle_gain, *tensors)


def place_call(places, me, blocks, shape):
    return pl.pallas_call(
        functools.partial(place_kernel, places),
        out_shape=jax.ShapeDtypeStruct(shape, NARROW),
        in_specs=[SMEM] + [ANY] * len(blocks),
        out_specs=ANY,
        scratch_shapes=[pltpu.SemaphoreType.DMA((sum(len(p) for p in places),))],
        compiler_params=pltpu.CompilerParams(vmem_limit_bytes=8 << 20),
        name="place",
    )(me, *blocks)


def make_shards(count):
    bits = [1 << b for b in range(count.bit_length() - 1)]
    right_bits = bits[0::2][::-1]
    left_bits = bits[1::2][::-1]
    pieces = 2

    def swap(values, mask):
        return lax.ppermute(values, "wide", [(d, d ^ mask) for d in range(count)])

    def shards(
        pair,
        residue_mask,
        input_gain,
        left_gate,
        left_value,
        right_gate,
        right_value,
        middle_gain,
        output_gate,
        output_value,
    ):
        rows = pair.shape[0]
        me = lax.axis_index("wide").astype(jnp.int32).reshape(1)
        mask = residue_mask.reshape(1, -1)
        gain = input_gain.reshape(1, -1)
        part = rows // pieces
        far_bit, near_bits = left_bits[0], left_bits[1:]

        far = [swap(pair[n * part : (n + 1) * part], far_bit) for n in range(pieces)]
        near = {0: pair}
        for bit in near_bits:
            for unit in list(near):
                near[unit | bit] = swap(near[unit], bit)
        own_right = edge_call(0, me, residue_mask, pair, mask, gain, right_gate, right_value)
        right = {0: own_right}
        for bit in right_bits:
            for unit in list(right):
                right[unit | bit] = swap(right[unit], bit)
        order = list(right)
        rights = [right[unit] for unit in order]

        far_units = {far_bit: far}
        for bit in near_bits:
            for unit in list(far_units):
                far_units[unit | bit] = [swap(piece, bit) for piece in far_units[unit]]

        blocks = []
        places = []

        def left_edges(unit, offset, raw, cost):
            return left_call(
                unit, (offset, rows), cost, me, residue_mask, raw, mask, gain, left_gate, left_value
            )

        def finish(firsts, pairs, lefts):
            outs = triangle_call(
                order, me, middle_gain, gain, output_gate, output_value, rights, pairs, lefts
            )
            for unit, out in zip(order, outs):
                blocks.append(out if unit == 0 else swap(out, unit))
                place, start = [], 0
                for (left_unit, offset), source in zip(firsts, pairs):
                    place.append((left_unit | unit, start, source.shape[0], offset, rows))
                    start += source.shape[0]
                places.append(place)

        lefts = []
        after = own_right
        for unit, raw in near.items():
            raw, after = lax.optimization_barrier((raw, after))
            lefts.append(left_edges(unit, 0, raw, SHORT))
            after = lefts[-1][0]
        finish([(unit, 0) for unit in near], list(near.values()), lefts)
        for unit, raws in far_units.items():
            lefts = [left_edges(unit, n * part, raws[n], LONG) for n in range(pieces)]
            finish([(unit, n * part) for n in range(pieces)], raws, lefts)
        return place_call(places, me, blocks, (count * rows, rows, pair.shape[2]))

    return shards


def solution(mesh):
    in_specs = (P(("groups", "wide"), None, None), P("groups")) + (P(),) * 8
    out_specs = P("groups", "wide", None)
    return jax.shard_map(
        make_shards(mesh.shape["wide"]), mesh=mesh, in_specs=in_specs, out_specs=out_specs, check_vma=False
    )
```

time: 171 us -> 92.9 us (0.54)
  waiting for transfers between devices: 84.4 us -> 41.6 us
  Pallas kernels: 0 us -> 30.9 us
  local copies, waits for them, and re-layouts: 26.9 us -> 2.7 us
  other arithmetic: 22 us -> 0 us
  matrix products: 19.2 us -> 0 us
    ppermute x18 -> x17, waiting for transfers between devices: 84.4 us -> 41.6 us  [swap(): return lax.ppermute(values, 'wide', [(d, d ^ mask) for d in range(count)])]
    pallas_call x0 -> x11, Pallas kernels: none -> 30.9 us  [the longest x3 15.7 us: triangle_call(): pl.pallas_call(functools.partial(triangle_kernel, len(pairs), order), out...]
    dot_general x22 -> x0, matrix products: 19.2 us -> none  [the longest x5 7.54 us: edge_side(): jnp.einsum('ikc,ch->hik', normed, value_weight, preferred_element_type=jn...]
    convert_element_type x4 -> x0, local copies, waits for them, and re-layouts: 9.87 us -> none  [edge_side(): (jax.nn.sigmoid(gated) * valued * pair_mask[None, :, :]).astype(jnp.bfloa...]
    convert_element_type x3 -> x0, other arithmetic: 9.22 us -> none  [the longest x1 7.83 us: norm(): layer_norm(values.astype(jnp.float32), input_gain, 2).astype(jnp.bfloat16)]
    reduce_sum x12 -> x0, other arithmetic: 8.67 us -> none  [the longest x8 6.03 us: layer_norm(): variance = jnp.mean(centred * centred, axis=axis, keepdims=True)]
    concatenate x1 -> x0, local copies, waits for them, and re-layouts: 6.96 us -> none  [shards(): right_edges = jnp.concatenate([right_units[m] for m in right_order], axis=1)]
    dynamic_slice x7 -> x0, local copies, waits for them, and re-layouts: 6.58 us -> none  [the longest x6 6.49 us: shards(): lax.dynamic_slice_in_dim(v, (me ^ m) * rows, rows, 1)]
  transfers between devices with their start and end apart: 18 -> 17, of which waited for: 9 -> 7; matrix products, arithmetic and copies ran while one was open for 19% -> 0% of each run, Pallas kernels for 0% -> 32%
where the time goes in v2:
time: 92.9 us; the launch traced here: 92.7 us
  waiting for transfers between devices  41.6 us (45%)
  Pallas kernels  30.9 us (33%)
  starting transfers between devices  17.4 us (19%)
  local copies, waits for them, and re-layouts  2.7 us (3%)
    ppermute x17, waiting for transfers between devices, swap(): return lax.ppermute(values, 'wide', [(d, d ^ mask) for d in range(count)])  41.6 us
    ppermute x17, starting transfers between devices, swap(): return lax.ppermute(values, 'wide', [(d, d ^ mask) for d in range(count)])  17.4 us
    pallas_call x3, Pallas kernels, triangle_call(): pl.pallas_call(functools.partial(triangle_kernel, len(pairs), order), out...  15.7 us
    pallas_call x6, Pallas kernels, left_call(): pl.pallas_call(functools.partial(left_kernel, unit, offset), out_shape=[j...  11.2 us
    pallas_call x1, Pallas kernels, edge_call(): pl.pallas_call(functools.partial(edge_kernel, unit), out_shape=jax.ShapeD...  2.82 us
  transfers between devices with their start and end apart: 17, of which 7 were waited for; matrix products, arithmetic and copies ran while one was open for 0% of the time, Pallas kernels for 32%

profile of v2, /device:TPU:0, one launch (start us, length us, event | category | flops | bytes accessed | tf_op | source)
XLA Modules:
  0.0 92.7 jit_solution(13720401353791582972)
XLA Ops:
  0.0 1.4 %fusion = (bf16[8,256,128]{2,1,0:T(8,128)(2,1)S(1)}, bf16[8,256,128]{2,1,0:T(8,128)(2,1)S(1)}) fusion(bf16[16,256,128]{2,1,0:T(8,128)(2,1)} %rest_4_.1), kind=kLoop, calls=%fused_computation | loop fusion | bytes 2097152 | tf_op jit(solution)/shard_map/slice | solution.py:269
  1.4 4.1 %collective-permute-start.7 = (bf16[8,256,128]{2,1,0:T(8,128)(2,1)S(1)}, bf16[8,256,128]{2,1,0:T(8,128)(2,1)S(1)}, u32[]{:S(2)}, u32[]{:S(2)}) collective-permute-start(bf16[8,256,128]{2,1,0:T(8,128)(2,1)S(1)} %get-tuple-element.58), channel_id=1, source_target_pairs={{0,8},{1,9},{2,10},{3,11},{4,12},{5,13},{6,14},{7,15},{8,0},{9,1},... | collective-permute-start | bytes 1572872 | tf_op jit(solution)/shard_map/ppermute | solution.py:248
  6.2 2.8 %edges.1.rest_0_ = bf16[128,16,256]{2,1,0:T(8,128)(2,1)S(1)} custom-call(s32[1]{0:T(128)} %bitcast.me_ref, s32[256]{0:T(256)S(1)} %copy-done.5, bf16[16,256,128]{2,1,0:T(8,128)(2,1)S(1)} %copy-done, s32[1,256]{1,0:T(1,128)S(1)} %bitcast.3, f32[1,128]{1,0:T(1,128)S(1)} %bitcast.10, bf16[128,128]{1,0:T(8,128)(2,1)S(1)} %copy-done.6, bf16[128,128]{1,0:T(8,128)(2,1)S(1)} %copy-done.7), custom_call_target="tpu_custom_call" | custom-call | flops 1048576 | bytes 1024 | tf_op jit(solution)/shard_map/edges/pallas_call | solution.py:183
  9.0 1.7 %collective-permute-start = (bf16[128,16,256]{2,1,0:T(8,128)(2,1)S(1)}, bf16[128,16,256]{2,1,0:T(8,128)(2,1)S(1)}, u32[]{:S(2)}, u32[]{:S(2)}) collective-permute-start(bf16[128,16,256]{2,1,0:T(8,128)(2,1)S(1)} %edges.1.rest_0_), channel_id=1, source_target_pairs={{0,4},{1,5},{2,6},{3,7},{4,0},{5,1},{6,2},{7,3},{8,12},{9,13},{10,... | collective-permute-start | bytes 3145736 | tf_op jit(solution)/shard_map/ppermute | solution.py:248
  10.6 1.5 %collective-permute-start.3 = (bf16[16,256,128]{2,1,0:T(8,128)(2,1)S(1)}, bf16[16,256,128]{2,1,0:T(8,128)(2,1)S(1)}, u32[]{:S(2)}, u32[]{:S(2)}) collective-permute-start(bf16[16,256,128]{2,1,0:T(8,128)(2,1)S(1)} %copy-done), channel_id=1, source_target_pairs={{0,2},{1,3},{2,0},{3,1},{4,6},{5,7},{6,4},{7,5},{8,10},{9,11},{10,... | collective-permute-start | bytes 3145736 | tf_op jit(solution)/shard_map/ppermute | solution.py:248
  12.5 2.7 %left_edges.6 = (f32[2048,128]{1,0:T(8,128)S(1)}, f32[2048,128]{1,0:T(8,128)S(1)}) custom-call(s32[1]{0:T(128)} %bitcast.me_ref, s32[256]{0:T(256)S(1)} %copy-done.5, bf16[16,256,128]{2,1,0:T(8,128)(2,1)S(1)} %copy-done, s32[1,256]{1,0:T(1,128)S(1)} %bitcast.4, f32[1,128]{1,0:T(1,128)S(1)} %bitcast.11, bf16[128,128]{1,0:T(8,128)(2,1)S(1)} %copy-done.3, ...), custom_call_target="tpu_custom_call" | custom-call | flops 1048576 | bytes 1024 | tf_op jit(solution)/shard_map/left_edges/pallas_call | solution.py:198
  15.2 14.4 %collective-permute-done.7.pair_ref.rest_4_ = bf16[8,256,128]{2,1,0:T(8,128)(2,1)S(1)} collective-permute-done((bf16[8,256,128]{2,1,0:T(8,128)(2,1)S(1)}, bf16[8,256,128]{2,1,0:T(8,128)(2,1)S(1)}, u32[]{:S(2)}, u32[]{:S(2)}) %collective-permute-start.7) | collective-permute-done | bytes 524320 | tf_op jit(solution)/shard_map/ppermute | solution.py:248
  29.6 1.4 %left_edges.8 = (f32[1024,128]{1,0:T(8,128)S(1)}, f32[1024,128]{1,0:T(8,128)S(1)}) custom-call(s32[1]{0:T(128)} %bitcast.me_ref, s32[256]{0:T(256)S(1)} %copy-done.5, bf16[8,256,128]{2,1,0:T(8,128)(2,1)S(1)} %collective-permute-done.7.pair_ref.rest_4_, s32[1,256]{1,0:T(1,128)S(1)} %bitcast.5, f32[1,128]{1,0:T(1,128)S(1)} %bitcast.12, ...), custom_call_target="tpu_custom_call" | custom-call | flops 34359738368 | bytes 1024 | tf_op jit(solution)/shard_map/left_edges/pallas_call | solution.py:198
  31.0 1.9 %collective-permute-start.12 = (bf16[8,256,128]{2,1,0:T(8,128)(2,1)S(1)}, bf16[8,256,128]{2,1,0:T(8,128)(2,1)S(1)}, u32[]{:S(2)}, u32[]{:S(2)}) collective-permute-start(bf16[8,256,128]{2,1,0:T(8,128)(2,1)S(1)} %collective-permute-done.7.pair_ref.rest_4_), channel_id=1, source_target_pairs={{0,2},{1,3},{2,0},{3,1},{4,6},{5,7},{6,4},{7,5},{8,10},{9,11},{10,... | collective-permute-start | bytes 1572872 | tf_op jit(solution)/shard_map/ppermute | solution.py:248
  33.0 17.5 %collective-permute-done.8.pair_ref.rest_5_ = bf16[8,256,128]{2,1,0:T(8,128)(2,1)S(1)} collective-permute-done((bf16[8,256,128]{2,1,0:T(8,128)(2,1)S(1)}, bf16[8,256,128]{2,1,0:T(8,128)(2,1)S(1)}, u32[]{:S(2)}, u32[]{:S(2)}) %collective-permute-start.8) | collective-permute-done | bytes 524320 | tf_op jit(solution)/shard_map/ppermute | solution.py:248
  50.4 1.5 %left_edges.9 = (f32[1024,128]{1,0:T(8,128)S(1)}, f32[1024,128]{1,0:T(8,128)S(1)}) custom-call(s32[1]{0:T(128)} %bitcast.me_ref, s32[256]{0:T(256)S(1)} %copy-done.5, bf16[8,256,128]{2,1,0:T(8,128)(2,1)S(1)} %collective-permute-done.8.pair_ref.rest_5_, s32[1,256]{1,0:T(1,128)S(1)} %bitcast.6, f32[1,128]{1,0:T(1,128)S(1)} %bitcast.13, ...), custom_call_target="tpu_custom_call" | custom-call | flops 34359738368 | bytes 1024 | tf_op jit(solution)/shard_map/left_edges/pallas_call | solution.py:198
  51.9 1.6 %collective-permute-start.13 = (bf16[8,256,128]{2,1,0:T(8,128)(2,1)S(1)}, bf16[8,256,128]{2,1,0:T(8,128)(2,1)S(1)}, u32[]{:S(2)}, u32[]{:S(2)}) collective-permute-start(bf16[8,256,128]{2,1,0:T(8,128)(2,1)S(1)} %collective-permute-done.8.pair_ref.rest_5_), channel_id=1, source_target_pairs={{0,2},{1,3},{2,0},{3,1},{4,6},{5,7},{6,4},{7,5},{8,10},{9,11},{10,... | collective-permute-start | bytes 1572872 | tf_op jit(solution)/shard_map/ppermute | solution.py:248
  53.5 1.5 %collective-permute-done.rest_1_ = bf16[128,16,256]{2,1,0:T(8,128)(2,1)S(1)} collective-permute-done((bf16[128,16,256]{2,1,0:T(8,128)(2,1)S(1)}, bf16[128,16,256]{2,1,0:T(8,128)(2,1)S(1)}, u32[]{:S(2)}, u32[]{:S(2)}) %collective-permute-start) | collective-permute-done | bytes 1048608 | tf_op jit(solution)/shard_map/ppermute | solution.py:248
  55.0 1.5 %left_edges.10 = (f32[1024,128]{1,0:T(8,128)S(1)}, f32[1024,128]{1,0:T(8,128)S(1)}) custom-call(s32[1]{0:T(128)} %bitcast.me_ref, s32[256]{0:T(256)S(1)} %copy-done.5, bf16[8,256,128]{2,1,0:T(8,128)(2,1)S(1)} %collective-permute-done.12.pair_ref.rest_4_, s32[1,256]{1,0:T(1,128)S(1)} %bitcast.7, f32[1,128]{1,0:T(1,128)S(1)} %bitcast.14, ...), custom_call_target="tpu_custom_call" | custom-call | flops 34359738368 | bytes 1024 | tf_op jit(solution)/shard_map/left_edges/pallas_call | solution.py:198
  56.5 1.2 %collective-permute-done.2.rest_3_ = bf16[128,16,256]{2,1,0:T(8,128)(2,1)S(1)} collective-permute-done((bf16[128,16,256]{2,1,0:T(8,128)(2,1)S(1)}, bf16[128,16,256]{2,1,0:T(8,128)(2,1)S(1)}, u32[]{:S(2)}, u32[]{:S(2)}) %collective-permute-start.2) | collective-permute-done | bytes 1048608 | tf_op jit(solution)/shard_map/ppermute | solution.py:248
  58.3 4.5 %triangle.4 = (bf16[16,16,128]{2,1,0:T(8,128)(2,1)S(1)}, bf16[16,16,128]{2,1,0:T(8,128)(2,1)S(1)}, bf16[16,16,128]{2,1,0:T(8,128)(2,1)S(1)}, bf16[16,16,128]{2,1,0:T(8,128)(2,1)S(1)}) custom-call(s32[1]{0:T(128)} %bitcast.me_ref, f32[128]{0:T(128)S(1)} %copy-done.9, f32[1,128]{1,0:T(1,128)S(1)} %bitcast.15, bf16[128,128]{1,0:T(8,128)(2,1)S(1)} %copy-done.1, ...), custom_call_target="tpu_custom_call" | custom-call | flops 1048576 | bytes 1024 | tf_op jit(solution)/shard_map/triangle/pallas_call | solution.py:217
  64.7 1.4 %left_edges.11 = (f32[1024,128]{1,0:T(8,128)S(1)}, f32[1024,128]{1,0:T(8,128)S(1)}) custom-call(s32[1]{0:T(128)} %bitcast.me_ref, s32[256]{0:T(256)S(1)} %copy-done.5, bf16[8,256,128]{2,1,0:T(8,128)(2,1)S(1)} %collective-permute-done.13.pair_ref.rest_5_, s32[1,256]{1,0:T(1,128)S(1)} %bitcast.8, f32[1,128]{1,0:T(1,128)S(1)} %bitcast.16, ...), custom_call_target="tpu_custom_call" | custom-call | flops 34359738368 | bytes 1024 | tf_op jit(solution)/shard_map/left_edges/pallas_call | solution.py:198
  66.2 2.7 %left_edges.7 = (f32[2048,128]{1,0:T(8,128)S(1)}, f32[2048,128]{1,0:T(8,128)S(1)}) custom-call(s32[1]{0:T(128)} %bitcast.me_ref, s32[256]{0:T(256)S(1)} %copy-done.5, bf16[16,256,128]{2,1,0:T(8,128)(2,1)S(1)} %collective-permute-done.3.pair_ref.rest_5_, s32[1,256]{1,0:T(1,128)S(1)} %bitcast.9, f32[1,128]{1,0:T(1,128)S(1)} %bitcast.17, ...), custom_call_target="tpu_custom_call" | custom-call | flops 1048576 | bytes 1024 | tf_op jit(solution)/shard_map/left_edges/pallas_call | solution.py:198
  68.9 6.8 %triangle.3 = (bf16[32,16,128]{2,1,0:T(8,128)(2,1)S(1)}, bf16[32,16,128]{2,1,0:T(8,128)(2,1)S(1)}, bf16[32,16,128]{2,1,0:T(8,128)(2,1)S(1)}, bf16[32,16,128]{2,1,0:T(8,128)(2,1)S(1)}) custom-call(s32[1]{0:T(128)} %bitcast.me_ref, f32[128]{0:T(128)S(1)} %copy-done.9, f32[1,128]{1,0:T(1,128)S(1)} %bitcast.18, bf16[128,128]{1,0:T(8,128)(2,1)S(1)} %copy-done.1, ...), custom_call_target="tpu_custom_call" | custom-call | flops 1048576 | bytes 1024 | tf_op jit(solution)/shard_map/triangle/pallas_call | solution.py:217
  75.7 2.5 %collective-permute-start.4 = (bf16[32,16,128]{2,1,0:T(8,128)(2,1)S(1)}, bf16[32,16,128]{2,1,0:T(8,128)(2,1)S(1)}, u32[]{:S(2)}, u32[]{:S(2)}) collective-permute-start(bf16[32,16,128]{2,1,0:T(8,128)(2,1)S(1)} %get-tuple-element.38), channel_id=1, source_target_pairs={{0,4},{1,5},{2,6},{3,7},{4,0},{5,1},{6,2},{7,3},{8,12},{9,13},{10,... | collective-permute-start | bytes 393224 | tf_op jit(solution)/shard_map/ppermute | solution.py:248
  78.2 4.4 %triangle.5 = (bf16[16,16,128]{2,1,0:T(8,128)(2,1)S(1)}, bf16[16,16,128]{2,1,0:T(8,128)(2,1)S(1)}, bf16[16,16,128]{2,1,0:T(8,128)(2,1)S(1)}, bf16[16,16,128]{2,1,0:T(8,128)(2,1)S(1)}) custom-call(s32[1]{0:T(128)} %bitcast.me_ref, f32[128]{0:T(128)S(1)} %copy-done.9, f32[1,128]{1,0:T(1,128)S(1)} %bitcast.19, bf16[128,128]{1,0:T(8,128)(2,1)S(1)} %copy-done.1, ...), custom_call_target="tpu_custom_call" | custom-call | flops 1048576 | bytes 1024 | tf_op jit(solution)/shard_map/triangle/pallas_call | solution.py:217
  82.8 1.8 %collective-permute-start.5 = (bf16[32,16,128]{2,1,0:T(8,128)(2,1)S(1)}, bf16[32,16,128]{2,1,0:T(8,128)(2,1)S(1)}, u32[]{:S(2)}, u32[]{:S(2)}) collective-permute-start(bf16[32,16,128]{2,1,0:T(8,128)(2,1)S(1)} %get-tuple-element.39), channel_id=1, source_target_pairs={{0,1},{1,0},{2,3},{3,2},{4,5},{5,4},{6,7},{7,6},{8,9},{9,8},{10,11... | collective-permute-start | bytes 393224 | tf_op jit(solution)/shard_map/ppermute | solution.py:248
  85.1 2.0 %collective-permute-done.14.rest_9_ = bf16[16,16,128]{2,1,0:T(8,128)(2,1)S(1)} collective-permute-done((bf16[16,16,128]{2,1,0:T(8,128)(2,1)S(1)}, bf16[16,16,128]{2,1,0:T(8,128)(2,1)S(1)}, u32[]{:S(2)}, u32[]{:S(2)}) %collective-permute-start.14) | collective-permute-done | bytes 65568 | tf_op jit(solution)/shard_map/ppermute | solution.py:248
  87.6 4.0 %collective-permute-done.16.rest_11_ = bf16[16,16,128]{2,1,0:T(8,128)(2,1)S(1)} collective-permute-done((bf16[16,16,128]{2,1,0:T(8,128)(2,1)S(1)}, bf16[16,16,128]{2,1,0:T(8,128)(2,1)S(1)}, u32[]{:S(2)}, u32[]{:S(2)}) %collective-permute-start.16) | collective-permute-done | bytes 65568 | tf_op jit(solution)/shard_map/ppermute | solution.py:248
  (42 shorter events, 6.0 us)
Async XLA Ops:
  0.0 5.5 %copy-start = (bf16[16,256,128]{2,1,0:T(8,128)(2,1)S(1)}, bf16[16,256,128]{2,1,0:T(8,128)(2,1)}, u32[]{:S(2)}) copy-start(bf16[16,256,128]{2,1,0:T(8,128)(2,1)} %rest_4_.1) | copy-start | bytes 3145732
  0.0 5.5 %copy-start.6 = (bf16[128,128]{1,0:T(8,128)(2,1)S(1)}, bf16[128,128]{1,0:T(8,128)(2,1)}, u32[]{:S(2)}) copy-start(bf16[128,128]{1,0:T(8,128)(2,1)} %gate_ref.7) | copy-start | bytes 98308
  0.0 5.5 %copy-start.7 = (bf16[128,128]{1,0:T(8,128)(2,1)S(1)}, bf16[128,128]{1,0:T(8,128)(2,1)}, u32[]{:S(2)}) copy-start(bf16[128,128]{1,0:T(8,128)(2,1)} %value_ref.7) | copy-start | bytes 98308
  1.4 28.2 %collective-permute-start.7 = (bf16[8,256,128]{2,1,0:T(8,128)(2,1)S(1)}, bf16[8,256,128]{2,1,0:T(8,128)(2,1)S(1)}, u32[]{:S(2)}, u32[]{:S(2)}) collective-permute-start(bf16[8,256,128]{2,1,0:T(8,128)(2,1)S(1)} %get-tuple-element.58), channel_id=1, source_target_pairs={{0,8},{1,9},{2,10},{3,11},{4,12},{5,13},{6,14},{7,15},{8,0},{9,1},... | collective-permute-start | bytes 1572872 | tf_op jit(solution)/shard_map/ppermute | solution.py:248
  6.2 6.3 %copy-start.3 = (bf16[128,128]{1,0:T(8,128)(2,1)S(1)}, bf16[128,128]{1,0:T(8,128)(2,1)}, u32[]{:S(2)}) copy-start(bf16[128,128]{1,0:T(8,128)(2,1)} %gate_ref.13) | copy-start | bytes 98308
  6.2 6.3 %copy-start.4 = (bf16[128,128]{1,0:T(8,128)(2,1)S(1)}, bf16[128,128]{1,0:T(8,128)(2,1)}, u32[]{:S(2)}) copy-start(bf16[128,128]{1,0:T(8,128)(2,1)} %value_ref.13) | copy-start | bytes 98308
  9.0 46.0 %collective-permute-start = (bf16[128,16,256]{2,1,0:T(8,128)(2,1)S(1)}, bf16[128,16,256]{2,1,0:T(8,128)(2,1)S(1)}, u32[]{:S(2)}, u32[]{:S(2)}) collective-permute-start(bf16[128,16,256]{2,1,0:T(8,128)(2,1)S(1)} %edges.1.rest_0_), channel_id=1, source_target_pairs={{0,4},{1,5},{2,6},{3,7},{4,0},{5,1},{6,2},{7,3},{8,12},{9,13},{10,... | collective-permute-start | bytes 3145736 | tf_op jit(solution)/shard_map/ppermute | solution.py:248
  10.6 45.8 %collective-permute-start.1 = (bf16[128,16,256]{2,1,0:T(8,128)(2,1)S(1)}, bf16[128,16,256]{2,1,0:T(8,128)(2,1)S(1)}, u32[]{:S(2)}, u32[]{:S(2)}) collective-permute-start(bf16[128,16,256]{2,1,0:T(8,128)(2,1)S(1)} %edges.1.rest_0_), channel_id=1, source_target_pairs={{0,1},{1,0},{2,3},{3,2},{4,5},{5,4},{6,7},{7,6},{8,9},{9,8},{10,11... | collective-permute-start | bytes 3145736 | tf_op jit(solution)/shard_map/ppermute | solution.py:248
  10.6 55.6 %collective-permute-start.3 = (bf16[16,256,128]{2,1,0:T(8,128)(2,1)S(1)}, bf16[16,256,128]{2,1,0:T(8,128)(2,1)S(1)}, u32[]{:S(2)}, u32[]{:S(2)}) collective-permute-start(bf16[16,256,128]{2,1,0:T(8,128)(2,1)S(1)} %copy-done), channel_id=1, source_target_pairs={{0,2},{1,3},{2,0},{3,1},{4,6},{5,7},{6,4},{7,5},{8,10},{9,11},{10,... | collective-permute-start | bytes 3145736 | tf_op jit(solution)/shard_map/ppermute | solution.py:248
  12.2 38.2 %collective-permute-start.8 = (bf16[8,256,128]{2,1,0:T(8,128)(2,1)S(1)}, bf16[8,256,128]{2,1,0:T(8,128)(2,1)S(1)}, u32[]{:S(2)}, u32[]{:S(2)}) collective-permute-start(bf16[8,256,128]{2,1,0:T(8,128)(2,1)S(1)} %get-tuple-element.57), channel_id=1, source_target_pairs={{0,8},{1,9},{2,10},{3,11},{4,12},{5,13},{6,14},{7,15},{8,0},{9,1},... | collective-permute-start | bytes 1572872 | tf_op jit(solution)/shard_map/ppermute | solution.py:248
  31.0 24.0 %collective-permute-start.12 = (bf16[8,256,128]{2,1,0:T(8,128)(2,1)S(1)}, bf16[8,256,128]{2,1,0:T(8,128)(2,1)S(1)}, u32[]{:S(2)}, u32[]{:S(2)}) collective-permute-start(bf16[8,256,128]{2,1,0:T(8,128)(2,1)S(1)} %collective-permute-done.7.pair_ref.rest_4_), channel_id=1, source_target_pairs={{0,2},{1,3},{2,0},{3,1},{4,6},{5,7},{6,4},{7,5},{8,10},{9,11},{10,... | collective-permute-start | bytes 1572872 | tf_op jit(solution)/shard_map/ppermute | solution.py:248
  51.9 5.8 %copy-start.1 = (bf16[128,128]{1,0:T(8,128)(2,1)S(1)}, bf16[128,128]{1,0:T(8,128)(2,1)}, u32[]{:S(2)}) copy-start(bf16[128,128]{1,0:T(8,128)(2,1)} %output_gate_ref.5) | copy-start | bytes 98308
  51.9 5.8 %copy-start.2 = (bf16[128,128]{1,0:T(8,128)(2,1)S(1)}, bf16[128,128]{1,0:T(8,128)(2,1)}, u32[]{:S(2)}) copy-start(bf16[128,128]{1,0:T(8,128)(2,1)} %output_value_ref.5) | copy-start | bytes 98308
  51.9 12.9 %collective-permute-start.13 = (bf16[8,256,128]{2,1,0:T(8,128)(2,1)S(1)}, bf16[8,256,128]{2,1,0:T(8,128)(2,1)S(1)}, u32[]{:S(2)}, u32[]{:S(2)}) collective-permute-start(bf16[8,256,128]{2,1,0:T(8,128)(2,1)S(1)} %collective-permute-done.8.pair_ref.rest_5_), channel_id=1, source_target_pairs={{0,2},{1,3},{2,0},{3,1},{4,6},{5,7},{6,4},{7,5},{8,10},{9,11},{10,... | collective-permute-start | bytes 1572872 | tf_op jit(solution)/shard_map/ppermute | solution.py:248
  55.0 2.7 %collective-permute-start.2 = (bf16[128,16,256]{2,1,0:T(8,128)(2,1)S(1)}, bf16[128,16,256]{2,1,0:T(8,128)(2,1)S(1)}, u32[]{:S(2)}, u32[]{:S(2)}) collective-permute-start(bf16[128,16,256]{2,1,0:T(8,128)(2,1)S(1)} %collective-permute-done.rest_1_), channel_id=1, source_target_pairs={{0,1},{1,0},{2,3},{3,2},{4,5},{5,4},{6,7},{7,6},{8,9},{9,8},{10,11... | collective-permute-start | bytes 3145736 | tf_op jit(solution)/shard_map/ppermute | solution.py:248
  62.8 20.0 %collective-permute-start.9 = (bf16[16,16,128]{2,1,0:T(8,128)(2,1)S(1)}, bf16[16,16,128]{2,1,0:T(8,128)(2,1)S(1)}, u32[]{:S(2)}, u32[]{:S(2)}) collective-permute-start(bf16[16,16,128]{2,1,0:T(8,128)(2,1)S(1)} %get-tuple-element.46), channel_id=1, source_target_pairs={{0,4},{1,5},{2,6},{3,7},{4,0},{5,1},{6,2},{7,3},{8,12},{9,13},{10,... | collective-permute-start | bytes 196616 | tf_op jit(solution)/shard_map/ppermute | solution.py:248
  63.7 20.9 %collective-permute-start.10 = (bf16[16,16,128]{2,1,0:T(8,128)(2,1)S(1)}, bf16[16,16,128]{2,1,0:T(8,128)(2,1)S(1)}, u32[]{:S(2)}, u32[]{:S(2)}) collective-permute-start(bf16[16,16,128]{2,1,0:T(8,128)(2,1)S(1)} %get-tuple-element.47), channel_id=1, source_target_pairs={{0,1},{1,0},{2,3},{3,2},{4,5},{5,4},{6,7},{7,6},{8,9},{9,8},{10,11... | collective-permute-start | bytes 196616 | tf_op jit(solution)/shard_map/ppermute | solution.py:248
  75.7 15.8 %collective-permute-start.4 = (bf16[32,16,128]{2,1,0:T(8,128)(2,1)S(1)}, bf16[32,16,128]{2,1,0:T(8,128)(2,1)S(1)}, u32[]{:S(2)}, u32[]{:S(2)}) collective-permute-start(bf16[32,16,128]{2,1,0:T(8,128)(2,1)S(1)} %get-tuple-element.38), channel_id=1, source_target_pairs={{0,4},{1,5},{2,6},{3,7},{4,0},{5,1},{6,2},{7,3},{8,12},{9,13},{10,... | collective-permute-start | bytes 393224 | tf_op jit(solution)/shard_map/ppermute | solution.py:248
  78.2 6.7 %collective-permute-start.11 = (bf16[16,16,128]{2,1,0:T(8,128)(2,1)S(1)}, bf16[16,16,128]{2,1,0:T(8,128)(2,1)S(1)}, u32[]{:S(2)}, u32[]{:S(2)}) collective-permute-start(bf16[16,16,128]{2,1,0:T(8,128)(2,1)S(1)} %get-tuple-element.48), channel_id=1, source_target_pairs={{0,5},{1,4},{2,7},{3,6},{4,1},{5,0},{6,3},{7,2},{8,13},{9,12},{10,... | collective-permute-start | bytes 196616 | tf_op jit(solution)/shard_map/ppermute | solution.py:248
  82.6 4.5 %collective-permute-start.14 = (bf16[16,16,128]{2,1,0:T(8,128)(2,1)S(1)}, bf16[16,16,128]{2,1,0:T(8,128)(2,1)S(1)}, u32[]{:S(2)}, u32[]{:S(2)}) collective-permute-start(bf16[16,16,128]{2,1,0:T(8,128)(2,1)S(1)} %get-tuple-element.54), channel_id=1, source_target_pairs={{0,4},{1,5},{2,6},{3,7},{4,0},{5,1},{6,2},{7,3},{8,12},{9,13},{10,... | collective-permute-start | bytes 196616 | tf_op jit(solution)/shard_map/ppermute | solution.py:248
  82.8 8.7 %collective-permute-start.5 = (bf16[32,16,128]{2,1,0:T(8,128)(2,1)S(1)}, bf16[32,16,128]{2,1,0:T(8,128)(2,1)S(1)}, u32[]{:S(2)}, u32[]{:S(2)}) collective-permute-start(bf16[32,16,128]{2,1,0:T(8,128)(2,1)S(1)} %get-tuple-element.39), channel_id=1, source_target_pairs={{0,1},{1,0},{2,3},{3,2},{4,5},{5,4},{6,7},{7,6},{8,9},{9,8},{10,11... | collective-permute-start | bytes 393224 | tf_op jit(solution)/shard_map/ppermute | solution.py:248
  84.6 7.0 %collective-permute-start.6 = (bf16[32,16,128]{2,1,0:T(8,128)(2,1)S(1)}, bf16[32,16,128]{2,1,0:T(8,128)(2,1)S(1)}, u32[]{:S(2)}, u32[]{:S(2)}) collective-permute-start(bf16[32,16,128]{2,1,0:T(8,128)(2,1)S(1)} %get-tuple-element.40), channel_id=1, source_target_pairs={{0,5},{1,4},{2,7},{3,6},{4,1},{5,0},{6,3},{7,2},{8,13},{9,12},{10,... | collective-permute-start | bytes 393224 | tf_op jit(solution)/shard_map/ppermute | solution.py:248
  84.9 2.7 %collective-permute-start.15 = (bf16[16,16,128]{2,1,0:T(8,128)(2,1)S(1)}, bf16[16,16,128]{2,1,0:T(8,128)(2,1)S(1)}, u32[]{:S(2)}, u32[]{:S(2)}) collective-permute-start(bf16[16,16,128]{2,1,0:T(8,128)(2,1)S(1)} %get-tuple-element.55), channel_id=1, source_target_pairs={{0,1},{1,0},{2,3},{3,2},{4,5},{5,4},{6,7},{7,6},{8,9},{9,8},{10,11... | collective-permute-start | bytes 196616 | tf_op jit(solution)/shard_map/ppermute | solution.py:248
  87.1 4.4 %collective-permute-start.16 = (bf16[16,16,128]{2,1,0:T(8,128)(2,1)S(1)}, bf16[16,16,128]{2,1,0:T(8,128)(2,1)S(1)}, u32[]{:S(2)}, u32[]{:S(2)}) collective-permute-start(bf16[16,16,128]{2,1,0:T(8,128)(2,1)S(1)} %get-tuple-element.56), channel_id=1, source_target_pairs={{0,5},{1,4},{2,7},{3,6},{4,1},{5,0},{6,3},{7,2},{8,13},{9,12},{10,... | collective-permute-start | bytes 196616 | tf_op jit(solution)/shard_map/ppermute | solution.py:248
  (3 other events, 2.0 us)

commit v3 on v2

--- a/solution.py
+++ b/solution.py
@@ -54,7 +54,7 @@
             ]
         return carry
 
-    lax.fori_loop(0, rows, one_row, 0, unroll=8)
+    lax.fori_loop(0, rows, one_row, 0, unroll=min(rows, 8))
 
 
 def read_edges(edges, start, size):
@@ -73,10 +73,18 @@
     lax.fori_loop(0, out_ref.shape[0], one_channel, 0, unroll=16)
 
 
-def left_kernel(unit, offset, me_ref, chain_ref, pair_ref, mask_ref, gain_ref, gate_ref, value_ref, *edges):
-    rows = pair_ref.shape[0]
-    first = (me_ref[0] ^ unit) * offset[1] + offset[0]
-    fill_edges(first, 0, rows, pair_ref, chain_ref, mask_ref, gain_ref, (gate_ref, value_ref), edges)
+def left_kernel(unit, span, offsets, keep, me_ref, chain_ref, mask_ref, gain_ref, gate_ref, value_ref, *rest):
+    count = len(offsets)
+    pair_refs, edges = rest[:count], rest[count:]
+    if keep:
+        edges, copy_ref = edges[:-1], edges[-1]
+        copy_ref[...] = pair_refs[0][...]
+    total = sum(ref.shape[0] for ref in pair_refs)
+    at = 0
+    for offset, pair_ref in zip(offsets, pair_refs):
+        first = (me_ref[0] ^ unit) * span + offset
+        fill_edges(first, at, total, pair_ref, chain_ref, mask_ref, gain_ref, (gate_ref, value_ref), edges)
+        at += pair_ref.shape[0]
 
 
 def triangle_kernel(
@@ -87,7 +95,8 @@
     pair_refs, rest = rest[:count], rest[count:]
     out_refs, triangle = rest[-1 - units : -1], rest[-1]
     parts = pair_refs[0].shape[1] // LANES
-    left_refs = [rest[n * parts : (n + 1) * parts] for n in range(count)]
+    left_refs = [rest[n * parts : (n + 1) * parts] for n in range((len(rest) - 1 - units) // parts)]
+    left_sizes = [refs[0].shape[0] // output_value_ref.shape[0] for refs in left_refs]
     me = me_ref[0]
     sizes = [ref.shape[0] for ref in pair_refs]
     rows = sum(sizes)
@@ -99,7 +108,7 @@
     def read_left(h):
         whole = [
             jnp.concatenate([ref[pl.ds(pl.multiple_of(h * size, size), size), :] for ref in refs], axis=1)
-            for refs, size in zip(left_refs, sizes)
+            for refs, size in zip(left_refs, left_sizes)
         ]
         return jnp.concatenate(whole, axis=0).astype(NARROW)
 
@@ -150,7 +159,7 @@
                 out_refs[u][row] = updated[u * width : (u + 1) * width]
             return carry
 
-        lax.fori_loop(0, sizes[n], finish, 0, unroll=4)
+        lax.fori_loop(0, sizes[n], finish, 0, unroll=min(sizes[n], 4))
 
 
 def place_kernel(places, me_ref, *rest):
@@ -173,40 +182,51 @@
         copy.wait()
 
 
+def behind(kernel, count):
+    def body(*refs):
+        kernel(*refs[count:])
+
+    return body
+
+
 def edge_scratch(rows, hidden, residues):
     return [pltpu.VMEM((hidden * rows, LANES), WIDE_TYPE)] * (residues // LANES)
 
 
-def edge_call(unit, me, chain, pair, mask, gain, gate, value):
+def edge_call(deps, unit, me, chain, pair, mask, gain, gate, value):
     rows, residues, _ = pair.shape
     hidden = gate.shape[1]
     return pl.pallas_call(
-        functools.partial(edge_kernel, unit),
+        behind(functools.partial(edge_kernel, unit), len(deps)),
         out_shape=jax.ShapeDtypeStruct((hidden, rows, residues), NARROW),
-        in_specs=[SMEM] * 2 + [VMEM] * 5,
+        in_specs=[ANY] * len(deps) + [SMEM] * 2 + [VMEM] * 5,
         out_specs=VMEM,
         scratch_shapes=edge_scratch(rows, hidden, residues),
         compiler_params=pltpu.CompilerParams(vmem_limit_bytes=16 << 20),
         cost_estimate=pl.CostEstimate(flops=1 << 20, bytes_accessed=1 << 10, transcendentals=0),
         name="edges",
-    )(me, chain, pair, mask, gain, gate, value)
-
-
-def left_call(unit, offset, cost, me, chain, pair, mask, gain, gate, value):
-    rows, residues, _ = pair.shape
+    )(*deps, me, chain, pair, mask, gain, gate, value)
+
+
+def left_call(deps, unit, span, offsets, keep, cost, me, chain, mask, gain, gate, value, pairs):
+    rows = sum(p.shape[0] for p in pairs)
+    residues = pairs[0].shape[1]
     hidden = gate.shape[1]
-    return pl.pallas_call(
-        functools.partial(left_kernel, unit, offset),
-        out_shape=[jax.ShapeDtypeStruct((hidden * rows, LANES), WIDE_TYPE)] * (residues // LANES),
-        in_specs=[SMEM] * 2 + [VMEM] * 5,
-        out_specs=[VMEM] * (residues // LANES),
+    shapes = [jax.ShapeDtypeStruct((hidden * rows, LANES), WIDE_TYPE)] * (residues // LANES)
+    if keep:
+        shapes.append(jax.ShapeDtypeStruct(pairs[0].shape, NARROW))
+    return pl.pallas_call(
+        behind(functools.partial(left_kernel, unit, span, offsets, keep), len(deps)),
+        out_shape=shapes,
+        in_specs=[ANY] * len(deps) + [SMEM] * 2 + [VMEM] * (4 + len(pairs)),
+        out_specs=[VMEM] * len(shapes),
         compiler_params=pltpu.CompilerParams(vmem_limit_bytes=16 << 20),
         cost_estimate=cost,
         name="left_edges",
-    )(me, chain, pair, mask, gain, gate, value)
-
-
-def triangle_call(order, me, middle_gain, gain, output_gate, output_value, right, pairs, lefts):
+    )(*deps, me, chain, mask, gain, gate, value, *pairs)
+
+
+def triangle_call(deps, order, me, middle_gain, gain, output_gate, output_value, right, pairs, lefts):
     _, _, channels = pairs[0].shape
     rows = sum(p.shape[0] for p in pairs)
     hidden = output_value.shape[0]
@@ -215,15 +235,15 @@
     for left in lefts:
         tensors += left
     return pl.pallas_call(
-        functools.partial(triangle_kernel, len(pairs), order),
+        behind(functools.partial(triangle_kernel, len(pairs), order), len(deps)),
         out_shape=[jax.ShapeDtypeStruct((rows, width, channels), NARROW)] * len(order),
-        in_specs=[SMEM] * 2 + [VMEM] * len(tensors),
+        in_specs=[ANY] * len(deps) + [SMEM] * 2 + [VMEM] * len(tensors),
         out_specs=[VMEM] * len(order),
         scratch_shapes=[pltpu.VMEM((hidden * rows, LANES), WIDE_TYPE)],
         compiler_params=pltpu.CompilerParams(vmem_limit_bytes=40 << 20),
         cost_estimate=pl.CostEstimate(flops=1 << 20, bytes_accessed=1 << 10, transcendentals=0),
         name="triangle",
-    )(me, middle_gain, *tensors)
+    )(*deps, me, middle_gain, *tensors)
 
 
 def place_call(places, me, blocks, shape):
@@ -238,11 +258,27 @@
     )(me, *blocks)
 
 
+def hold_kernel(*refs):
+    pass
+
+
+def hold(value, *deps):
+    return pl.pallas_call(
+        hold_kernel,
+        out_shape=jax.ShapeDtypeStruct(value.shape, value.dtype),
+        in_specs=[ANY] * (1 + len(deps)),
+        out_specs=ANY,
+        input_output_aliases={0: 0},
+        compiler_params=pltpu.CompilerParams(vmem_limit_bytes=1 << 20),
+        cost_estimate=SHORT,
+        name="hold",
+    )(value, *deps)
+
+
 def make_shards(count):
     bits = [1 << b for b in range(count.bit_length() - 1)]
     right_bits = bits[0::2][::-1]
     left_bits = bits[1::2][::-1]
-    pieces = 2
 
     def swap(values, mask):
         return lax.ppermute(values, "wide", [(d, d ^ mask) for d in range(count)])
@@ -263,57 +299,70 @@
         me = lax.axis_index("wide").astype(jnp.int32).reshape(1)
         mask = residue_mask.reshape(1, -1)
         gain = input_gain.reshape(1, -1)
-        part = rows // pieces
         far_bit, near_bits = left_bits[0], left_bits[1:]
-
-        far = [swap(pair[n * part : (n + 1) * part], far_bit) for n in range(pieces)]
-        near = {0: pair}
-        for bit in near_bits:
-            for unit in list(near):
-                near[unit | bit] = swap(near[unit], bit)
-        own_right = edge_call(0, me, residue_mask, pair, mask, gain, right_gate, right_value)
-        right = {0: own_right}
-        for bit in right_bits:
-            for unit in list(right):
-                right[unit | bit] = swap(right[unit], bit)
-        order = list(right)
-        rights = [right[unit] for unit in order]
-
-        far_units = {far_bit: far}
-        for bit in near_bits:
-            for unit in list(far_units):
-                far_units[unit | bit] = [swap(piece, bit) for piece in far_units[unit]]
+        cuts = [(0, rows // 2), (rows // 2, rows // 2)]
+
+        def gather(own, bits):
+            units = {0: own}
+            for bit in bits:
+                for unit in list(units):
+                    units[unit | bit] = swap(units[unit], bit)
+            return units
+
+        def left_edges(deps, unit, pieces, cost, raws, keep=False):
+            offsets = tuple(start for start, _ in pieces)
+            return left_call(
+                deps, unit, rows, offsets, keep, cost, me, residue_mask, mask, gain, left_gate, left_value, raws
+            )
 
         blocks = []
         places = []
 
-        def left_edges(unit, offset, raw, cost):
-            return left_call(
-                unit, (offset, rows), cost, me, residue_mask, raw, mask, gain, left_gate, left_value
-            )
-
-        def finish(firsts, pairs, lefts):
+        def finish(deps, sources, pairs, lefts):
             outs = triangle_call(
-                order, me, middle_gain, gain, output_gate, output_value, rights, pairs, lefts
+                deps, order, me, middle_gain, gain, output_gate, output_value, rights, pairs, lefts
             )
             for unit, out in zip(order, outs):
                 blocks.append(out if unit == 0 else swap(out, unit))
                 place, start = [], 0
-                for (left_unit, offset), source in zip(firsts, pairs):
+                for (left_unit, offset), source in zip(sources, pairs):
                     place.append((left_unit | unit, start, source.shape[0], offset, rows))
                     start += source.shape[0]
                 places.append(place)
-
+            return outs[0]
+
+        whole = ((0, rows),)
+        far = [swap(pair[start : start + size], far_bit) for start, size in cuts]
+        near = gather(pair, near_bits)
+        own_right = edge_call((), 0, me, residue_mask, pair, mask, gain, right_gate, right_value)
         lefts = []
-        after = own_right
         for unit, raw in near.items():
-            raw, after = lax.optimization_barrier((raw, after))
-            lefts.append(left_edges(unit, 0, raw, SHORT))
-            after = lefts[-1][0]
-        finish([(unit, 0) for unit in near], list(near.values()), lefts)
-        for unit, raws in far_units.items():
-            lefts = [left_edges(unit, n * part, raws[n], LONG) for n in range(pieces)]
-            finish([(unit, n * part) for n in range(pieces)], raws, lefts)
+            cost = LONG if unit else SHORT
+            lefts.append(left_edges(() if unit else (own_right,), unit, whole, cost, [raw]))
+        far_first = left_edges((), far_bit, cuts[:1], LONG, far[:1])
+
+        right = {0: own_right}
+        for bit in right_bits:
+            for unit in list(right):
+                moved = swap(right[unit], bit)
+                if bit == right_bits[0]:
+                    moved = hold(moved, far_first[0], lefts[0][0])
+                right[unit | bit] = moved
+        order = list(right)
+        rights = [right[unit] for unit in order]
+
+        far_last = left_edges((), far_bit, cuts[1:], SHORT, far[1:])
+        done = finish(
+            (),
+            [(unit, 0) for unit in near] + [(far_bit, start) for start, _ in cuts],
+            list(near.values()) + far,
+            lefts + [far_first, far_last],
+        )
+        pieces = [gather(piece, near_bits) for piece in far]
+        for unit in list(near)[1:]:
+            raws = [piece[unit] for piece in pieces]
+            edges = left_edges((done,), far_bit | unit, cuts, SHORT, raws)
+            finish((), [(far_bit | unit, start) for start, _ in cuts], raws, [edges])
         return place_call(places, me, blocks, (count * rows, rows, pair.shape[2]))
 
     return shards

time: 92.9 us -> 85.2 us (0.917)
  Pallas kernels: 30.9 us -> 27.3 us
  starting transfers between devices: 17.4 us -> 14.2 us
    pallas_call x10 -> x9, Pallas kernels: 29.7 us -> 26.1 us  [the longest x2 12.6 us: triangle_call(): pl.pallas_call(behind(functools.partial(triangle_kernel, len(pairs), orde...]
    ppermute x17 -> x14, starting transfers between devices: 17.4 us -> 14.2 us  [swap(): return lax.ppermute(values, 'wide', [(d, d ^ mask) for d in range(count)])]
    ppermute x17 -> x14, waiting for transfers between devices: 41.6 us -> 40.7 us  [swap(): return lax.ppermute(values, 'wide', [(d, d ^ mask) for d in range(count)])]
  transfers between devices with their start and end apart: 17 -> 14, of which waited for: 7 -> 5; matrix products, arithmetic and copies ran while one was open for 0% -> 0% of each run, Pallas kernels for 32% -> 31%
where the time goes in v3:
time: 85.2 us; the launch traced here: 85 us
  waiting for transfers between devices  40.7 us (48%)
  Pallas kernels  27.3 us (32%)
  starting transfers between devices  14.2 us (17%)
  local copies, waits for them, and re-layouts  2.68 us (3%)
    ppermute x14, waiting for transfers between devices, swap(): return lax.ppermute(values, 'wide', [(d, d ^ mask) for d in range(count)])  40.7 us
    ppermute x14, starting transfers between devices, swap(): return lax.ppermute(values, 'wide', [(d, d ^ mask) for d in range(count)])  14.2 us
    pallas_call x2, Pallas kernels, triangle_call(): pl.pallas_call(behind(functools.partial(triangle_kernel, len(pairs), orde...  12.6 us
    pallas_call x5, Pallas kernels, left_call(): pl.pallas_call(behind(functools.partial(left_kernel, unit, span, offsets,...  10.7 us
    pallas_call x1, Pallas kernels, edge_call(): pl.pallas_call(behind(functools.partial(edge_kernel, unit), len(deps)), o...  2.82 us
  transfers between devices with their start and end apart: 14, of which 5 were waited for; matrix products, arithmetic and copies ran while one was open for 0% of the time, Pallas kernels for 31%

profile of v3, /device:TPU:0, one launch (start us, length us, event | category | flops | bytes accessed | tf_op | source)
XLA Modules:
  0.0 85.0 jit_solution(2521485649332483877)
XLA Ops:
  0.0 1.4 %fusion = (bf16[8,256,128]{2,1,0:T(8,128)(2,1)S(1)}, bf16[8,256,128]{2,1,0:T(8,128)(2,1)S(1)}) fusion(bf16[16,256,128]{2,1,0:T(8,128)(2,1)} %refs_9_.1), kind=kLoop, calls=%fused_computation | loop fusion | bytes 2097152 | tf_op jit(solution)/shard_map/slice | solution.py:335
  1.4 4.1 %collective-permute-start.1 = (bf16[8,256,128]{2,1,0:T(8,128)(2,1)S(1)}, bf16[8,256,128]{2,1,0:T(8,128)(2,1)S(1)}, u32[]{:S(2)}, u32[]{:S(2)}) collective-permute-start(bf16[8,256,128]{2,1,0:T(8,128)(2,1)S(1)} %get-tuple-element.42), channel_id=1, source_target_pairs={{0,8},{1,9},{2,10},{3,11},{4,12},{5,13},{6,14},{7,15},{8,0},{9,1},... | collective-permute-start | bytes 1572872 | tf_op jit(solution)/shard_map/ppermute | solution.py:284
  5.5 0.7 copy-done.5
  6.2 2.8 %edges.1.refs_0_.refs_5_ = bf16[128,16,256]{2,1,0:T(8,128)(2,1)S(1)} custom-call(s32[1]{0:T(128)} %bitcast.refs_0_.refs_1_.me_ref, s32[256]{0:T(256)S(1)} %copy-done.5, bf16[16,256,128]{2,1,0:T(8,128)(2,1)S(1)} %copy-done, s32[1,256]{1,0:T(1,128)S(1)} %bitcast.3, f32[1,128]{1,0:T(1,128)S(1)} %bitcast.9, bf16[128,128]{1,0:T(8,128)(2,1)S(1)} %copy-done.6, ...), custom_call_target="tpu_custom_call" | custom-call | flops 1048576 | bytes 1024 | tf_op jit(solution)/shard_map/edges/pallas_call | solution.py:199
  9.0 1.7 %collective-permute-start = (bf16[128,16,256]{2,1,0:T(8,128)(2,1)S(1)}, bf16[128,16,256]{2,1,0:T(8,128)(2,1)S(1)}, u32[]{:S(2)}, u32[]{:S(2)}) collective-permute-start(bf16[128,16,256]{2,1,0:T(8,128)(2,1)S(1)} %edges.1.refs_0_.refs_5_), channel_id=1, source_target_pairs={{0,4},{1,5},{2,6},{3,7},{4,0},{5,1},{6,2},{7,3},{8,12},{9,13},{10,... | collective-permute-start | bytes 3145736 | tf_op jit(solution)/shard_map/ppermute | solution.py:284
  10.6 1.5 %collective-permute-start.4 = (bf16[16,256,128]{2,1,0:T(8,128)(2,1)S(1)}, bf16[16,256,128]{2,1,0:T(8,128)(2,1)S(1)}, u32[]{:S(2)}, u32[]{:S(2)}) collective-permute-start(bf16[16,256,128]{2,1,0:T(8,128)(2,1)S(1)} %copy-done), channel_id=1, source_target_pairs={{0,2},{1,3},{2,0},{3,1},{4,6},{5,7},{6,4},{7,5},{8,10},{9,11},{10,... | collective-permute-start | bytes 3145736 | tf_op jit(solution)/shard_map/ppermute | solution.py:284
  12.5 2.6 %left_edges.6 = (f32[2048,128]{1,0:T(8,128)S(1)}, f32[2048,128]{1,0:T(8,128)S(1)}) custom-call(bf16[128,16,256]{2,1,0:T(8,128)(2,1)S(1)} %edges.1.refs_0_.refs_5_, s32[1]{0:T(128)} %bitcast.refs_0_.refs_1_.me_ref, s32[256]{0:T(256)S(1)} %copy-done.5, s32[1,256]{1,0:T(1,128)S(1)} %bitcast.4, f32[1,128]{1,0:T(1,128)S(1)} %bitcast.10, ...), custom_call_target="tpu_custom_call" | custom-call | flops 1048576 | bytes 1024 | tf_op jit(solution)/shard_map/left_edges/pallas_call | solution.py:218
  15.1 14.5 %collective-permute-done.1.refs_6_.refs_11_ = bf16[8,256,128]{2,1,0:T(8,128)(2,1)S(1)} collective-permute-done((bf16[8,256,128]{2,1,0:T(8,128)(2,1)S(1)}, bf16[8,256,128]{2,1,0:T(8,128)(2,1)S(1)}, u32[]{:S(2)}, u32[]{:S(2)}) %collective-permute-start.1) | collective-permute-done | bytes 524320 | tf_op jit(solution)/shard_map/ppermute | solution.py:284
  29.6 1.5 %left_edges.5 = (f32[1024,128]{1,0:T(8,128)S(1)}, f32[1024,128]{1,0:T(8,128)S(1)}) custom-call(s32[1]{0:T(128)} %bitcast.refs_0_.refs_1_.me_ref, s32[256]{0:T(256)S(1)} %copy-done.5, s32[1,256]{1,0:T(1,128)S(1)} %bitcast.5, f32[1,128]{1,0:T(1,128)S(1)} %bitcast.11, bf16[128,128]{1,0:T(8,128)(2,1)S(1)} %copy-done.1, bf16[128,128]{1,0:T(8,128)(2,1)S(1)} %copy-done.2, ...), custom_call_target="tpu_custom_call" | custom-call | flops 34359738368 | bytes 1024 | tf_op jit(solution)/shard_map/left_edges/pallas_call | solution.py:218
  31.0 1.9 %collective-permute-start.9 = (bf16[8,256,128]{2,1,0:T(8,128)(2,1)S(1)}, bf16[8,256,128]{2,1,0:T(8,128)(2,1)S(1)}, u32[]{:S(2)}, u32[]{:S(2)}) collective-permute-start(bf16[8,256,128]{2,1,0:T(8,128)(2,1)S(1)} %collective-permute-done.1.refs_6_.refs_11_), channel_id=1, source_target_pairs={{0,2},{1,3},{2,0},{3,1},{4,6},{5,7},{6,4},{7,5},{8,10},{9,11},{10,... | collective-permute-start | bytes 1572872 | tf_op jit(solution)/shard_map/ppermute | solution.py:284
  33.0 17.4 %collective-permute-done.5.refs_6_.refs_12_ = bf16[8,256,128]{2,1,0:T(8,128)(2,1)S(1)} collective-permute-done((bf16[8,256,128]{2,1,0:T(8,128)(2,1)S(1)}, bf16[8,256,128]{2,1,0:T(8,128)(2,1)S(1)}, u32[]{:S(2)}, u32[]{:S(2)}) %collective-permute-start.5) | collective-permute-done | bytes 524320 | tf_op jit(solution)/shard_map/ppermute | solution.py:284
  50.4 1.5 %collective-permute-start.10 = (bf16[8,256,128]{2,1,0:T(8,128)(2,1)S(1)}, bf16[8,256,128]{2,1,0:T(8,128)(2,1)S(1)}, u32[]{:S(2)}, u32[]{:S(2)}) collective-permute-start(bf16[8,256,128]{2,1,0:T(8,128)(2,1)S(1)} %collective-permute-done.5.refs_6_.refs_12_), channel_id=1, source_target_pairs={{0,2},{1,3},{2,0},{3,1},{4,6},{5,7},{6,4},{7,5},{8,10},{9,11},{10,... | collective-permute-start | bytes 1572872 | tf_op jit(solution)/shard_map/ppermute | solution.py:284
  51.9 1.5 %left_edges.8 = (f32[1024,128]{1,0:T(8,128)S(1)}, f32[1024,128]{1,0:T(8,128)S(1)}) custom-call(s32[1]{0:T(128)} %bitcast.refs_0_.refs_1_.me_ref, s32[256]{0:T(256)S(1)} %copy-done.5, s32[1,256]{1,0:T(1,128)S(1)} %bitcast.6, f32[1,128]{1,0:T(1,128)S(1)} %bitcast.12, bf16[128,128]{1,0:T(8,128)(2,1)S(1)} %copy-done.1, bf16[128,128]{1,0:T(8,128)(2,1)S(1)} %copy-done.2, ...), custom_call_target="tpu_custom_call" | custom-call | flops 1048576 | bytes 1024 | tf_op jit(solution)/shard_map/left_edges/pallas_call | solution.py:218
  53.4 1.6 %collective-permute-done.refs_0_ = bf16[128,16,256]{2,1,0:T(8,128)(2,1)S(1)} collective-permute-done((bf16[128,16,256]{2,1,0:T(8,128)(2,1)S(1)}, bf16[128,16,256]{2,1,0:T(8,128)(2,1)S(1)}, u32[]{:S(2)}, u32[]{:S(2)}) %collective-permute-start) | collective-permute-done | bytes 1048608 | tf_op jit(solution)/shard_map/ppermute | solution.py:284
  55.0 2.6 %left_edges.7 = (f32[2048,128]{1,0:T(8,128)S(1)}, f32[2048,128]{1,0:T(8,128)S(1)}) custom-call(s32[1]{0:T(128)} %bitcast.refs_0_.refs_1_.me_ref, s32[256]{0:T(256)S(1)} %copy-done.5, s32[1,256]{1,0:T(1,128)S(1)} %bitcast.7, f32[1,128]{1,0:T(1,128)S(1)} %bitcast.13, bf16[128,128]{1,0:T(8,128)(2,1)S(1)} %copy-done.1, bf16[128,128]{1,0:T(8,128)(2,1)S(1)} %copy-done.2, ...), custom_call_target="tpu_custom_call" | custom-call | flops 34359738368 | bytes 1024 | tf_op jit(solution)/shard_map/left_edges/pallas_call | solution.py:218
  58.3 8.1 %triangle.2 = (bf16[48,16,128]{2,1,0:T(8,128)(2,1)S(1)}, bf16[48,16,128]{2,1,0:T(8,128)(2,1)S(1)}, bf16[48,16,128]{2,1,0:T(8,128)(2,1)S(1)}, bf16[48,16,128]{2,1,0:T(8,128)(2,1)S(1)}) custom-call(s32[1]{0:T(128)} %bitcast.refs_0_.refs_1_.me_ref, f32[128]{0:T(128)S(1)} %copy-done.9, f32[1,128]{1,0:T(1,128)S(1)} %bitcast.14, bf16[128,128]{1,0:T(8,128)(2,1)S(1)} %copy-done.3, ...), custom_call_target="tpu_custom_call" | custom-call | flops 1048576 | bytes 1024 | tf_op jit(solution)/shard_map/triangle/pallas_call | solution.py:237
  66.4 0.9 %collective-permute-start.6 = (bf16[48,16,128]{2,1,0:T(8,128)(2,1)S(1)}, bf16[48,16,128]{2,1,0:T(8,128)(2,1)S(1)}, u32[]{:S(2)}, u32[]{:S(2)}) collective-permute-start(bf16[48,16,128]{2,1,0:T(8,128)(2,1)S(1)} %get-tuple-element.32), channel_id=1, source_target_pairs={{0,4},{1,5},{2,6},{3,7},{4,0},{5,1},{6,2},{7,3},{8,12},{9,13},{10,... | collective-permute-start | bytes 589832 | tf_op jit(solution)/shard_map/ppermute | solution.py:284
  67.6 1.1 %collective-permute-start.8 = (bf16[48,16,128]{2,1,0:T(8,128)(2,1)S(1)}, bf16[48,16,128]{2,1,0:T(8,128)(2,1)S(1)}, u32[]{:S(2)}, u32[]{:S(2)}) collective-permute-start(bf16[48,16,128]{2,1,0:T(8,128)(2,1)S(1)} %get-tuple-element.34), channel_id=1, source_target_pairs={{0,5},{1,4},{2,7},{3,6},{4,1},{5,0},{6,3},{7,2},{8,13},{9,12},{10,... | collective-permute-start | bytes 589832 | tf_op jit(solution)/shard_map/ppermute | solution.py:284
  68.6 2.6 %left_edges.9 = (f32[2048,128]{1,0:T(8,128)S(1)}, f32[2048,128]{1,0:T(8,128)S(1)}) custom-call(bf16[48,16,128]{2,1,0:T(8,128)(2,1)S(1)} %get-tuple-element.31.refs_0_.rest_0_, s32[1]{0:T(128)} %bitcast.refs_0_.refs_1_.me_ref, s32[256]{0:T(256)S(1)} %copy-done.5, s32[1,256]{1,0:T(1,128)S(1)} %bitcast.8, f32[1,128]{1,0:T(1,128)S(1)} %bitcast.15, ...), custom_call_target="tpu_custom_call" | custom-call | flops 1048576 | bytes 1024 | tf_op jit(solution)/shard_map/left_edges/pallas_call | solution.py:218
  71.2 4.5 %triangle.3 = (bf16[16,16,128]{2,1,0:T(8,128)(2,1)S(1)}, bf16[16,16,128]{2,1,0:T(8,128)(2,1)S(1)}, bf16[16,16,128]{2,1,0:T(8,128)(2,1)S(1)}, bf16[16,16,128]{2,1,0:T(8,128)(2,1)S(1)}) custom-call(s32[1]{0:T(128)} %bitcast.refs_0_.refs_1_.me_ref, f32[128]{0:T(128)S(1)} %copy-done.9, f32[1,128]{1,0:T(1,128)S(1)} %bitcast.16, bf16[128,128]{1,0:T(8,128)(2,1)S(1)} %copy-done.3, ...), custom_call_target="tpu_custom_call" | custom-call | flops 1048576 | bytes 1024 | tf_op jit(solution)/shard_map/triangle/pallas_call | solution.py:237
  75.7 1.0 %collective-permute-start.11 = (bf16[16,16,128]{2,1,0:T(8,128)(2,1)S(1)}, bf16[16,16,128]{2,1,0:T(8,128)(2,1)S(1)}, u32[]{:S(2)}, u32[]{:S(2)}) collective-permute-start(bf16[16,16,128]{2,1,0:T(8,128)(2,1)S(1)} %get-tuple-element.38), channel_id=1, source_target_pairs={{0,4},{1,5},{2,6},{3,7},{4,0},{5,1},{6,2},{7,3},{8,12},{9,13},{10,... | collective-permute-start | bytes 196616 | tf_op jit(solution)/shard_map/ppermute | solution.py:284
  76.7 3.4 %collective-permute-done.11.rest_5_ = bf16[16,16,128]{2,1,0:T(8,128)(2,1)S(1)} collective-permute-done((bf16[16,16,128]{2,1,0:T(8,128)(2,1)S(1)}, bf16[16,16,128]{2,1,0:T(8,128)(2,1)S(1)}, u32[]{:S(2)}, u32[]{:S(2)}) %collective-permute-start.11) | collective-permute-done | bytes 65568 | tf_op jit(solution)/shard_map/ppermute | solution.py:284
  80.0 3.8 %collective-permute-done.13.rest_7_ = bf16[16,16,128]{2,1,0:T(8,128)(2,1)S(1)} collective-permute-done((bf16[16,16,128]{2,1,0:T(8,128)(2,1)S(1)}, bf16[16,16,128]{2,1,0:T(8,128)(2,1)S(1)}, u32[]{:S(2)}, u32[]{:S(2)}) %collective-permute-start.13) | collective-permute-done | bytes 65568 | tf_op jit(solution)/shard_map/ppermute | solution.py:284
  83.9 1.2 %place.1 = bf16[256,16,128]{2,1,0:T(8,128)(2,1)} custom-call(s32[1]{0:T(128)} %bitcast.refs_0_.refs_1_.me_ref, bf16[48,16,128]{2,1,0:T(8,128)(2,1)S(1)} %get-tuple-element.31.refs_0_.rest_0_, bf16[48,16,128]{2,1,0:T(8,128)(2,1)S(1)} %collective-permute-done.6.rest_1_, bf16[48,16,128]{2,1,0:T(8,128)(2,1)S(1)} %collective-permute-done.7.rest_2_, ...), custom_call_target="tpu_custom_call" | custom-call | tf_op jit(solution)/shard_map/place/pallas_call | solution.py:250
  (35 shorter events, 1.2 us)
Async XLA Ops:
  0.0 5.5 %copy-start = (bf16[16,256,128]{2,1,0:T(8,128)(2,1)S(1)}, bf16[16,256,128]{2,1,0:T(8,128)(2,1)}, u32[]{:S(2)}) copy-start(bf16[16,256,128]{2,1,0:T(8,128)(2,1)} %refs_9_.1) | copy-start | bytes 3145732
  0.0 5.5 %copy-start.6 = (bf16[128,128]{1,0:T(8,128)(2,1)S(1)}, bf16[128,128]{1,0:T(8,128)(2,1)}, u32[]{:S(2)}) copy-start(bf16[128,128]{1,0:T(8,128)(2,1)} %refs_5_.6) | copy-start | bytes 98308
  0.0 5.5 %copy-start.7 = (bf16[128,128]{1,0:T(8,128)(2,1)S(1)}, bf16[128,128]{1,0:T(8,128)(2,1)}, u32[]{:S(2)}) copy-start(bf16[128,128]{1,0:T(8,128)(2,1)} %refs_6_.3) | copy-start | bytes 98308
  1.4 28.2 %collective-permute-start.1 = (bf16[8,256,128]{2,1,0:T(8,128)(2,1)S(1)}, bf16[8,256,128]{2,1,0:T(8,128)(2,1)S(1)}, u32[]{:S(2)}, u32[]{:S(2)}) collective-permute-start(bf16[8,256,128]{2,1,0:T(8,128)(2,1)S(1)} %get-tuple-element.42), channel_id=1, source_target_pairs={{0,8},{1,9},{2,10},{3,11},{4,12},{5,13},{6,14},{7,15},{8,0},{9,1},... | collective-permute-start | bytes 1572872 | tf_op jit(solution)/shard_map/ppermute | solution.py:284
  5.5 0.7 copy-start.5
  5.5 0.7 copy-start.8
  6.2 6.3 %copy-start.1 = (bf16[128,128]{1,0:T(8,128)(2,1)S(1)}, bf16[128,128]{1,0:T(8,128)(2,1)}, u32[]{:S(2)}) copy-start(bf16[128,128]{1,0:T(8,128)(2,1)} %refs_5_.11) | copy-start | bytes 98308
  6.2 6.3 %copy-start.2 = (bf16[128,128]{1,0:T(8,128)(2,1)S(1)}, bf16[128,128]{1,0:T(8,128)(2,1)}, u32[]{:S(2)}) copy-start(bf16[128,128]{1,0:T(8,128)(2,1)} %refs_6_.5) | copy-start | bytes 98308
  9.0 46.0 %collective-permute-start = (bf16[128,16,256]{2,1,0:T(8,128)(2,1)S(1)}, bf16[128,16,256]{2,1,0:T(8,128)(2,1)S(1)}, u32[]{:S(2)}, u32[]{:S(2)}) collective-permute-start(bf16[128,16,256]{2,1,0:T(8,128)(2,1)S(1)} %edges.1.refs_0_.refs_5_), channel_id=1, source_target_pairs={{0,4},{1,5},{2,6},{3,7},{4,0},{5,1},{6,2},{7,3},{8,12},{9,13},{10,... | collective-permute-start | bytes 3145736 | tf_op jit(solution)/shard_map/ppermute | solution.py:284
  10.6 47.0 %collective-permute-start.2 = (bf16[128,16,256]{2,1,0:T(8,128)(2,1)S(1)}, bf16[128,16,256]{2,1,0:T(8,128)(2,1)S(1)}, u32[]{:S(2)}, u32[]{:S(2)}) collective-permute-start(bf16[128,16,256]{2,1,0:T(8,128)(2,1)S(1)} %edges.1.refs_0_.refs_5_), channel_id=1, source_target_pairs={{0,1},{1,0},{2,3},{3,2},{4,5},{5,4},{6,7},{7,6},{8,9},{9,8},{10,11... | collective-permute-start | bytes 3145736 | tf_op jit(solution)/shard_map/ppermute | solution.py:284
  10.6 44.3 %collective-permute-start.4 = (bf16[16,256,128]{2,1,0:T(8,128)(2,1)S(1)}, bf16[16,256,128]{2,1,0:T(8,128)(2,1)S(1)}, u32[]{:S(2)}, u32[]{:S(2)}) collective-permute-start(bf16[16,256,128]{2,1,0:T(8,128)(2,1)S(1)} %copy-done), channel_id=1, source_target_pairs={{0,2},{1,3},{2,0},{3,1},{4,6},{5,7},{6,4},{7,5},{8,10},{9,11},{10,... | collective-permute-start | bytes 3145736 | tf_op jit(solution)/shard_map/ppermute | solution.py:284
  12.2 38.2 %collective-permute-start.5 = (bf16[8,256,128]{2,1,0:T(8,128)(2,1)S(1)}, bf16[8,256,128]{2,1,0:T(8,128)(2,1)S(1)}, u32[]{:S(2)}, u32[]{:S(2)}) collective-permute-start(bf16[8,256,128]{2,1,0:T(8,128)(2,1)S(1)} %get-tuple-element.41), channel_id=1, source_target_pairs={{0,8},{1,9},{2,10},{3,11},{4,12},{5,13},{6,14},{7,15},{8,0},{9,1},... | collective-permute-start | bytes 1572872 | tf_op jit(solution)/shard_map/ppermute | solution.py:284
  31.0 37.6 %collective-permute-start.9 = (bf16[8,256,128]{2,1,0:T(8,128)(2,1)S(1)}, bf16[8,256,128]{2,1,0:T(8,128)(2,1)S(1)}, u32[]{:S(2)}, u32[]{:S(2)}) collective-permute-start(bf16[8,256,128]{2,1,0:T(8,128)(2,1)S(1)} %collective-permute-done.1.refs_6_.refs_11_), channel_id=1, source_target_pairs={{0,2},{1,3},{2,0},{3,1},{4,6},{5,7},{6,4},{7,5},{8,10},{9,11},{10,... | collective-permute-start | bytes 1572872 | tf_op jit(solution)/shard_map/ppermute | solution.py:284
  50.4 18.2 %collective-permute-start.10 = (bf16[8,256,128]{2,1,0:T(8,128)(2,1)S(1)}, bf16[8,256,128]{2,1,0:T(8,128)(2,1)S(1)}, u32[]{:S(2)}, u32[]{:S(2)}) collective-permute-start(bf16[8,256,128]{2,1,0:T(8,128)(2,1)S(1)} %collective-permute-done.5.refs_6_.refs_12_), channel_id=1, source_target_pairs={{0,2},{1,3},{2,0},{3,1},{4,6},{5,7},{6,4},{7,5},{8,10},{9,11},{10,... | collective-permute-start | bytes 1572872 | tf_op jit(solution)/shard_map/ppermute | solution.py:284
  55.0 2.7 %collective-permute-start.3 = (bf16[128,16,256]{2,1,0:T(8,128)(2,1)S(1)}, bf16[128,16,256]{2,1,0:T(8,128)(2,1)S(1)}, u32[]{:S(2)}, u32[]{:S(2)}) collective-permute-start(bf16[128,16,256]{2,1,0:T(8,128)(2,1)S(1)} %hold.1.refs_6_), channel_id=1, source_target_pairs={{0,1},{1,0},{2,3},{3,2},{4,5},{5,4},{6,7},{7,6},{8,9},{9,8},{10,11... | collective-permute-start | bytes 3145736 | tf_op jit(solution)/shard_map/ppermute | solution.py:284
  55.0 2.7 %copy-start.3 = (bf16[128,128]{1,0:T(8,128)(2,1)S(1)}, bf16[128,128]{1,0:T(8,128)(2,1)}, u32[]{:S(2)}) copy-start(bf16[128,128]{1,0:T(8,128)(2,1)} %refs_3_.3) | copy-start | bytes 98308
  55.0 2.7 %copy-start.4 = (bf16[128,128]{1,0:T(8,128)(2,1)S(1)}, bf16[128,128]{1,0:T(8,128)(2,1)}, u32[]{:S(2)}) copy-start(bf16[128,128]{1,0:T(8,128)(2,1)} %refs_4_.9) | copy-start | bytes 98308
  57.7 0.7 copy-start.9
  66.4 17.4 %collective-permute-start.6 = (bf16[48,16,128]{2,1,0:T(8,128)(2,1)S(1)}, bf16[48,16,128]{2,1,0:T(8,128)(2,1)S(1)}, u32[]{:S(2)}, u32[]{:S(2)}) collective-permute-start(bf16[48,16,128]{2,1,0:T(8,128)(2,1)S(1)} %get-tuple-element.32), channel_id=1, source_target_pairs={{0,4},{1,5},{2,6},{3,7},{4,0},{5,1},{6,2},{7,3},{8,12},{9,13},{10,... | collective-permute-start | bytes 589832 | tf_op jit(solution)/shard_map/ppermute | solution.py:284
  67.4 16.5 %collective-permute-start.7 = (bf16[48,16,128]{2,1,0:T(8,128)(2,1)S(1)}, bf16[48,16,128]{2,1,0:T(8,128)(2,1)S(1)}, u32[]{:S(2)}, u32[]{:S(2)}) collective-permute-start(bf16[48,16,128]{2,1,0:T(8,128)(2,1)S(1)} %get-tuple-element.33), channel_id=1, source_target_pairs={{0,1},{1,0},{2,3},{3,2},{4,5},{5,4},{6,7},{7,6},{8,9},{9,8},{10,11... | collective-permute-start | bytes 589832 | tf_op jit(solution)/shard_map/ppermute | solution.py:284
  67.6 16.3 %collective-permute-start.8 = (bf16[48,16,128]{2,1,0:T(8,128)(2,1)S(1)}, bf16[48,16,128]{2,1,0:T(8,128)(2,1)S(1)}, u32[]{:S(2)}, u32[]{:S(2)}) collective-permute-start(bf16[48,16,128]{2,1,0:T(8,128)(2,1)S(1)} %get-tuple-element.34), channel_id=1, source_target_pairs={{0,5},{1,4},{2,7},{3,6},{4,1},{5,0},{6,3},{7,2},{8,13},{9,12},{10,... | collective-permute-start | bytes 589832 | tf_op jit(solution)/shard_map/ppermute | solution.py:284
  75.7 4.3 %collective-permute-start.11 = (bf16[16,16,128]{2,1,0:T(8,128)(2,1)S(1)}, bf16[16,16,128]{2,1,0:T(8,128)(2,1)S(1)}, u32[]{:S(2)}, u32[]{:S(2)}) collective-permute-start(bf16[16,16,128]{2,1,0:T(8,128)(2,1)S(1)} %get-tuple-element.38), channel_id=1, source_target_pairs={{0,4},{1,5},{2,6},{3,7},{4,0},{5,1},{6,2},{7,3},{8,12},{9,13},{10,... | collective-permute-start | bytes 196616 | tf_op jit(solution)/shard_map/ppermute | solution.py:284
  76.7 3.4 %collective-permute-start.12 = (bf16[16,16,128]{2,1,0:T(8,128)(2,1)S(1)}, bf16[16,16,128]{2,1,0:T(8,128)(2,1)S(1)}, u32[]{:S(2)}, u32[]{:S(2)}) collective-permute-start(bf16[16,16,128]{2,1,0:T(8,128)(2,1)S(1)} %get-tuple-element.39), channel_id=1, source_target_pairs={{0,1},{1,0},{2,3},{3,2},{4,5},{5,4},{6,7},{7,6},{8,9},{9,8},{10,11... | collective-permute-start | bytes 196616 | tf_op jit(solution)/shard_map/ppermute | solution.py:284
  80.0 3.8 %collective-permute-start.13 = (bf16[16,16,128]{2,1,0:T(8,128)(2,1)S(1)}, bf16[16,16,128]{2,1,0:T(8,128)(2,1)S(1)}, u32[]{:S(2)}, u32[]{:S(2)}) collective-permute-start(bf16[16,16,128]{2,1,0:T(8,128)(2,1)S(1)} %get-tuple-element.40), channel_id=1, source_target_pairs={{0,5},{1,4},{2,7},{3,6},{4,1},{5,0},{6,3},{7,2},{8,13},{9,12},{10,... | collective-permute-start | bytes 196616 | tf_op jit(solution)/shard_map/ppermute | solution.py:284

commit v4 on v3

v4 whole, which is shorter than its diff:
```python
import functools

import jax
import jax.numpy as jnp
from jax import lax
from jax.experimental import pallas as pl
from jax.experimental.pallas import tpu as pltpu
from jax.sharding import PartitionSpec as P

LANES = 128
WIDE_TYPE = jnp.float32
NARROW = jnp.bfloat16
LAST_BY_LAST = (((1,), (1,)), ((), ()))
VMEM = pl.BlockSpec(memory_space=pltpu.VMEM)
SMEM = pl.BlockSpec(memory_space=pltpu.SMEM)
ANY = pl.BlockSpec(memory_space=pl.ANY)


SHORT = pl.CostEstimate(flops=1 << 20, bytes_accessed=1 << 10, transcendentals=0)
LONG = pl.CostEstimate(flops=1 << 35, bytes_accessed=1 << 10, transcendentals=0)


def sigmoid(values):
    return 0.5 * jnp.tanh(0.5 * values) + 0.5


def norm_rows(values, gain):
    values = values.astype(WIDE_TYPE)
    mean_value = jnp.mean(values, axis=1, keepdims=True)
    centred = values - mean_value
    variance = jnp.mean(centred * centred, axis=1, keepdims=True)
    return (centred * lax.rsqrt(variance + 1e-05) * gain).astype(NARROW)


def home_of(me, unit, base):
    far_bit, low_bit = base
    inner = jnp.where((me & far_bit) != 0, 1, 0) ^ jnp.where((me & low_bit) != 0, 1, 0)
    return me ^ unit ^ (inner * (far_bit | low_bit))


def fill_edges(first, at, rows, total, load, chain_ref, mask_ref, gain_ref, weight_refs, edges):
    channels, hidden = weight_refs[0].shape
    gain = jnp.broadcast_to(gain_ref[...], (channels, channels)).T[:, :1]
    weights = jnp.concatenate([ref[...].T for ref in weight_refs], axis=0)
    column_mask = mask_ref[...].astype(WIDE_TYPE)

    def one_row(i, carry):
        values = load(i).T
        mean_value = jnp.mean(values, axis=0, keepdims=True)
        centred = values - mean_value
        variance = jnp.mean(centred * centred, axis=0, keepdims=True)
        normed = (centred * lax.rsqrt(variance + 1e-05) * gain).astype(NARROW)
        both = jnp.dot(weights, normed, preferred_element_type=WIDE_TYPE)
        row_mask = chain_ref[first + i].astype(WIDE_TYPE)
        masked = sigmoid(both[:hidden]) * both[hidden:] * (column_mask * row_mask)
        for part in range(len(edges)):
            edges[part][pl.ds(at + i, hidden, stride=total), :] = masked[
                :, part * LANES : (part + 1) * LANES
            ]
        return carry

    lax.fori_loop(0, rows, one_row, 0, unroll=min(rows, 8))


def read_edges(edges, start, size):
    return jnp.concatenate([part[pl.ds(start, size), :] for part in edges], axis=1).astype(NARROW)


def edge_kernel(unit, count, me_ref, chain_ref, mask_ref, gain_ref, gate_ref, value_ref, *rest):
    pair_refs, out_ref, edges = rest[:count], rest[count], rest[count + 1 :]
    rows = out_ref.shape[1]
    at = 0
    for pair_ref in pair_refs:
        size = pair_ref.shape[0]
        first = (me_ref[0] ^ unit) * rows + at
        load = lambda i: pair_ref[i].astype(WIDE_TYPE)
        fill_edges(first, at, size, rows, load, chain_ref, mask_ref, gain_ref, (gate_ref, value_ref), edges)
        at += size

    def one_channel(h, carry):
        out_ref[h] = read_edges(edges, pl.multiple_of(h * rows, rows), rows)
        return carry

    lax.fori_loop(0, out_ref.shape[0], one_channel, 0, unroll=16)


def left_kernel(unit, base, span, offsets, me_ref, chain_ref, mask_ref, gain_ref, gate_ref, value_ref, *rest):
    count = len(offsets)
    pair_refs, edges = rest[:count], rest[count:]
    total = sum(ref.shape[0] for ref in pair_refs)
    at = 0
    for offset, pair_ref in zip(offsets, pair_refs):
        size = pair_ref.shape[0]
        first = home_of(me_ref[0], unit, base) * span + offset
        load = lambda i: pair_ref[i].astype(WIDE_TYPE)
        fill_edges(first, at, size, total, load, chain_ref, mask_ref, gain_ref, (gate_ref, value_ref), edges)
        at += size


def triangle_kernel(
    count, order, me_ref, middle_gain_ref, gain_ref, output_gate_ref, output_value_ref, *rest
):
    units = len(order)
    right_refs, rest = rest[:units], rest[units:]
    pair_refs, rest = rest[:count], rest[count:]
    out_refs, triangle = rest[-1 - units : -1], rest[-1]
    parts = pair_refs[0].shape[1] // LANES
    left_refs = [rest[n * parts : (n + 1) * parts] for n in range((len(rest) - 1 - units) // parts)]
    left_sizes = [refs[0].shape[0] // output_value_ref.shape[0] for refs in left_refs]
    me = me_ref[0]
    sizes = [ref.shape[0] for ref in pair_refs]
    rows = sum(sizes)
    hidden = output_value_ref.shape[0]
    width = right_refs[0].shape[1]
    span = units * width

    def read_left(h):
        whole = [
            jnp.concatenate([ref[pl.ds(pl.multiple_of(h * size, size), size), :] for ref in refs], axis=1)
            for refs, size in zip(left_refs, left_sizes)
        ]
        return jnp.concatenate(whole, axis=0).astype(NARROW)

    fold = 2 if rows >= 32 and rows % 16 == 0 and 2 * span <= LANES else 1
    deep = rows // fold
    lower = lax.broadcasted_iota(jnp.int32, (deep, fold * span), 1) < span

    def multiply(h, total):
        right = jnp.concatenate([ref[h] for ref in right_refs] * fold, axis=0)
        product = lax.dot_general(read_left(h), right, LAST_BY_LAST, preferred_element_type=WIDE_TYPE)
        if fold == 2:
            product = jnp.where(lower, product[:deep], product[deep:])
        product = product.astype(NARROW).astype(WIDE_TYPE)
        triangle[pl.ds(pl.multiple_of(h * deep, deep), deep), : fold * span] = product
        return total + product

    zeros = jnp.zeros((deep, fold * span), WIDE_TYPE)
    mean_value = lax.fori_loop(0, hidden, multiply, zeros, unroll=16) * (1.0 / hidden)

    def spread(h, total):
        at = pl.multiple_of(h * deep, deep)
        centred = triangle[pl.ds(at, deep), : fold * span] - mean_value
        return total + centred * centred

    variance = lax.fori_loop(0, hidden, spread, zeros, unroll=16) * (1.0 / hidden)
    scale = lax.rsqrt(variance + 1e-05)

    def normalise(h, carry):
        at = pl.multiple_of(h * deep, deep)
        triangle[pl.ds(at, deep), : fold * span] = (
            (triangle[pl.ds(at, deep), : fold * span] - mean_value) * scale * middle_gain_ref[h]
        )
        return carry

    lax.fori_loop(0, hidden, normalise, 0, unroll=16)
    homes = [(ref, i) for ref in pair_refs for i in range(ref.shape[0])]
    columns = [pl.multiple_of((me ^ unit) * width, width) for unit in order]
    for row in range(deep):
        middle = triangle[pl.ds(row, hidden, stride=deep), :].T[: fold * span].astype(NARROW)
        projected = jnp.dot(middle, output_value_ref[...], preferred_element_type=WIDE_TYPE)
        base = jnp.concatenate(
            [
                homes[row + f * deep][0][homes[row + f * deep][1], pl.ds(column, width), :]
                for f in range(fold)
                for column in columns
            ],
            axis=0,
        )
        normed = norm_rows(base, gain_ref[...])
        gating = sigmoid(jnp.dot(normed, output_gate_ref[...], preferred_element_type=WIDE_TYPE))
        updated = (base.astype(WIDE_TYPE) + gating * projected).astype(NARROW)
        for f in range(fold):
            for u in range(units):
                at = (f * units + u) * width
                out_refs[u][row + f * deep] = updated[at : at + width]


def place_kernel(places, base, rows, me_ref, *rest):
    count = len(places)
    in_refs, out_ref, sem = rest[:count], rest[count], rest[count + 1]
    me = me_ref[0]
    copies = []
    for n, (right_unit, parts) in enumerate(places):
        start = 0
        for unit, offset, size in parts:
            at = home_of(me ^ right_unit, unit, base) * rows + offset
            copies.append(
                pltpu.make_async_copy(
                    in_refs[n].at[pl.ds(start, size)], out_ref.at[pl.ds(at, size)], sem.at[len(copies)]
                )
            )
            start += size
    for copy in copies:
        copy.start()
    for copy in copies:
        copy.wait()


def behind(kernel, count):
    def body(*refs):
        kernel(*refs[count:])

    return body


def edge_scratch(rows, hidden, residues):
    return [pltpu.VMEM((hidden * rows, LANES), WIDE_TYPE)] * (residues // LANES)


def edge_call(deps, unit, me, chain, mask, gain, gate, value, pairs):
    rows = sum(p.shape[0] for p in pairs)
    residues = pairs[0].shape[1]
    hidden = gate.shape[1]
    return pl.pallas_call(
        behind(functools.partial(edge_kernel, unit, len(pairs)), len(deps)),
        out_shape=jax.ShapeDtypeStruct((hidden, rows, residues), NARROW),
        in_specs=[ANY] * len(deps) + [SMEM] * 2 + [VMEM] * (4 + len(pairs)),
        out_specs=VMEM,
        scratch_shapes=edge_scratch(rows, hidden, residues),
        compiler_params=pltpu.CompilerParams(vmem_limit_bytes=16 << 20),
        cost_estimate=SHORT,
        name="edges",
    )(*deps, me, chain, mask, gain, gate, value, *pairs)


def left_call(deps, unit, base, span, offsets, cost, me, chain, mask, gain, gate, value, pairs):
    rows = sum(p.shape[0] for p in pairs)
    residues = pairs[0].shape[1]
    hidden = gate.shape[1]
    shapes = [jax.ShapeDtypeStruct((hidden * rows, LANES), WIDE_TYPE)] * (residues // LANES)
    return pl.pallas_call(
        behind(functools.partial(left_kernel, unit, base, span, offsets), len(deps)),
        out_shape=shapes,
        in_specs=[ANY] * len(deps) + [SMEM] * 2 + [VMEM] * (4 + len(pairs)),
        out_specs=[VMEM] * len(shapes),
        compiler_params=pltpu.CompilerParams(vmem_limit_bytes=16 << 20),
        cost_estimate=cost,
        name="left_edges",
    )(*deps, me, chain, mask, gain, gate, value, *pairs)


def triangle_call(deps, order, me, middle_gain, gain, output_gate, output_value, right, pairs, lefts):
    _, _, channels = pairs[0].shape
    rows = sum(p.shape[0] for p in pairs)
    hidden = output_value.shape[0]
    width = right[0].shape[1]
    tensors = [gain, output_gate, output_value, *right, *pairs]
    for left in lefts:
        tensors += left
    return pl.pallas_call(
        behind(functools.partial(triangle_kernel, len(pairs), order), len(deps)),
        out_shape=[jax.ShapeDtypeStruct((rows, width, channels), NARROW)] * len(order),
        in_specs=[ANY] * len(deps) + [SMEM] * 2 + [VMEM] * len(tensors),
        out_specs=[VMEM] * len(order),
        scratch_shapes=[pltpu.VMEM((hidden * rows, LANES), WIDE_TYPE)],
        compiler_params=pltpu.CompilerParams(vmem_limit_bytes=40 << 20),
        cost_estimate=pl.CostEstimate(flops=1 << 20, bytes_accessed=1 << 10, transcendentals=0),
        name="triangle",
    )(*deps, me, middle_gain, *tensors)


def place_call(places, base, rows, me, blocks, shape):
    return pl.pallas_call(
        functools.partial(place_kernel, places, base, rows),
        out_shape=jax.ShapeDtypeStruct(shape, NARROW),
        in_specs=[SMEM] + [ANY] * len(blocks),
        out_specs=ANY,
        scratch_shapes=[pltpu.SemaphoreType.DMA((sum(len(parts) for _, parts in places),))],
        compiler_params=pltpu.CompilerParams(vmem_limit_bytes=8 << 20),
        name="place",
    )(me, *blocks)


def hold_kernel(*refs):
    pass


def hold(value, *deps, cost=SHORT):
    return pl.pallas_call(
        hold_kernel,
        out_shape=jax.ShapeDtypeStruct(value.shape, value.dtype),
        in_specs=[ANY] * (1 + len(deps)),
        out_specs=ANY,
        input_output_aliases={0: 0},
        compiler_params=pltpu.CompilerParams(vmem_limit_bytes=1 << 20),
        cost_estimate=cost,
        name="hold",
    )(value, *deps)


def split_kernel(count, in_ref, *rest):
    out_refs, sem = rest[:count], rest[count]
    size = in_ref.shape[0] // count
    copies = [
        pltpu.make_async_copy(in_ref.at[pl.ds(n * size, size)], out_refs[n], sem.at[n]) for n in range(count)
    ]
    for copy in copies:
        copy.start()
    for copy in copies:
        copy.wait()


def split_call(values, count):
    shape = (values.shape[0] // count, *values.shape[1:])
    return pl.pallas_call(
        functools.partial(split_kernel, count),
        out_shape=[jax.ShapeDtypeStruct(shape, values.dtype)] * count,
        in_specs=[ANY],
        out_specs=[VMEM] * count,
        scratch_shapes=[pltpu.SemaphoreType.DMA((count,))],
        compiler_params=pltpu.CompilerParams(vmem_limit_bytes=8 << 20),
        cost_estimate=SHORT,
        name="split",
    )(values)


def make_shards(count):
    bits = [1 << b for b in range(count.bit_length() - 1)]
    right_bits = bits[0::2][::-1]
    left_bits = bits[1::2][::-1]

    far_bit, near_bits = left_bits[0], left_bits[1:]
    low_bit = right_bits[0]
    base = (far_bit, low_bit)

    def swap(values, mask):
        return lax.ppermute(values, "wide", [(d, d ^ mask) for d in range(count)])

    def cross(values):
        inner = lambda d: bool(d & far_bit) != bool(d & low_bit)
        pairs = [(d, d ^ far_bit ^ low_bit if inner(d) else d) for d in range(count)]
        return lax.ppermute(values, "wide", pairs)

    def gather(own, bits):
        units = {0: own}
        for bit in bits:
            for unit in list(units):
                units[unit ^ bit] = swap(units[unit], bit)
        return units

    def shards(
        pair,
        residue_mask,
        input_gain,
        left_gate,
        left_value,
        right_gate,
        right_value,
        middle_gain,
        output_gate,
        output_value,
    ):
        rows = pair.shape[0]
        me = lax.axis_index("wide").astype(jnp.int32).reshape(1)
        mask = residue_mask.reshape(1, -1)
        gain = input_gain.reshape(1, -1)
        half = rows // 2
        offsets = (0, half)
        own = split_call(pair, 2)

        def right_edges(deps, unit, raws):
            return edge_call(deps, unit, me, residue_mask, mask, gain, right_gate, right_value, raws)

        def left_edges(deps, unit, at, cost, raws):
            return left_call(
                deps, unit, base, rows, at, cost, me, residue_mask, mask, gain, left_gate, left_value, raws
            )

        blocks = []
        places = []

        def finish(deps, sources, lefts):
            pairs = [raw for _, _, raw in sources]
            outs = triangle_call(
                deps, order, me, middle_gain, gain, output_gate, output_value, rights, pairs, lefts
            )
            parts = [(unit, offset, raw.shape[0]) for unit, offset, raw in sources]
            for unit, out in zip(order, outs):
                blocks.append(out if unit == 0 else swap(out, unit))
                places.append((unit, parts))
            return outs[0]

        side = [swap(piece, low_bit) for piece in own]
        first = [cross(piece) for piece in own]
        near_first = [gather(piece, near_bits) for piece in first]
        units = list(near_first[0])[1:]
        right_own = right_edges((), 0, own)
        right_side = right_edges((right_own, *[near_first[0][unit] for unit in units]), low_bit, side)
        right = {}
        for unit, edges in ((0, right_own), (low_bit, right_side)):
            for more, moved in gather(edges, right_bits[1:]).items():
                right[unit ^ more] = moved
        order = list(right)
        rights = [right[unit] for unit in order]
        second = [cross(piece) for piece in side]

        left_first = left_edges((right_side,), 0, offsets, SHORT, first)
        start = [(0, at, raw) for at, raw in zip(offsets, first)]
        early = [(unit, 0, near_first[0][unit]) for unit in units]
        lefts = [left_edges((left_first[0],), unit, (at,), SHORT, [raw]) for unit, at, raw in early]
        second[0] = hold(second[0], *[left[0] for left in lefts])
        late = [(low_bit, 0, second[0])] + [(unit, half, near_first[1][unit]) for unit in units]
        for unit, at, raw in late:
            lefts.append(left_edges((), unit, (at,), SHORT, [raw]))
        early[0] = (*early[0][:2], hold(early[0][2], lefts[len(early)][0], cost=LONG))
        done = finish((), start + early + late, [left_first] + lefts)
        sent = len(blocks)

        second[1] = hold(second[1], done)
        near_second = [gather(piece, near_bits) for piece in second]
        batch = [(low_bit, half, second[1])]
        batch += [(low_bit ^ unit, 0, near_second[0][unit]) for unit in units]
        lefts = [left_edges((done,), unit, (at,), SHORT, [raw]) for unit, at, raw in batch]
        done = finish((), batch, lefts)

        batch = [(low_bit ^ unit, half, near_second[1][unit]) for unit in units]
        deps = (done, *blocks[1:sent])
        lefts = [left_edges(deps, unit, (at,), SHORT, [raw]) for unit, at, raw in batch]
        finish((), batch, lefts)
        return place_call(places, base, rows, me, blocks, (count * rows, rows, pair.shape[2]))

    return shards


def solution(mesh):
    in_specs = (P(("groups", "wide"), None, None), P("groups")) + (P(),) * 8
    out_specs = P("groups", "wide", None)
    return jax.shard_map(
        make_shards(mesh.shape["wide"]), mesh=mesh, in_specs=in_specs, out_specs=out_specs, check_vma=False
    )
```

time: 85.2 us -> 82.4 us (0.967)
  waiting for transfers between devices: 40.7 us -> 15.8 us
  starting transfers between devices: 14.2 us -> 30.7 us
  Pallas kernels: 27.3 us -> 32.5 us
    ppermute x14 -> x17, waiting for transfers between devices: 40.7 us -> 15.8 us  [swap(): return lax.ppermute(values, 'wide', [(d, d ^ mask) for d in range(count)])]
    ppermute x14 -> x17, starting transfers between devices: 14.2 us -> 26 us  [swap(): return lax.ppermute(values, 'wide', [(d, d ^ mask) for d in range(count)])]
    ppermute x0 -> x4, starting transfers between devices: none -> 4.75 us  [cross(): return lax.ppermute(values, 'wide', pairs)]
    pallas_call x7 -> x11, Pallas kernels: 14.7 us -> 18.9 us  [the longest x7 11.3 us: left_call(): pl.pallas_call(behind(functools.partial(left_kernel, unit, base, span, of...]
    slice x1 -> x0, local copies, waits for them, and re-layouts: 1.36 us -> none  [shards(): far = [swap(pair[start:start + size], far_bit) for start, size in cuts]]
    unnamed x20, local copies, waits for them, and re-layouts: 1.32 us -> 2.55 us
    pallas_call x2 -> x3, Pallas kernels: 12.6 us -> 13.5 us  [triangle_call(): pl.pallas_call(behind(functools.partial(triangle_kernel, len(pairs), orde...]
  transfers between devices with their start and end apart: 14 -> 21, of which waited for: 5 -> 5; matrix products, arithmetic and copies ran while one was open for 0% -> 0% of each run, Pallas kernels for 31% -> 38%
where the time goes in v4:
time: 82.4 us; the launch traced here: 82 us
  Pallas kernels  32.5 us (39%)
  starting transfers between devices  30.7 us (37%)
  waiting for transfers between devices  15.8 us (19%)
  local copies, waits for them, and re-layouts  2.55 us (3%)
    ppermute x17, starting transfers between devices, swap(): return lax.ppermute(values, 'wide', [(d, d ^ mask) for d in range(count)])  26 us
    ppermute x17, waiting for transfers between devices, swap(): return lax.ppermute(values, 'wide', [(d, d ^ mask) for d in range(count)])  15.8 us
    pallas_call x3, Pallas kernels, triangle_call(): pl.pallas_call(behind(functools.partial(triangle_kernel, len(pairs), orde...  13.5 us
    pallas_call x7, Pallas kernels, left_call(): pl.pallas_call(behind(functools.partial(left_kernel, unit, base, span, of...  11.3 us
    pallas_call x2, Pallas kernels, edge_call(): pl.pallas_call(behind(functools.partial(edge_kernel, unit, len(pairs)), l...  6.25 us
    ppermute x4, starting transfers between devices, cross(): return lax.ppermute(values, 'wide', pairs)  4.75 us
    unnamed x20, local copies, waits for them, and re-layouts  2.55 us
  transfers between devices with their start and end apart: 21, of which 5 were waited for; matrix products, arithmetic and copies ran while one was open for 0% of the time, Pallas kernels for 38%

profile of v4, /device:TPU:0, one launch (start us, length us, event | category | flops | bytes accessed | tf_op | source)
XLA Modules:
  0.0 82.0 jit_solution(6319435707062277262)
XLA Ops:
  2.0 5.9 %collective-permute-start.3 = (bf16[8,256,128]{2,1,0:T(8,128)(2,1)S(1)}, bf16[8,256,128]{2,1,0:T(8,128)(2,1)}, u32[]{:S(2)}, u32[]{:S(2)}) collective-permute-start(bf16[8,256,128]{2,1,0:T(8,128)(2,1)S(1)} %get-tuple-element.33.refs_6_), channel_id=1, source_target_pairs={{0,4},{1,5},{2,6},{3,7},{4,0},{5,1},{6,2},{7,3},{8,12},{9,13},{10,... | collective-permute-start | bytes 1572872 | tf_op jit(solution)/shard_map/ppermute | solution.py:327
  8.6 1.8 %collective-permute-start.4 = (bf16[8,256,128]{2,1,0:T(8,128)(2,1)S(1)}, bf16[8,256,128]{2,1,0:T(8,128)(2,1)}, u32[]{:S(2)}, u32[]{:S(2)}) collective-permute-start(bf16[8,256,128]{2,1,0:T(8,128)(2,1)S(1)} %get-tuple-element.34.refs_7_), channel_id=1, source_target_pairs={{0,4},{1,5},{2,6},{3,7},{4,0},{5,1},{6,2},{7,3},{8,12},{9,13},{10,... | collective-permute-start | bytes 1572872 | tf_op jit(solution)/shard_map/ppermute | solution.py:327
  10.4 1.5 %collective-permute-start.2 = (bf16[8,256,128]{2,1,0:T(8,128)(2,1)S(1)}, bf16[8,256,128]{2,1,0:T(8,128)(2,1)S(1)}, u32[]{:S(2)}, u32[]{:S(2)}) collective-permute-start(bf16[8,256,128]{2,1,0:T(8,128)(2,1)S(1)} %collective-permute-done.1.refs_7_.refs_9_), channel_id=1, source_target_pairs={{0,2},{1,3},{2,0},{3,1},{4,6},{5,7},{6,4},{7,5},{8,10},{9,11},{10,... | collective-permute-start | bytes 1572872 | tf_op jit(solution)/shard_map/ppermute | solution.py:327
  11.9 8.9 %collective-permute-done.3.refs_8_ = bf16[8,256,128]{2,1,0:T(8,128)(2,1)} collective-permute-done((bf16[8,256,128]{2,1,0:T(8,128)(2,1)S(1)}, bf16[8,256,128]{2,1,0:T(8,128)(2,1)}, u32[]{:S(2)}, u32[]{:S(2)}) %collective-permute-start.3) | collective-permute-done | bytes 524320 | tf_op jit(solution)/shard_map/ppermute | solution.py:327
  20.8 1.7 %collective-permute-start.7 = (bf16[8,256,128]{2,1,0:T(8,128)(2,1)}, bf16[8,256,128]{2,1,0:T(8,128)(2,1)S(1)}, u32[]{:S(2)}, u32[]{:S(2)}) collective-permute-start(bf16[8,256,128]{2,1,0:T(8,128)(2,1)} %collective-permute-done.3.refs_8_), channel_id=1, source_target_pairs={{0,0},{1,1},{2,2},{3,3},{4,8},{5,9},{6,10},{7,11},{8,4},{9,5},{10,... | collective-permute-start | bytes 1572872 | tf_op jit(solution)/shard_map/ppermute | solution.py:332
  23.2 2.7 %edges.2.refs_0_.refs_5_ = bf16[128,16,256]{2,1,0:T(8,128)(2,1)S(1)} custom-call(s32[1]{0:T(128)} %bitcast.refs_0_.refs_2_.refs_1_.refs_4_.me_ref, s32[256]{0:T(256)S(1)} %copy-done.3, s32[1,256]{1,0:T(1,128)S(1)} %bitcast.3, f32[1,128]{1,0:T(1,128)S(1)} %bitcast.12, bf16[128,128]{1,0:T(8,128)(2,1)S(1)} %copy-done.6, bf16[128,128]{1,0:T(8,128)(2,1)S(1)} %copy-done.7, ...), custom_call_target="tpu_custom_call" | custom-call | flops 1048576 | bytes 1024 | tf_op jit(solution)/shard_map/edges/pallas_call | solution.py:214
  26.0 1.6 %collective-permute-start.8 = (bf16[8,256,128]{2,1,0:T(8,128)(2,1)S(1)}, bf16[8,256,128]{2,1,0:T(8,128)(2,1)S(1)}, u32[]{:S(2)}, u32[]{:S(2)}) collective-permute-start(bf16[8,256,128]{2,1,0:T(8,128)(2,1)S(1)} %collective-permute-done.6.refs_8_.refs_10_), channel_id=1, source_target_pairs={{0,2},{1,3},{2,0},{3,1},{4,6},{5,7},{6,4},{7,5},{8,10},{9,11},{10,... | collective-permute-start | bytes 1572872 | tf_op jit(solution)/shard_map/ppermute | solution.py:327
  27.6 3.3 %collective-permute-done.4.refs_9_ = bf16[8,256,128]{2,1,0:T(8,128)(2,1)} collective-permute-done((bf16[8,256,128]{2,1,0:T(8,128)(2,1)S(1)}, bf16[8,256,128]{2,1,0:T(8,128)(2,1)}, u32[]{:S(2)}, u32[]{:S(2)}) %collective-permute-start.4) | collective-permute-done | bytes 524320 | tf_op jit(solution)/shard_map/ppermute | solution.py:327
  30.9 1.7 %collective-permute-start.12 = (bf16[8,256,128]{2,1,0:T(8,128)(2,1)}, bf16[8,256,128]{2,1,0:T(8,128)(2,1)S(1)}, u32[]{:S(2)}, u32[]{:S(2)}) collective-permute-start(bf16[8,256,128]{2,1,0:T(8,128)(2,1)} %collective-permute-done.4.refs_9_), channel_id=1, source_target_pairs={{0,0},{1,1},{2,2},{3,3},{4,8},{5,9},{6,10},{7,11},{8,4},{9,5},{10,... | collective-permute-start | bytes 1572872 | tf_op jit(solution)/shard_map/ppermute | solution.py:332
  32.6 3.5 %edges.3.refs_0_.refs_7_ = bf16[128,16,256]{2,1,0:T(8,128)(2,1)S(1)} custom-call(bf16[128,16,256]{2,1,0:T(8,128)(2,1)S(1)} %edges.2.refs_0_.refs_5_, bf16[8,256,128]{2,1,0:T(8,128)(2,1)S(1)} %collective-permute-done.2.refs_1_.refs_7_.refs_0_, s32[1]{0:T(128)} %bitcast.refs_0_.refs_2_.refs_1_.refs_4_.me_ref, s32[256]{0:T(256)S(1)} %copy-done.3, ...), custom_call_target="tpu_custom_call" | custom-call | flops 1048576 | bytes 1024 | tf_op jit(solution)/shard_map/edges/pallas_call | solution.py:214
  36.2 2.6 %left_edges.7 = (f32[2048,128]{1,0:T(8,128)S(1)}, f32[2048,128]{1,0:T(8,128)S(1)}) custom-call(bf16[128,16,256]{2,1,0:T(8,128)(2,1)S(1)} %edges.3.refs_0_.refs_7_, s32[1]{0:T(128)} %bitcast.refs_0_.refs_2_.refs_1_.refs_4_.me_ref, s32[256]{0:T(256)S(1)} %copy-done.3, s32[1,256]{1,0:T(1,128)S(1)} %bitcast.5, f32[1,128]{1,0:T(1,128)S(1)} %bitcast.14, ...), custom_call_target="tpu_custom_call" | custom-call | flops 1048576 | bytes 1024 | tf_op jit(solution)/shard_map/left_edges/pallas_call | solution.py:231
  38.8 1.5 %left_edges.8 = (f32[1024,128]{1,0:T(8,128)S(1)}, f32[1024,128]{1,0:T(8,128)S(1)}) custom-call(f32[2048,128]{1,0:T(8,128)S(1)} %get-tuple-element.35.refs_0_.refs_14_, s32[1]{0:T(128)} %bitcast.refs_0_.refs_2_.refs_1_.refs_4_.me_ref, s32[256]{0:T(256)S(1)} %copy-done.3, s32[1,256]{1,0:T(1,128)S(1)} %bitcast.6, f32[1,128]{1,0:T(1,128)S(1)} %bitcast.15, ...), custom_call_target="tpu_custom_call" | custom-call | flops 1048576 | bytes 1024 | tf_op jit(solution)/shard_map/left_edges/pallas_call | solution.py:231
  41.8 1.6 %collective-permute-start.13 = (bf16[8,256,128]{2,1,0:T(8,128)(2,1)S(1)}, bf16[8,256,128]{2,1,0:T(8,128)(2,1)S(1)}, u32[]{:S(2)}, u32[]{:S(2)}) collective-permute-start(bf16[8,256,128]{2,1,0:T(8,128)(2,1)S(1)} %hold.3.refs_6_.refs_12_), channel_id=1, source_target_pairs={{0,2},{1,3},{2,0},{3,1},{4,6},{5,7},{6,4},{7,5},{8,10},{9,11},{10,... | collective-permute-start | bytes 1572872 | tf_op jit(solution)/shard_map/ppermute | solution.py:327
  43.4 1.5 %left_edges.10 = (f32[1024,128]{1,0:T(8,128)S(1)}, f32[1024,128]{1,0:T(8,128)S(1)}) custom-call(s32[1]{0:T(128)} %bitcast.refs_0_.refs_2_.refs_1_.refs_4_.me_ref, s32[256]{0:T(256)S(1)} %copy-done.3, s32[1,256]{1,0:T(1,128)S(1)} %bitcast.8, f32[1,128]{1,0:T(1,128)S(1)} %bitcast.17, bf16[128,128]{1,0:T(8,128)(2,1)S(1)} %copy-done, ...), custom_call_target="tpu_custom_call" | custom-call | flops 1048576 | bytes 1024 | tf_op jit(solution)/shard_map/left_edges/pallas_call | solution.py:231
  45.6 6.0 %triangle.3 = (bf16[40,16,128]{2,1,0:T(8,128)(2,1)S(1)}, bf16[40,16,128]{2,1,0:T(8,128)(2,1)S(1)}, bf16[40,16,128]{2,1,0:T(8,128)(2,1)S(1)}, bf16[40,16,128]{2,1,0:T(8,128)(2,1)S(1)}) custom-call(s32[1]{0:T(128)} %bitcast.refs_0_.refs_2_.refs_1_.refs_4_.me_ref, f32[128]{0:T(128)S(1)} %copy-done.9, f32[1,128]{1,0:T(1,128)S(1)} %bitcast.18, ...), custom_call_target="tpu_custom_call" | custom-call | flops 1048576 | bytes 1024 | tf_op jit(solution)/shard_map/triangle/pallas_call | solution.py:250
  52.1 4.7 %collective-permute-start.10 = (bf16[40,16,128]{2,1,0:T(8,128)(2,1)S(1)}, bf16[40,16,128]{2,1,0:T(8,128)(2,1)S(1)}, u32[]{:S(2)}, u32[]{:S(2)}) collective-permute-start(bf16[40,16,128]{2,1,0:T(8,128)(2,1)S(1)} %get-tuple-element.45), channel_id=1, source_target_pairs={{0,4},{1,5},{2,6},{3,7},{4,0},{5,1},{6,2},{7,3},{8,12},{9,13},{10,... | collective-permute-start | bytes 491528 | tf_op jit(solution)/shard_map/ppermute | solution.py:327
  57.0 1.5 %left_edges.11 = (f32[1024,128]{1,0:T(8,128)S(1)}, f32[1024,128]{1,0:T(8,128)S(1)}) custom-call(bf16[40,16,128]{2,1,0:T(8,128)(2,1)S(1)} %get-tuple-element.43.refs_1_.refs_0_.rest_0_, s32[1]{0:T(128)} %bitcast.refs_0_.refs_2_.refs_1_.refs_4_.me_ref, s32[256]{0:T(256)S(1)} %copy-done.3, s32[1,256]{1,0:T(1,128)S(1)} %bitcast.9, f32[1,128]{1,0:T(1,128)S(1)} %bitcast.19, ...), custom_call_target="tpu_custom_call" | custom-call | flops 1048576 | bytes 1024 | tf_op jit(solution)/shard_map/left_edges/pallas_call | solution.py:231
  58.4 1.5 %left_edges.12 = (f32[1024,128]{1,0:T(8,128)S(1)}, f32[1024,128]{1,0:T(8,128)S(1)}) custom-call(bf16[40,16,128]{2,1,0:T(8,128)(2,1)S(1)} %get-tuple-element.43.refs_1_.refs_0_.rest_0_, s32[1]{0:T(128)} %bitcast.refs_0_.refs_2_.refs_1_.refs_4_.me_ref, s32[256]{0:T(256)S(1)} %copy-done.3, s32[1,256]{1,0:T(1,128)S(1)} %bitcast.10, f32[1,128]{1,0:T(1,128)S(1)} %bitcast.20, ...), custom_call_target="tpu_custom_call" | custom-call | flops 1048576 | bytes 1024 | tf_op jit(solution)/shard_map/left_edges/pallas_call | solution.py:231
  59.9 4.0 %triangle.4 = (bf16[16,16,128]{2,1,0:T(8,128)(2,1)S(1)}, bf16[16,16,128]{2,1,0:T(8,128)(2,1)S(1)}, bf16[16,16,128]{2,1,0:T(8,128)(2,1)S(1)}, bf16[16,16,128]{2,1,0:T(8,128)(2,1)S(1)}) custom-call(s32[1]{0:T(128)} %bitcast.refs_0_.refs_2_.refs_1_.refs_4_.me_ref, f32[128]{0:T(128)S(1)} %copy-done.9, f32[1,128]{1,0:T(1,128)S(1)} %bitcast.21, ...), custom_call_target="tpu_custom_call" | custom-call | flops 1048576 | bytes 1024 | tf_op jit(solution)/shard_map/triangle/pallas_call | solution.py:250
  64.4 2.6 %collective-permute-start.15 = (bf16[16,16,128]{2,1,0:T(8,128)(2,1)S(1)}, bf16[16,16,128]{2,1,0:T(8,128)(2,1)S(1)}, u32[]{:S(2)}, u32[]{:S(2)}) collective-permute-start(bf16[16,16,128]{2,1,0:T(8,128)(2,1)S(1)} %get-tuple-element.53), channel_id=1, source_target_pairs={{0,4},{1,5},{2,6},{3,7},{4,0},{5,1},{6,2},{7,3},{8,12},{9,13},{10,... | collective-permute-start | bytes 196616 | tf_op jit(solution)/shard_map/ppermute | solution.py:327
  67.4 1.5 %left_edges.13 = (f32[1024,128]{1,0:T(8,128)S(1)}, f32[1024,128]{1,0:T(8,128)S(1)}) custom-call(bf16[16,16,128]{2,1,0:T(8,128)(2,1)S(1)} %get-tuple-element.51.refs_0_.rest_4_, bf16[40,16,128]{2,1,0:T(8,128)(2,1)S(1)} %collective-permute-done.9.refs_1_.rest_1_, bf16[40,16,128]{2,1,0:T(8,128)(2,1)S(1)} %collective-permute-done.10.refs_2_.rest_2_, ...), custom_call_target="tpu_custom_call" | custom-call | flops 1048576 | bytes 1024 | tf_op jit(solution)/shard_map/left_edges/pallas_call | solution.py:231
  68.9 3.5 %triangle.5 = (bf16[8,16,128]{2,1,0:T(8,128)(2,1)S(1)}, bf16[8,16,128]{2,1,0:T(8,128)(2,1)S(1)}, bf16[8,16,128]{2,1,0:T(8,128)(2,1)S(1)}, bf16[8,16,128]{2,1,0:T(8,128)(2,1)S(1)}) custom-call(s32[1]{0:T(128)} %bitcast.refs_0_.refs_2_.refs_1_.refs_4_.me_ref, f32[128]{0:T(128)S(1)} %copy-done.9, f32[1,128]{1,0:T(1,128)S(1)} %bitcast.23, ...), custom_call_target="tpu_custom_call" | custom-call | flops 1048576 | bytes 1024 | tf_op jit(solution)/shard_map/triangle/pallas_call | solution.py:250
  72.5 4.8 %collective-permute-start.19 = (bf16[8,16,128]{2,1,0:T(8,128)(2,1)S(1)}, bf16[8,16,128]{2,1,0:T(8,128)(2,1)S(1)}, u32[]{:S(2)}, u32[]{:S(2)}) collective-permute-start(bf16[8,16,128]{2,1,0:T(8,128)(2,1)S(1)} %get-tuple-element.59), channel_id=1, source_target_pairs={{0,4},{1,5},{2,6},{3,7},{4,0},{5,1},{6,2},{7,3},{8,12},{9,13},{10,... | collective-permute-start | bytes 98312 | tf_op jit(solution)/shard_map/ppermute | solution.py:327
  77.4 1.9 %collective-permute-done.19.rest_10_ = bf16[8,16,128]{2,1,0:T(8,128)(2,1)S(1)} collective-permute-done((bf16[8,16,128]{2,1,0:T(8,128)(2,1)S(1)}, bf16[8,16,128]{2,1,0:T(8,128)(2,1)S(1)}, u32[]{:S(2)}, u32[]{:S(2)}) %collective-permute-start.19) | collective-permute-done | bytes 32800 | tf_op jit(solution)/shard_map/ppermute | solution.py:327
  (55 shorter events, 9.9 us)
Async XLA Ops:
  1.2 21.3 %copy-start.6 = (bf16[128,128]{1,0:T(8,128)(2,1)S(1)}, bf16[128,128]{1,0:T(8,128)(2,1)}, u32[]{:S(2)}) copy-start(bf16[128,128]{1,0:T(8,128)(2,1)} %refs_6_.5) | copy-start | bytes 98308
  1.2 21.3 %copy-start.7 = (bf16[128,128]{1,0:T(8,128)(2,1)S(1)}, bf16[128,128]{1,0:T(8,128)(2,1)}, u32[]{:S(2)}) copy-start(bf16[128,128]{1,0:T(8,128)(2,1)} %refs_7_.1) | copy-start | bytes 98308
  1.3 9.0 %collective-permute-start.1 = (bf16[8,256,128]{2,1,0:T(8,128)(2,1)S(1)}, bf16[8,256,128]{2,1,0:T(8,128)(2,1)S(1)}, u32[]{:S(2)}, u32[]{:S(2)}) collective-permute-start(bf16[8,256,128]{2,1,0:T(8,128)(2,1)S(1)} %get-tuple-element.33.refs_6_), channel_id=1, source_target_pairs={{0,0},{1,1},{2,2},{3,3},{4,8},{5,9},{6,10},{7,11},{8,4},{9,5},{10,... | collective-permute-start | bytes 1572872 | tf_op jit(solution)/shard_map/ppermute | solution.py:332
  2.0 18.8 %collective-permute-start.3 = (bf16[8,256,128]{2,1,0:T(8,128)(2,1)S(1)}, bf16[8,256,128]{2,1,0:T(8,128)(2,1)}, u32[]{:S(2)}, u32[]{:S(2)}) collective-permute-start(bf16[8,256,128]{2,1,0:T(8,128)(2,1)S(1)} %get-tuple-element.33.refs_6_), channel_id=1, source_target_pairs={{0,4},{1,5},{2,6},{3,7},{4,0},{5,1},{6,2},{7,3},{8,12},{9,13},{10,... | collective-permute-start | bytes 1572872 | tf_op jit(solution)/shard_map/ppermute | solution.py:327
  7.9 18.1 %collective-permute-start.6 = (bf16[8,256,128]{2,1,0:T(8,128)(2,1)S(1)}, bf16[8,256,128]{2,1,0:T(8,128)(2,1)S(1)}, u32[]{:S(2)}, u32[]{:S(2)}) collective-permute-start(bf16[8,256,128]{2,1,0:T(8,128)(2,1)S(1)} %get-tuple-element.34.refs_7_), channel_id=1, source_target_pairs={{0,0},{1,1},{2,2},{3,3},{4,8},{5,9},{6,10},{7,11},{8,4},{9,5},{10,... | collective-permute-start | bytes 1572872 | tf_op jit(solution)/shard_map/ppermute | solution.py:332
  8.6 22.3 %collective-permute-start.4 = (bf16[8,256,128]{2,1,0:T(8,128)(2,1)S(1)}, bf16[8,256,128]{2,1,0:T(8,128)(2,1)}, u32[]{:S(2)}, u32[]{:S(2)}) collective-permute-start(bf16[8,256,128]{2,1,0:T(8,128)(2,1)S(1)} %get-tuple-element.34.refs_7_), channel_id=1, source_target_pairs={{0,4},{1,5},{2,6},{3,7},{4,0},{5,1},{6,2},{7,3},{8,12},{9,13},{10,... | collective-permute-start | bytes 1572872 | tf_op jit(solution)/shard_map/ppermute | solution.py:327
  10.4 22.2 %collective-permute-start.2 = (bf16[8,256,128]{2,1,0:T(8,128)(2,1)S(1)}, bf16[8,256,128]{2,1,0:T(8,128)(2,1)S(1)}, u32[]{:S(2)}, u32[]{:S(2)}) collective-permute-start(bf16[8,256,128]{2,1,0:T(8,128)(2,1)S(1)} %collective-permute-done.1.refs_7_.refs_9_), channel_id=1, source_target_pairs={{0,2},{1,3},{2,0},{3,1},{4,6},{5,7},{6,4},{7,5},{8,10},{9,11},{10,... | collective-permute-start | bytes 1572872 | tf_op jit(solution)/shard_map/ppermute | solution.py:327
  20.8 19.5 %collective-permute-start.7 = (bf16[8,256,128]{2,1,0:T(8,128)(2,1)}, bf16[8,256,128]{2,1,0:T(8,128)(2,1)S(1)}, u32[]{:S(2)}, u32[]{:S(2)}) collective-permute-start(bf16[8,256,128]{2,1,0:T(8,128)(2,1)} %collective-permute-done.3.refs_8_), channel_id=1, source_target_pairs={{0,0},{1,1},{2,2},{3,3},{4,8},{5,9},{6,10},{7,11},{8,4},{9,5},{10,... | collective-permute-start | bytes 1572872 | tf_op jit(solution)/shard_map/ppermute | solution.py:332
  25.9 10.3 %copy-start = (bf16[128,128]{1,0:T(8,128)(2,1)S(1)}, bf16[128,128]{1,0:T(8,128)(2,1)}, u32[]{:S(2)}) copy-start(bf16[128,128]{1,0:T(8,128)(2,1)} %refs_8_.1) | copy-start | bytes 98308
  25.9 19.0 %collective-permute-start = (bf16[128,16,256]{2,1,0:T(8,128)(2,1)S(1)}, bf16[128,16,256]{2,1,0:T(8,128)(2,1)S(1)}, u32[]{:S(2)}, u32[]{:S(2)}) collective-permute-start(bf16[128,16,256]{2,1,0:T(8,128)(2,1)S(1)} %edges.2.refs_0_.refs_5_), channel_id=1, source_target_pairs={{0,1},{1,0},{2,3},{3,2},{4,5},{5,4},{6,7},{7,6},{8,9},{9,8},{10,11... | collective-permute-start | bytes 3145736 | tf_op jit(solution)/shard_map/ppermute | solution.py:327
  26.0 17.4 %collective-permute-start.8 = (bf16[8,256,128]{2,1,0:T(8,128)(2,1)S(1)}, bf16[8,256,128]{2,1,0:T(8,128)(2,1)S(1)}, u32[]{:S(2)}, u32[]{:S(2)}) collective-permute-start(bf16[8,256,128]{2,1,0:T(8,128)(2,1)S(1)} %collective-permute-done.6.refs_8_.refs_10_), channel_id=1, source_target_pairs={{0,2},{1,3},{2,0},{3,1},{4,6},{5,7},{6,4},{7,5},{8,10},{9,11},{10,... | collective-permute-start | bytes 1572872 | tf_op jit(solution)/shard_map/ppermute | solution.py:327
  30.9 20.6 %collective-permute-start.12 = (bf16[8,256,128]{2,1,0:T(8,128)(2,1)}, bf16[8,256,128]{2,1,0:T(8,128)(2,1)S(1)}, u32[]{:S(2)}, u32[]{:S(2)}) collective-permute-start(bf16[8,256,128]{2,1,0:T(8,128)(2,1)} %collective-permute-done.4.refs_9_), channel_id=1, source_target_pairs={{0,0},{1,1},{2,2},{3,3},{4,8},{5,9},{6,10},{7,11},{8,4},{9,5},{10,... | collective-permute-start | bytes 1572872 | tf_op jit(solution)/shard_map/ppermute | solution.py:332
  36.1 8.7 %collective-permute-start.5 = (bf16[128,16,256]{2,1,0:T(8,128)(2,1)S(1)}, bf16[128,16,256]{2,1,0:T(8,128)(2,1)S(1)}, u32[]{:S(2)}, u32[]{:S(2)}) collective-permute-start(bf16[128,16,256]{2,1,0:T(8,128)(2,1)S(1)} %edges.3.refs_0_.refs_7_), channel_id=1, source_target_pairs={{0,1},{1,0},{2,3},{3,2},{4,5},{5,4},{6,7},{7,6},{8,9},{9,8},{10,11... | collective-permute-start | bytes 3145736 | tf_op jit(solution)/shard_map/ppermute | solution.py:327
  41.8 16.6 %collective-permute-start.13 = (bf16[8,256,128]{2,1,0:T(8,128)(2,1)S(1)}, bf16[8,256,128]{2,1,0:T(8,128)(2,1)S(1)}, u32[]{:S(2)}, u32[]{:S(2)}) collective-permute-start(bf16[8,256,128]{2,1,0:T(8,128)(2,1)S(1)} %hold.3.refs_6_.refs_12_), channel_id=1, source_target_pairs={{0,2},{1,3},{2,0},{3,1},{4,6},{5,7},{6,4},{7,5},{8,10},{9,11},{10,... | collective-permute-start | bytes 1572872 | tf_op jit(solution)/shard_map/ppermute | solution.py:327
  51.5 15.9 %collective-permute-start.17 = (bf16[8,256,128]{2,1,0:T(8,128)(2,1)S(1)}, bf16[8,256,128]{2,1,0:T(8,128)(2,1)S(1)}, u32[]{:S(2)}, u32[]{:S(2)}) collective-permute-start(bf16[8,256,128]{2,1,0:T(8,128)(2,1)S(1)} %hold.5.refs_7_.refs_9_), channel_id=1, source_target_pairs={{0,2},{1,3},{2,0},{3,1},{4,6},{5,7},{6,4},{7,5},{8,10},{9,11},{10,... | collective-permute-start | bytes 1572872 | tf_op jit(solution)/shard_map/ppermute | solution.py:327
  52.1 12.3 %collective-permute-start.10 = (bf16[40,16,128]{2,1,0:T(8,128)(2,1)S(1)}, bf16[40,16,128]{2,1,0:T(8,128)(2,1)S(1)}, u32[]{:S(2)}, u32[]{:S(2)}) collective-permute-start(bf16[40,16,128]{2,1,0:T(8,128)(2,1)S(1)} %get-tuple-element.45), channel_id=1, source_target_pairs={{0,4},{1,5},{2,6},{3,7},{4,0},{5,1},{6,2},{7,3},{8,12},{9,13},{10,... | collective-permute-start | bytes 491528 | tf_op jit(solution)/shard_map/ppermute | solution.py:327
  56.8 10.2 %collective-permute-start.11 = (bf16[40,16,128]{2,1,0:T(8,128)(2,1)S(1)}, bf16[40,16,128]{2,1,0:T(8,128)(2,1)S(1)}, u32[]{:S(2)}, u32[]{:S(2)}) collective-permute-start(bf16[40,16,128]{2,1,0:T(8,128)(2,1)S(1)} %get-tuple-element.46), channel_id=1, source_target_pairs={{0,5},{1,4},{2,7},{3,6},{4,1},{5,0},{6,3},{7,2},{8,13},{9,12},{10,... | collective-permute-start | bytes 491528 | tf_op jit(solution)/shard_map/ppermute | solution.py:327
  56.8 10.3 %collective-permute-start.9 = (bf16[40,16,128]{2,1,0:T(8,128)(2,1)S(1)}, bf16[40,16,128]{2,1,0:T(8,128)(2,1)S(1)}, u32[]{:S(2)}, u32[]{:S(2)}) collective-permute-start(bf16[40,16,128]{2,1,0:T(8,128)(2,1)S(1)} %get-tuple-element.44), channel_id=1, source_target_pairs={{0,1},{1,0},{2,3},{3,2},{4,5},{5,4},{6,7},{7,6},{8,9},{9,8},{10,11... | collective-permute-start | bytes 491528 | tf_op jit(solution)/shard_map/ppermute | solution.py:327
  64.0 13.3 %collective-permute-start.14 = (bf16[16,16,128]{2,1,0:T(8,128)(2,1)S(1)}, bf16[16,16,128]{2,1,0:T(8,128)(2,1)S(1)}, u32[]{:S(2)}, u32[]{:S(2)}) collective-permute-start(bf16[16,16,128]{2,1,0:T(8,128)(2,1)S(1)} %get-tuple-element.52), channel_id=1, source_target_pairs={{0,1},{1,0},{2,3},{3,2},{4,5},{5,4},{6,7},{7,6},{8,9},{9,8},{10,11... | collective-permute-start | bytes 196616 | tf_op jit(solution)/shard_map/ppermute | solution.py:327
  64.4 13.0 %collective-permute-start.15 = (bf16[16,16,128]{2,1,0:T(8,128)(2,1)S(1)}, bf16[16,16,128]{2,1,0:T(8,128)(2,1)S(1)}, u32[]{:S(2)}, u32[]{:S(2)}) collective-permute-start(bf16[16,16,128]{2,1,0:T(8,128)(2,1)S(1)} %get-tuple-element.53), channel_id=1, source_target_pairs={{0,4},{1,5},{2,6},{3,7},{4,0},{5,1},{6,2},{7,3},{8,12},{9,13},{10,... | collective-permute-start | bytes 196616 | tf_op jit(solution)/shard_map/ppermute | solution.py:327
  67.0 10.4 %collective-permute-start.16 = (bf16[16,16,128]{2,1,0:T(8,128)(2,1)S(1)}, bf16[16,16,128]{2,1,0:T(8,128)(2,1)S(1)}, u32[]{:S(2)}, u32[]{:S(2)}) collective-permute-start(bf16[16,16,128]{2,1,0:T(8,128)(2,1)S(1)} %get-tuple-element.54), channel_id=1, source_target_pairs={{0,5},{1,4},{2,7},{3,6},{4,1},{5,0},{6,3},{7,2},{8,13},{9,12},{10,... | collective-permute-start | bytes 196616 | tf_op jit(solution)/shard_map/ppermute | solution.py:327
  72.4 5.0 %collective-permute-start.18 = (bf16[8,16,128]{2,1,0:T(8,128)(2,1)S(1)}, bf16[8,16,128]{2,1,0:T(8,128)(2,1)S(1)}, u32[]{:S(2)}, u32[]{:S(2)}) collective-permute-start(bf16[8,16,128]{2,1,0:T(8,128)(2,1)S(1)} %get-tuple-element.58), channel_id=1, source_target_pairs={{0,1},{1,0},{2,3},{3,2},{4,5},{5,4},{6,7},{7,6},{8,9},{9,8},{10,11... | collective-permute-start | bytes 98312 | tf_op jit(solution)/shard_map/ppermute | solution.py:327
  72.5 6.8 %collective-permute-start.19 = (bf16[8,16,128]{2,1,0:T(8,128)(2,1)S(1)}, bf16[8,16,128]{2,1,0:T(8,128)(2,1)S(1)}, u32[]{:S(2)}, u32[]{:S(2)}) collective-permute-start(bf16[8,16,128]{2,1,0:T(8,128)(2,1)S(1)} %get-tuple-element.59), channel_id=1, source_target_pairs={{0,4},{1,5},{2,6},{3,7},{4,0},{5,1},{6,2},{7,3},{8,12},{9,13},{10,... | collective-permute-start | bytes 98312 | tf_op jit(solution)/shard_map/ppermute | solution.py:327
  77.3 3.3 %collective-permute-start.20 = (bf16[8,16,128]{2,1,0:T(8,128)(2,1)S(1)}, bf16[8,16,128]{2,1,0:T(8,128)(2,1)S(1)}, u32[]{:S(2)}, u32[]{:S(2)}) collective-permute-start(bf16[8,16,128]{2,1,0:T(8,128)(2,1)S(1)} %get-tuple-element.60), channel_id=1, source_target_pairs={{0,5},{1,4},{2,7},{3,6},{4,1},{5,0},{6,3},{7,2},{8,13},{9,12},{10,... | collective-permute-start | bytes 98312 | tf_op jit(solution)/shard_map/ppermute | solution.py:327
  (7 other events, 16.6 us)

commit v5 on v4

--- a/solution.py
+++ b/solution.py
@@ -45,7 +45,7 @@
     column_mask = mask_ref[...].astype(WIDE_TYPE)
 
     def one_row(i, carry):
-        values = load(i).T
+        values = load(i).T.astype(WIDE_TYPE)
         mean_value = jnp.mean(values, axis=0, keepdims=True)
         centred = values - mean_value
         variance = jnp.mean(centred * centred, axis=0, keepdims=True)
@@ -62,23 +62,29 @@
     lax.fori_loop(0, rows, one_row, 0, unroll=min(rows, 8))
 
 
-def read_edges(edges, start, size):
-    return jnp.concatenate([part[pl.ds(start, size), :] for part in edges], axis=1).astype(NARROW)
-
-
-def edge_kernel(unit, count, me_ref, chain_ref, mask_ref, gain_ref, gate_ref, value_ref, *rest):
-    pair_refs, out_ref, edges = rest[:count], rest[count], rest[count + 1 :]
+def read_rows(parts, h, size):
+    at = pl.ds(pl.multiple_of(h * size, size), size)
+    return jnp.concatenate([part[at, :] for part in parts], axis=1)
+
+
+def edge_kernel(unit, offset, count, ready, me_ref, chain_ref, mask_ref, gain_ref, gate_ref, value_ref, *rest):
+    pair_refs, ready_refs, out_ref, edges = rest[:count], rest[count:][:ready], rest[count + ready], rest[count + ready + 1 :]
     rows = out_ref.shape[1]
+    fresh = sum(ref.shape[0] for ref in pair_refs)
     at = 0
     for pair_ref in pair_refs:
         size = pair_ref.shape[0]
-        first = (me_ref[0] ^ unit) * rows + at
-        load = lambda i: pair_ref[i].astype(WIDE_TYPE)
-        fill_edges(first, at, size, rows, load, chain_ref, mask_ref, gain_ref, (gate_ref, value_ref), edges)
+        first = (me_ref[0] ^ unit) * rows + offset + at
+        load = lambda i: pair_ref[i]
+        fill_edges(first, at, size, fresh, load, chain_ref, mask_ref, gain_ref, (gate_ref, value_ref), edges)
         at += size
 
     def one_channel(h, carry):
-        out_ref[h] = read_edges(edges, pl.multiple_of(h * rows, rows), rows)
+        pieces = [(offset, read_rows(edges, h, fresh))]
+        if ready:
+            pieces.append((fresh - offset, read_rows(ready_refs, h, rows - fresh)))
+        pieces.sort(key=lambda piece: piece[0])
+        out_ref[h] = jnp.concatenate([piece for _, piece in pieces], axis=0).astype(NARROW)
         return carry
 
     lax.fori_loop(0, out_ref.shape[0], one_channel, 0, unroll=16)
@@ -91,8 +97,9 @@
     at = 0
     for offset, pair_ref in zip(offsets, pair_refs):
         size = pair_ref.shape[0]
-        first = home_of(me_ref[0], unit, base) * span + offset
-        load = lambda i: pair_ref[i].astype(WIDE_TYPE)
+        home = me_ref[0] ^ unit if base is None else home_of(me_ref[0], unit, base)
+        first = home * span + offset
+        load = lambda i: pair_ref[i]
         fill_edges(first, at, size, total, load, chain_ref, mask_ref, gain_ref, (gate_ref, value_ref), edges)
         at += size
 
@@ -207,20 +214,20 @@
     return [pltpu.VMEM((hidden * rows, LANES), WIDE_TYPE)] * (residues // LANES)
 
 
-def edge_call(deps, unit, me, chain, mask, gain, gate, value, pairs):
-    rows = sum(p.shape[0] for p in pairs)
+def edge_call(deps, unit, offset, rows, cost, me, chain, mask, gain, gate, value, pairs, ready=()):
+    fresh = sum(p.shape[0] for p in pairs)
     residues = pairs[0].shape[1]
     hidden = gate.shape[1]
     return pl.pallas_call(
-        behind(functools.partial(edge_kernel, unit, len(pairs)), len(deps)),
+        behind(functools.partial(edge_kernel, unit, offset, len(pairs), len(ready)), len(deps)),
         out_shape=jax.ShapeDtypeStruct((hidden, rows, residues), NARROW),
-        in_specs=[ANY] * len(deps) + [SMEM] * 2 + [VMEM] * (4 + len(pairs)),
+        in_specs=[ANY] * len(deps) + [SMEM] * 2 + [VMEM] * (4 + len(pairs) + len(ready)),
         out_specs=VMEM,
-        scratch_shapes=edge_scratch(rows, hidden, residues),
+        scratch_shapes=edge_scratch(fresh, hidden, residues),
         compiler_params=pltpu.CompilerParams(vmem_limit_bytes=16 << 20),
-        cost_estimate=SHORT,
+        cost_estimate=cost,
         name="edges",
-    )(*deps, me, chain, mask, gain, gate, value, *pairs)
+    )(*deps, me, chain, mask, gain, gate, value, *pairs, *ready)
 
 
 def left_call(deps, unit, base, span, offsets, cost, me, chain, mask, gain, gate, value, pairs):
@@ -316,11 +323,8 @@
 
 def make_shards(count):
     bits = [1 << b for b in range(count.bit_length() - 1)]
-    right_bits = bits[0::2][::-1]
-    left_bits = bits[1::2][::-1]
-
-    far_bit, near_bits = left_bits[0], left_bits[1:]
-    low_bit = right_bits[0]
+    near_bit, far_bit, low_bit = bits[0], bits[-1], bits[-2]
+    side_bits = bits[1:-2][::-1]
     base = (far_bit, low_bit)
 
     def swap(values, mask):
@@ -330,13 +334,6 @@
         inner = lambda d: bool(d & far_bit) != bool(d & low_bit)
         pairs = [(d, d ^ far_bit ^ low_bit if inner(d) else d) for d in range(count)]
         return lax.ppermute(values, "wide", pairs)
-
-    def gather(own, bits):
-        units = {0: own}
-        for bit in bits:
-            for unit in list(units):
-                units[unit ^ bit] = swap(units[unit], bit)
-        return units
 
     def shards(
         pair,
@@ -358,13 +355,18 @@
         offsets = (0, half)
         own = split_call(pair, 2)
 
-        def right_edges(deps, unit, raws):
-            return edge_call(deps, unit, me, residue_mask, mask, gain, right_gate, right_value, raws)
-
-        def left_edges(deps, unit, at, cost, raws):
+        def right_edges(deps, unit, offset, raws, ready=(), cost=SHORT):
+            return edge_call(
+                deps, unit, offset, rows, cost, me, residue_mask, mask, gain, right_gate, right_value, raws, ready
+            )
+
+        def piece_edges(weights, shift, deps, unit, at, cost, raws):
             return left_call(
-                deps, unit, base, rows, at, cost, me, residue_mask, mask, gain, left_gate, left_value, raws
+                deps, unit, shift, rows, at, cost, me, residue_mask, mask, gain, *weights, raws
             )
+
+        right_piece = functools.partial(piece_edges, (right_gate, right_value), None)
+        left_edges = functools.partial(piece_edges, (left_gate, left_value), base)
 
         blocks = []
         places = []
@@ -380,43 +382,59 @@
                 places.append((unit, parts))
             return outs[0]
 
+        first = cross(pair)
         side = [swap(piece, low_bit) for piece in own]
-        first = [cross(piece) for piece in own]
-        near_first = [gather(piece, near_bits) for piece in first]
-        units = list(near_first[0])[1:]
-        right_own = right_edges((), 0, own)
-        right_side = right_edges((right_own, *[near_first[0][unit] for unit in units]), low_bit, side)
-        right = {}
-        for unit, edges in ((0, right_own), (low_bit, right_side)):
-            for more, moved in gather(edges, right_bits[1:]).items():
-                right[unit ^ more] = moved
+        right = {0: right_edges((), 0, 0, own)}
+        last = right[0]
+        plain = {0: own[::-1]}
+        for bit in side_bits:
+            for unit in list(plain):
+                plain[unit ^ bit] = [swap(piece, bit) for piece in plain[unit]]
+        others = list(plain)[1:]
+        side[0] = hold(side[0], last)
+        side_ready = right_piece((last,), low_bit, (0,), SHORT, side[:1])
+        last = side_ready[0]
+        plain_ready = {}
+        for unit in others:
+            plain_ready[unit] = right_piece((last,), unit, (half,), SHORT, plain[unit][:1])
+            last = plain_ready[unit][0]
+        first = hold(first, last)
+        left = left_edges((last,), 0, (0,), SHORT, [first])
+        last = left[0]
+        for unit in others:
+            last = right[unit] = right_edges((last,), unit, 0, plain[unit][1:], plain_ready[unit])
+        side[1] = hold(side[1], last)
+        last = right[low_bit] = right_edges((last,), low_bit, half, side[1:], side_ready, LONG)
+        both = {low_bit: side}
+        for bit in side_bits:
+            for unit in [unit ^ low_bit for unit in both]:
+                across = hold(plain[unit ^ bit][0], first)
+                there = [swap(both[unit ^ low_bit][0], bit), swap(across, low_bit)]
+                both[unit ^ bit ^ low_bit] = there
+        second = [cross(piece) for piece in side]
+        first_near = swap(first, near_bit)
+        left_near = left_edges((last,), near_bit, (0,), SHORT, [first_near])
+        last = left_near[0]
+        second[0] = hold(second[0], last)
+        early = left_edges((), low_bit, (0,), SHORT, second[:1])
+        last = early[0]
+        for unit in list(both)[1:]:
+            last = right[unit] = right_edges((last,), unit, 0, both[unit])
         order = list(right)
-        rights = [right[unit] for unit in order]
-        second = [cross(piece) for piece in side]
-
-        left_first = left_edges((right_side,), 0, offsets, SHORT, first)
-        start = [(0, at, raw) for at, raw in zip(offsets, first)]
-        early = [(unit, 0, near_first[0][unit]) for unit in units]
-        lefts = [left_edges((left_first[0],), unit, (at,), SHORT, [raw]) for unit, at, raw in early]
-        second[0] = hold(second[0], *[left[0] for left in lefts])
-        late = [(low_bit, 0, second[0])] + [(unit, half, near_first[1][unit]) for unit in units]
-        for unit, at, raw in late:
-            lefts.append(left_edges((), unit, (at,), SHORT, [raw]))
-        early[0] = (*early[0][:2], hold(early[0][2], lefts[len(early)][0], cost=LONG))
-        done = finish((), start + early + late, [left_first] + lefts)
-        sent = len(blocks)
-
-        second[1] = hold(second[1], done)
-        near_second = [gather(piece, near_bits) for piece in second]
-        batch = [(low_bit, half, second[1])]
-        batch += [(low_bit ^ unit, 0, near_second[0][unit]) for unit in units]
-        lefts = [left_edges((done,), unit, (at,), SHORT, [raw]) for unit, at, raw in batch]
-        done = finish((), batch, lefts)
-
-        batch = [(low_bit ^ unit, half, near_second[1][unit]) for unit in units]
-        deps = (done, *blocks[1:sent])
-        lefts = [left_edges(deps, unit, (at,), SHORT, [raw]) for unit, at, raw in batch]
-        finish((), batch, lefts)
+        rights = list(right.values())
+        early_near = swap(second[0], near_bit)
+        left_early = left_edges((last,), low_bit ^ near_bit, (0,), SHORT, [early_near])
+        done = finish(
+            (),
+            [(0, 0, first), (near_bit, 0, first_near), (low_bit, 0, second[0]), (low_bit ^ near_bit, 0, early_near)],
+            [left, left_near, early, left_early],
+        )
+
+        late_raw = hold(second[1], done)
+        late_near = swap(late_raw, near_bit)
+        late = left_edges((done,), low_bit, (half,), SHORT, [late_raw])
+        left_late = left_edges((late[0],), low_bit ^ near_bit, (half,), SHORT, [late_near])
+        finish((), [(low_bit, half, late_raw), (low_bit ^ near_bit, half, late_near)], [late, left_late])
         return place_call(places, base, rows, me, blocks, (count * rows, rows, pair.shape[2]))
 
     return shards

time: 82.4 us -> 79.1 us (0.960)
  starting transfers between devices: 30.7 us -> 20.4 us
  waiting for transfers between devices: 15.8 us -> 19.7 us
  Pallas kernels: 32.5 us -> 34.8 us
    ppermute x17 -> x15, starting transfers between devices: 26 us -> 16.2 us  [swap(): return lax.ppermute(values, 'wide', [(d, d ^ mask) for d in range(count)])]
    ppermute x17 -> x15, waiting for transfers between devices: 15.8 us -> 19.7 us  [swap(): return lax.ppermute(values, 'wide', [(d, d ^ mask) for d in range(count)])]
    pallas_call x2 -> x4, Pallas kernels: 6.25 us -> 8.95 us  [edge_call(): pl.pallas_call(behind(functools.partial(edge_kernel, unit, offset, len(pa...]
    pallas_call x3 -> x2, Pallas kernels: 13.5 us -> 11.5 us  [triangle_call(): pl.pallas_call(behind(functools.partial(triangle_kernel, len(pairs), orde...]
    pallas_call x7 -> x8, Pallas kernels: 11.3 us -> 13.1 us  [left_call(): pl.pallas_call(behind(functools.partial(left_kernel, unit, base, span, of...]
    ppermute x4 -> x3, starting transfers between devices: 4.75 us -> 4.26 us  [cross(): return lax.ppermute(values, 'wide', pairs)]
  transfers between devices with their start and end apart: 21 -> 18, of which waited for: 5 -> 6; matrix products, arithmetic and copies ran while one was open for 0% -> 0% of each run, Pallas kernels for 38% -> 43%
where the time goes in v5:
time: 79.1 us; the launch traced here: 78.6 us
  Pallas kernels  34.8 us (44%)
  starting transfers between devices  20.4 us (26%)
  waiting for transfers between devices  19.7 us (25%)
  local copies, waits for them, and re-layouts  3.22 us (4%)
    ppermute x15, waiting for transfers between devices, swap(): return lax.ppermute(values, 'wide', [(d, d ^ mask) for d in range(count)])  19.7 us
    ppermute x15, starting transfers between devices, swap(): return lax.ppermute(values, 'wide', [(d, d ^ mask) for d in range(count)])  16.2 us
    pallas_call x8, Pallas kernels, left_call(): pl.pallas_call(behind(functools.partial(left_kernel, unit, base, span, of...  13.1 us
    pallas_call x2, Pallas kernels, triangle_call(): pl.pallas_call(behind(functools.partial(triangle_kernel, len(pairs), orde...  11.5 us
    pallas_call x4, Pallas kernels, edge_call(): pl.pallas_call(behind(functools.partial(edge_kernel, unit, offset, len(pa...  8.95 us
    ppermute x3, starting transfers between devices, cross(): return lax.ppermute(values, 'wide', pairs)  4.26 us
    unnamed x20, local copies, waits for them, and re-layouts  3.22 us
  transfers between devices with their start and end apart: 18, of which 6 were waited for; matrix products, arithmetic and copies ran while one was open for 0% of the time, Pallas kernels for 43%

profile of v5, /device:TPU:0, one launch (start us, length us, event | category | flops | bytes accessed | tf_op | source)
XLA Modules:
  0.0 78.6 jit_solution(9495573136230728097)
XLA Ops:
  0.0 1.9 %collective-permute-start.2 = (bf16[16,256,128]{2,1,0:T(8,128)(2,1)}, bf16[16,256,128]{2,1,0:T(8,128)(2,1)S(1)}, u32[]{:S(2)}, u32[]{:S(2)}) collective-permute-start(bf16[16,256,128]{2,1,0:T(8,128)(2,1)} %in_ref.1), channel_id=1, source_target_pairs={{0,0},{1,1},{2,2},{3,3},{4,8},{5,9},{6,10},{7,11},{8,4},{9,5},{10,... | collective-permute-start | bytes 3145736 | tf_op jit(solution)/shard_map/ppermute | solution.py:336
  3.2 4.7 %collective-permute-start = (bf16[8,256,128]{2,1,0:T(8,128)(2,1)S(1)}, bf16[8,256,128]{2,1,0:T(8,128)(2,1)S(1)}, u32[]{:S(2)}, u32[]{:S(2)}) collective-permute-start(bf16[8,256,128]{2,1,0:T(8,128)(2,1)S(1)} %get-tuple-element.31.refs_6_), channel_id=1, source_target_pairs={{0,4},{1,5},{2,6},{3,7},{4,0},{5,1},{6,2},{7,3},{8,12},{9,13},{10,... | collective-permute-start | bytes 1572872 | tf_op jit(solution)/shard_map/ppermute | solution.py:331
  7.9 1.5 %collective-permute-start.1 = (bf16[8,256,128]{2,1,0:T(8,128)(2,1)S(1)}, bf16[8,256,128]{2,1,0:T(8,128)(2,1)S(1)}, u32[]{:S(2)}, u32[]{:S(2)}) collective-permute-start(bf16[8,256,128]{2,1,0:T(8,128)(2,1)S(1)} %get-tuple-element.32.refs_7_), channel_id=1, source_target_pairs={{0,2},{1,3},{2,0},{3,1},{4,6},{5,7},{6,4},{7,5},{8,10},{9,11},{10,... | collective-permute-start | bytes 1572872 | tf_op jit(solution)/shard_map/ppermute | solution.py:331
  10.7 2.5 %edges.4.refs_1_.refs_0_.refs_5_ = bf16[128,16,256]{2,1,0:T(8,128)(2,1)S(1)} custom-call(s32[1]{0:T(128)} %bitcast.refs_0_.refs_1_.me_ref, s32[256]{0:T(256)S(1)} %copy-done.5, s32[1,256]{1,0:T(1,128)S(1)} %bitcast.3, f32[1,128]{1,0:T(1,128)S(1)} %bitcast.15, bf16[128,128]{1,0:T(8,128)(2,1)S(1)} %copy-done.3, bf16[128,128]{1,0:T(8,128)(2,1)S(1)} %copy-done.4, ...), custom_call_target="tpu_custom_call" | custom-call | flops 1048576 | bytes 1024 | tf_op jit(solution)/shard_map/edges/pallas_call | solution.py:221
  13.2 7.5 %collective-permute-done.refs_0_ = bf16[8,256,128]{2,1,0:T(8,128)(2,1)S(1)} collective-permute-done((bf16[8,256,128]{2,1,0:T(8,128)(2,1)S(1)}, bf16[8,256,128]{2,1,0:T(8,128)(2,1)S(1)}, u32[]{:S(2)}, u32[]{:S(2)}) %collective-permute-start) | collective-permute-done | bytes 524320 | tf_op jit(solution)/shard_map/ppermute | solution.py:331
  20.7 1.5 %collective-permute-start.7 = (bf16[8,256,128]{2,1,0:T(8,128)(2,1)S(1)}, bf16[8,256,128]{2,1,0:T(8,128)(2,1)S(1)}, u32[]{:S(2)}, u32[]{:S(2)}) collective-permute-start(bf16[8,256,128]{2,1,0:T(8,128)(2,1)S(1)} %hold.6.refs_7_), channel_id=1, source_target_pairs={{0,2},{1,3},{2,0},{3,1},{4,6},{5,7},{6,4},{7,5},{8,10},{9,11},{10,... | collective-permute-start | bytes 1572872 | tf_op jit(solution)/shard_map/ppermute | solution.py:331
  24.2 1.3 %left_edges.9 = (f32[1024,128]{1,0:T(8,128)S(1)}, f32[1024,128]{1,0:T(8,128)S(1)}) custom-call(f32[1024,128]{1,0:T(8,128)S(1)} %get-tuple-element.33.refs_0_.refs_8_, s32[1]{0:T(128)} %bitcast.refs_0_.refs_1_.me_ref, s32[256]{0:T(256)S(1)} %copy-done.5, s32[1,256]{1,0:T(1,128)S(1)} %bitcast.5, f32[1,128]{1,0:T(1,128)S(1)} %bitcast.17, ...), custom_call_target="tpu_custom_call" | custom-call | flops 1048576 | bytes 1024 | tf_op jit(solution)/shard_map/left_edges/pallas_call | solution.py:238
  26.4 2.6 %left_edges.10 = (f32[2048,128]{1,0:T(8,128)S(1)}, f32[2048,128]{1,0:T(8,128)S(1)}) custom-call(f32[1024,128]{1,0:T(8,128)S(1)} %get-tuple-element.34.refs_1_.refs_0_.refs_8_, s32[1]{0:T(128)} %bitcast.refs_0_.refs_1_.me_ref, s32[256]{0:T(256)S(1)} %copy-done.5, s32[1,256]{1,0:T(1,128)S(1)} %bitcast.6, f32[1,128]{1,0:T(1,128)S(1)} %bitcast.18, ...), custom_call_target="tpu_custom_call" | custom-call | flops 1048576 | bytes 1024 | tf_op jit(solution)/shard_map/left_edges/pallas_call | solution.py:238
  29.0 5.2 %collective-permute-done.3.refs_7_ = bf16[8,256,128]{2,1,0:T(8,128)(2,1)} collective-permute-done((bf16[8,256,128]{2,1,0:T(8,128)(2,1)S(1)}, bf16[8,256,128]{2,1,0:T(8,128)(2,1)}, u32[]{:S(2)}, u32[]{:S(2)}) %collective-permute-start.3) | collective-permute-done | bytes 524320 | tf_op jit(solution)/shard_map/ppermute | solution.py:331
  34.6 1.9 %edges.5.refs_1_.refs_0_.refs_6_ = bf16[128,16,256]{2,1,0:T(8,128)(2,1)S(1)} custom-call(f32[2048,128]{1,0:T(8,128)S(1)} %get-tuple-element.35.refs_0_.refs_13_, s32[1]{0:T(128)} %bitcast.refs_0_.refs_1_.me_ref, s32[256]{0:T(256)S(1)} %copy-done.5, s32[1,256]{1,0:T(1,128)S(1)} %bitcast.7, f32[1,128]{1,0:T(1,128)S(1)} %bitcast.19, ...), custom_call_target="tpu_custom_call" | custom-call | flops 1048576 | bytes 1024 | tf_op jit(solution)/shard_map/edges/pallas_call | solution.py:221
  36.6 2.0 %edges.6.refs_0_.refs_7_ = bf16[128,16,256]{2,1,0:T(8,128)(2,1)S(1)} custom-call(bf16[128,16,256]{2,1,0:T(8,128)(2,1)S(1)} %edges.5.refs_1_.refs_0_.refs_6_, s32[1]{0:T(128)} %bitcast.refs_0_.refs_1_.me_ref, s32[256]{0:T(256)S(1)} %copy-done.5, s32[1,256]{1,0:T(1,128)S(1)} %bitcast.8, f32[1,128]{1,0:T(1,128)S(1)} %bitcast.20, ...), custom_call_target="tpu_custom_call" | custom-call | flops 34359738368 | bytes 1024 | tf_op jit(solution)/shard_map/edges/pallas_call | solution.py:221
  38.6 2.6 %left_edges.11 = (f32[2048,128]{1,0:T(8,128)S(1)}, f32[2048,128]{1,0:T(8,128)S(1)}) custom-call(bf16[128,16,256]{2,1,0:T(8,128)(2,1)S(1)} %edges.6.refs_0_.refs_7_, s32[1]{0:T(128)} %bitcast.refs_0_.refs_1_.me_ref, s32[256]{0:T(256)S(1)} %copy-done.5, s32[1,256]{1,0:T(1,128)S(1)} %bitcast.9, f32[1,128]{1,0:T(1,128)S(1)} %bitcast.21, ...), custom_call_target="tpu_custom_call" | custom-call | flops 1048576 | bytes 1024 | tf_op jit(solution)/shard_map/left_edges/pallas_call | solution.py:238
  41.3 1.7 %collective-permute-start.13 = (bf16[8,256,128]{2,1,0:T(8,128)(2,1)}, bf16[8,256,128]{2,1,0:T(8,128)(2,1)S(1)}, u32[]{:S(2)}, u32[]{:S(2)}) collective-permute-start(bf16[8,256,128]{2,1,0:T(8,128)(2,1)} %hold.8.refs_7_), channel_id=1, source_target_pairs={{0,0},{1,1},{2,2},{3,3},{4,8},{5,9},{6,10},{7,11},{8,4},{9,5},{10,... | collective-permute-start | bytes 1572872 | tf_op jit(solution)/shard_map/ppermute | solution.py:336
  44.3 2.1 %collective-permute-done.8.refs_8_ = bf16[8,256,128]{2,1,0:T(8,128)(2,1)S(1)} collective-permute-done((bf16[8,256,128]{2,1,0:T(8,128)(2,1)S(1)}, bf16[8,256,128]{2,1,0:T(8,128)(2,1)S(1)}, u32[]{:S(2)}, u32[]{:S(2)}) %collective-permute-start.8) | collective-permute-done | bytes 524320 | tf_op jit(solution)/shard_map/ppermute | solution.py:331
  46.5 2.5 %edges.7.refs_0_.refs_8_ = bf16[128,16,256]{2,1,0:T(8,128)(2,1)S(1)} custom-call(f32[1024,128]{1,0:T(8,128)S(1)} %get-tuple-element.39.refs_0_.refs_17_, s32[1]{0:T(128)} %bitcast.refs_0_.refs_1_.me_ref, s32[256]{0:T(256)S(1)} %copy-done.5, s32[1,256]{1,0:T(1,128)S(1)} %bitcast.11, f32[1,128]{1,0:T(1,128)S(1)} %bitcast.23, bf16[128,128]{1,0:T(8,128)(2,1)S(1)} %copy-done.3, ...), custom_call_target="tpu_custom_call" | custom-call | flops 1048576 | bytes 1024 | tf_op jit(solution)/shard_map/edges/pallas_call | solution.py:221
  51.0 7.4 %triangle.2 = (bf16[48,16,128]{2,1,0:T(8,128)(2,1)S(1)}, bf16[48,16,128]{2,1,0:T(8,128)(2,1)S(1)}, bf16[48,16,128]{2,1,0:T(8,128)(2,1)S(1)}, bf16[48,16,128]{2,1,0:T(8,128)(2,1)S(1)}) custom-call(s32[1]{0:T(128)} %bitcast.refs_0_.refs_1_.me_ref, f32[128]{0:T(128)S(1)} %copy-done.9, f32[1,128]{1,0:T(1,128)S(1)} %bitcast.25, bf16[128,128]{1,0:T(8,128)(2,1)S(1)} %copy-done.6, ...), custom_call_target="tpu_custom_call" | custom-call | flops 1048576 | bytes 1024 | tf_op jit(solution)/shard_map/triangle/pallas_call | solution.py:257
  58.6 1.6 %collective-permute-start.10 = (bf16[48,16,128]{2,1,0:T(8,128)(2,1)S(1)}, bf16[48,16,128]{2,1,0:T(8,128)(2,1)S(1)}, u32[]{:S(2)}, u32[]{:S(2)}) collective-permute-start(bf16[48,16,128]{2,1,0:T(8,128)(2,1)S(1)} %get-tuple-element.46), channel_id=1, source_target_pairs={{0,2},{1,3},{2,0},{3,1},{4,6},{5,7},{6,4},{7,5},{8,10},{9,11},{10,... | collective-permute-start | bytes 589832 | tf_op jit(solution)/shard_map/ppermute | solution.py:331
  60.1 1.7 %collective-permute-start.11 = (bf16[48,16,128]{2,1,0:T(8,128)(2,1)S(1)}, bf16[48,16,128]{2,1,0:T(8,128)(2,1)S(1)}, u32[]{:S(2)}, u32[]{:S(2)}) collective-permute-start(bf16[48,16,128]{2,1,0:T(8,128)(2,1)S(1)} %get-tuple-element.47), channel_id=1, source_target_pairs={{0,4},{1,5},{2,6},{3,7},{4,0},{5,1},{6,2},{7,3},{8,12},{9,13},{10,... | collective-permute-start | bytes 589832 | tf_op jit(solution)/shard_map/ppermute | solution.py:331
  63.4 1.3 %left_edges.15 = (f32[1024,128]{1,0:T(8,128)S(1)}, f32[1024,128]{1,0:T(8,128)S(1)}) custom-call(f32[1024,128]{1,0:T(8,128)S(1)} %get-tuple-element.49.refs_0_.refs_11_, s32[1]{0:T(128)} %bitcast.refs_0_.refs_1_.me_ref, s32[256]{0:T(256)S(1)} %copy-done.5, s32[1,256]{1,0:T(1,128)S(1)} %bitcast.14, f32[1,128]{1,0:T(1,128)S(1)} %bitcast.27, ...), custom_call_target="tpu_custom_call" | custom-call | flops 1048576 | bytes 1024 | tf_op jit(solution)/shard_map/left_edges/pallas_call | solution.py:238
  64.8 4.0 %triangle.3 = (bf16[16,16,128]{2,1,0:T(8,128)(2,1)S(1)}, bf16[16,16,128]{2,1,0:T(8,128)(2,1)S(1)}, bf16[16,16,128]{2,1,0:T(8,128)(2,1)S(1)}, bf16[16,16,128]{2,1,0:T(8,128)(2,1)S(1)}) custom-call(s32[1]{0:T(128)} %bitcast.refs_0_.refs_1_.me_ref, f32[128]{0:T(128)S(1)} %copy-done.9, f32[1,128]{1,0:T(1,128)S(1)} %bitcast.28, bf16[128,128]{1,0:T(8,128)(2,1)S(1)} %copy-done.6, ...), custom_call_target="tpu_custom_call" | custom-call | flops 1048576 | bytes 1024 | tf_op jit(solution)/shard_map/triangle/pallas_call | solution.py:257
  68.8 1.6 %collective-permute-start.15 = (bf16[16,16,128]{2,1,0:T(8,128)(2,1)S(1)}, bf16[16,16,128]{2,1,0:T(8,128)(2,1)S(1)}, u32[]{:S(2)}, u32[]{:S(2)}) collective-permute-start(bf16[16,16,128]{2,1,0:T(8,128)(2,1)S(1)} %get-tuple-element.54), channel_id=1, source_target_pairs={{0,2},{1,3},{2,0},{3,1},{4,6},{5,7},{6,4},{7,5},{8,10},{9,11},{10,... | collective-permute-start | bytes 196616 | tf_op jit(solution)/shard_map/ppermute | solution.py:331
  70.4 1.7 %collective-permute-start.16 = (bf16[16,16,128]{2,1,0:T(8,128)(2,1)S(1)}, bf16[16,16,128]{2,1,0:T(8,128)(2,1)S(1)}, u32[]{:S(2)}, u32[]{:S(2)}) collective-permute-start(bf16[16,16,128]{2,1,0:T(8,128)(2,1)S(1)} %get-tuple-element.55), channel_id=1, source_target_pairs={{0,4},{1,5},{2,6},{3,7},{4,0},{5,1},{6,2},{7,3},{8,12},{9,13},{10,... | collective-permute-start | bytes 196616 | tf_op jit(solution)/shard_map/ppermute | solution.py:331
  73.2 2.0 %collective-permute-done.16.rest_6_ = bf16[16,16,128]{2,1,0:T(8,128)(2,1)S(1)} collective-permute-done((bf16[16,16,128]{2,1,0:T(8,128)(2,1)S(1)}, bf16[16,16,128]{2,1,0:T(8,128)(2,1)S(1)}, u32[]{:S(2)}, u32[]{:S(2)}) %collective-permute-start.16) | collective-permute-done | bytes 65568 | tf_op jit(solution)/shard_map/ppermute | solution.py:331
  75.2 2.2 %collective-permute-done.17.rest_7_ = bf16[16,16,128]{2,1,0:T(8,128)(2,1)S(1)} collective-permute-done((bf16[16,16,128]{2,1,0:T(8,128)(2,1)S(1)}, bf16[16,16,128]{2,1,0:T(8,128)(2,1)S(1)}, u32[]{:S(2)}, u32[]{:S(2)}) %collective-permute-start.17) | collective-permute-done | bytes 65568 | tf_op jit(solution)/shard_map/ppermute | solution.py:331
  (54 shorter events, 13.0 us)
Async XLA Ops:
  0.0 25.6 %collective-permute-start.2 = (bf16[16,256,128]{2,1,0:T(8,128)(2,1)}, bf16[16,256,128]{2,1,0:T(8,128)(2,1)S(1)}, u32[]{:S(2)}, u32[]{:S(2)}) collective-permute-start(bf16[16,256,128]{2,1,0:T(8,128)(2,1)} %in_ref.1), channel_id=1, source_target_pairs={{0,0},{1,1},{2,2},{3,3},{4,8},{5,9},{6,10},{7,11},{8,4},{9,5},{10,... | collective-permute-start | bytes 3145736 | tf_op jit(solution)/shard_map/ppermute | solution.py:336
  1.9 1.2 %copy-start.2 = (bf16[16,256,128]{2,1,0:T(8,128)(2,1)S(1)}, bf16[16,256,128]{2,1,0:T(8,128)(2,1)}, u32[]{:S(2)}) copy-start(bf16[16,256,128]{2,1,0:T(8,128)(2,1)} %in_ref.1) | copy-start | bytes 3145732
  3.1 6.9 %copy-start.3 = (bf16[128,128]{1,0:T(8,128)(2,1)S(1)}, bf16[128,128]{1,0:T(8,128)(2,1)}, u32[]{:S(2)}) copy-start(bf16[128,128]{1,0:T(8,128)(2,1)} %refs_5_.20) | copy-start | bytes 98308
  3.1 6.9 %copy-start.4 = (bf16[128,128]{1,0:T(8,128)(2,1)S(1)}, bf16[128,128]{1,0:T(8,128)(2,1)}, u32[]{:S(2)}) copy-start(bf16[128,128]{1,0:T(8,128)(2,1)} %refs_6_.16) | copy-start | bytes 98308
  3.2 17.5 %collective-permute-start = (bf16[8,256,128]{2,1,0:T(8,128)(2,1)S(1)}, bf16[8,256,128]{2,1,0:T(8,128)(2,1)S(1)}, u32[]{:S(2)}, u32[]{:S(2)}) collective-permute-start(bf16[8,256,128]{2,1,0:T(8,128)(2,1)S(1)} %get-tuple-element.31.refs_6_), channel_id=1, source_target_pairs={{0,4},{1,5},{2,6},{3,7},{4,0},{5,1},{6,2},{7,3},{8,12},{9,13},{10,... | collective-permute-start | bytes 1572872 | tf_op jit(solution)/shard_map/ppermute | solution.py:331
  7.9 15.6 %collective-permute-start.1 = (bf16[8,256,128]{2,1,0:T(8,128)(2,1)S(1)}, bf16[8,256,128]{2,1,0:T(8,128)(2,1)S(1)}, u32[]{:S(2)}, u32[]{:S(2)}) collective-permute-start(bf16[8,256,128]{2,1,0:T(8,128)(2,1)S(1)} %get-tuple-element.32.refs_7_), channel_id=1, source_target_pairs={{0,2},{1,3},{2,0},{3,1},{4,6},{5,7},{6,4},{7,5},{8,10},{9,11},{10,... | collective-permute-start | bytes 1572872 | tf_op jit(solution)/shard_map/ppermute | solution.py:331
  9.4 24.7 %collective-permute-start.3 = (bf16[8,256,128]{2,1,0:T(8,128)(2,1)S(1)}, bf16[8,256,128]{2,1,0:T(8,128)(2,1)}, u32[]{:S(2)}, u32[]{:S(2)}) collective-permute-start(bf16[8,256,128]{2,1,0:T(8,128)(2,1)S(1)} %get-tuple-element.31.refs_6_), channel_id=1, source_target_pairs={{0,2},{1,3},{2,0},{3,1},{4,6},{5,7},{6,4},{7,5},{8,10},{9,11},{10,... | collective-permute-start | bytes 1572872 | tf_op jit(solution)/shard_map/ppermute | solution.py:331
  9.9 26.6 %collective-permute-start.4 = (bf16[8,256,128]{2,1,0:T(8,128)(2,1)S(1)}, bf16[8,256,128]{2,1,0:T(8,128)(2,1)}, u32[]{:S(2)}, u32[]{:S(2)}) collective-permute-start(bf16[8,256,128]{2,1,0:T(8,128)(2,1)S(1)} %get-tuple-element.32.refs_7_), channel_id=1, source_target_pairs={{0,4},{1,5},{2,6},{3,7},{4,0},{5,1},{6,2},{7,3},{8,12},{9,13},{10,... | collective-permute-start | bytes 1572872 | tf_op jit(solution)/shard_map/ppermute | solution.py:331
  20.7 23.6 %collective-permute-start.7 = (bf16[8,256,128]{2,1,0:T(8,128)(2,1)S(1)}, bf16[8,256,128]{2,1,0:T(8,128)(2,1)S(1)}, u32[]{:S(2)}, u32[]{:S(2)}) collective-permute-start(bf16[8,256,128]{2,1,0:T(8,128)(2,1)S(1)} %hold.6.refs_7_), channel_id=1, source_target_pairs={{0,2},{1,3},{2,0},{3,1},{4,6},{5,7},{6,4},{7,5},{8,10},{9,11},{10,... | collective-permute-start | bytes 1572872 | tf_op jit(solution)/shard_map/ppermute | solution.py:331
  23.5 17.7 %collective-permute-start.5 = (bf16[8,256,128]{2,1,0:T(8,128)(2,1)S(1)}, bf16[8,256,128]{2,1,0:T(8,128)(2,1)S(1)}, u32[]{:S(2)}, u32[]{:S(2)}) collective-permute-start(bf16[8,256,128]{2,1,0:T(8,128)(2,1)S(1)} %hold.6.refs_7_), channel_id=1, source_target_pairs={{0,0},{1,1},{2,2},{3,3},{4,8},{5,9},{6,10},{7,11},{8,4},{9,5},{10,... | collective-permute-start | bytes 1572872 | tf_op jit(solution)/shard_map/ppermute | solution.py:336
  25.6 0.8 copy-start.1
  25.6 12.9 %collective-permute-start.6 = (bf16[16,256,128]{2,1,0:T(8,128)(2,1)S(1)}, bf16[16,256,128]{2,1,0:T(8,128)(2,1)S(1)}, u32[]{:S(2)}, u32[]{:S(2)}) collective-permute-start(bf16[16,256,128]{2,1,0:T(8,128)(2,1)S(1)} %hold.7.refs_7_.refs_1_.refs_9_), channel_id=1, source_target_pairs={{0,1},{1,0},{2,3},{3,2},{4,5},{5,4},{6,7},{7,6},{8,9},{9,8},{10,11... | collective-permute-start | bytes 3145736 | tf_op jit(solution)/shard_map/ppermute | solution.py:331
  34.1 12.4 %collective-permute-start.8 = (bf16[8,256,128]{2,1,0:T(8,128)(2,1)S(1)}, bf16[8,256,128]{2,1,0:T(8,128)(2,1)S(1)}, u32[]{:S(2)}, u32[]{:S(2)}) collective-permute-start(bf16[8,256,128]{2,1,0:T(8,128)(2,1)S(1)} %hold.10), channel_id=1, source_target_pairs={{0,4},{1,5},{2,6},{3,7},{4,0},{5,1},{6,2},{7,3},{8,12},{9,13},{10,... | collective-permute-start | bytes 1572872 | tf_op jit(solution)/shard_map/ppermute | solution.py:331
  41.2 7.8 %collective-permute-start.9 = (bf16[8,256,128]{2,1,0:T(8,128)(2,1)S(1)}, bf16[8,256,128]{2,1,0:T(8,128)(2,1)S(1)}, u32[]{:S(2)}, u32[]{:S(2)}) collective-permute-start(bf16[8,256,128]{2,1,0:T(8,128)(2,1)S(1)} %hold.9.refs_6_.refs_11_), channel_id=1, source_target_pairs={{0,1},{1,0},{2,3},{3,2},{4,5},{5,4},{6,7},{7,6},{8,9},{9,8},{10,11... | collective-permute-start | bytes 1572872 | tf_op jit(solution)/shard_map/ppermute | solution.py:331
  41.3 17.2 %collective-permute-start.13 = (bf16[8,256,128]{2,1,0:T(8,128)(2,1)}, bf16[8,256,128]{2,1,0:T(8,128)(2,1)S(1)}, u32[]{:S(2)}, u32[]{:S(2)}) collective-permute-start(bf16[8,256,128]{2,1,0:T(8,128)(2,1)} %hold.8.refs_7_), channel_id=1, source_target_pairs={{0,0},{1,1},{2,2},{3,3},{4,8},{5,9},{6,10},{7,11},{8,4},{9,5},{10,... | collective-permute-start | bytes 1572872 | tf_op jit(solution)/shard_map/ppermute | solution.py:336
  49.0 1.4 %copy-start.6 = (bf16[128,128]{1,0:T(8,128)(2,1)S(1)}, bf16[128,128]{1,0:T(8,128)(2,1)}, u32[]{:S(2)}) copy-start(bf16[128,128]{1,0:T(8,128)(2,1)} %refs_3_.3) | copy-start | bytes 98308
  49.0 1.4 %copy-start.7 = (bf16[128,128]{1,0:T(8,128)(2,1)S(1)}, bf16[128,128]{1,0:T(8,128)(2,1)}, u32[]{:S(2)}) copy-start(bf16[128,128]{1,0:T(8,128)(2,1)} %refs_4_.7) | copy-start | bytes 98308
  58.5 5.0 %collective-permute-start.14 = (bf16[8,256,128]{2,1,0:T(8,128)(2,1)S(1)}, bf16[8,256,128]{2,1,0:T(8,128)(2,1)S(1)}, u32[]{:S(2)}, u32[]{:S(2)}) collective-permute-start(bf16[8,256,128]{2,1,0:T(8,128)(2,1)S(1)} %hold.11.refs_7_.refs_9_), channel_id=1, source_target_pairs={{0,1},{1,0},{2,3},{3,2},{4,5},{5,4},{6,7},{7,6},{8,9},{9,8},{10,11... | collective-permute-start | bytes 1572872 | tf_op jit(solution)/shard_map/ppermute | solution.py:331
  58.6 13.6 %collective-permute-start.10 = (bf16[48,16,128]{2,1,0:T(8,128)(2,1)S(1)}, bf16[48,16,128]{2,1,0:T(8,128)(2,1)S(1)}, u32[]{:S(2)}, u32[]{:S(2)}) collective-permute-start(bf16[48,16,128]{2,1,0:T(8,128)(2,1)S(1)} %get-tuple-element.46), channel_id=1, source_target_pairs={{0,2},{1,3},{2,0},{3,1},{4,6},{5,7},{6,4},{7,5},{8,10},{9,11},{10,... | collective-permute-start | bytes 589832 | tf_op jit(solution)/shard_map/ppermute | solution.py:331
  60.1 12.2 %collective-permute-start.11 = (bf16[48,16,128]{2,1,0:T(8,128)(2,1)S(1)}, bf16[48,16,128]{2,1,0:T(8,128)(2,1)S(1)}, u32[]{:S(2)}, u32[]{:S(2)}) collective-permute-start(bf16[48,16,128]{2,1,0:T(8,128)(2,1)S(1)} %get-tuple-element.47), channel_id=1, source_target_pairs={{0,4},{1,5},{2,6},{3,7},{4,0},{5,1},{6,2},{7,3},{8,12},{9,13},{10,... | collective-permute-start | bytes 589832 | tf_op jit(solution)/shard_map/ppermute | solution.py:331
  61.9 10.5 %collective-permute-start.12 = (bf16[48,16,128]{2,1,0:T(8,128)(2,1)S(1)}, bf16[48,16,128]{2,1,0:T(8,128)(2,1)S(1)}, u32[]{:S(2)}, u32[]{:S(2)}) collective-permute-start(bf16[48,16,128]{2,1,0:T(8,128)(2,1)S(1)} %get-tuple-element.48), channel_id=1, source_target_pairs={{0,6},{1,7},{2,4},{3,5},{4,2},{5,3},{6,0},{7,1},{8,14},{9,15},{10,... | collective-permute-start | bytes 589832 | tf_op jit(solution)/shard_map/ppermute | solution.py:331
  68.8 4.3 %collective-permute-start.15 = (bf16[16,16,128]{2,1,0:T(8,128)(2,1)S(1)}, bf16[16,16,128]{2,1,0:T(8,128)(2,1)S(1)}, u32[]{:S(2)}, u32[]{:S(2)}) collective-permute-start(bf16[16,16,128]{2,1,0:T(8,128)(2,1)S(1)} %get-tuple-element.54), channel_id=1, source_target_pairs={{0,2},{1,3},{2,0},{3,1},{4,6},{5,7},{6,4},{7,5},{8,10},{9,11},{10,... | collective-permute-start | bytes 196616 | tf_op jit(solution)/shard_map/ppermute | solution.py:331
  70.4 4.7 %collective-permute-start.16 = (bf16[16,16,128]{2,1,0:T(8,128)(2,1)S(1)}, bf16[16,16,128]{2,1,0:T(8,128)(2,1)S(1)}, u32[]{:S(2)}, u32[]{:S(2)}) collective-permute-start(bf16[16,16,128]{2,1,0:T(8,128)(2,1)S(1)} %get-tuple-element.55), channel_id=1, source_target_pairs={{0,4},{1,5},{2,6},{3,7},{4,0},{5,1},{6,2},{7,3},{8,12},{9,13},{10,... | collective-permute-start | bytes 196616 | tf_op jit(solution)/shard_map/ppermute | solution.py:331
  72.2 5.2 %collective-permute-start.17 = (bf16[16,16,128]{2,1,0:T(8,128)(2,1)S(1)}, bf16[16,16,128]{2,1,0:T(8,128)(2,1)S(1)}, u32[]{:S(2)}, u32[]{:S(2)}) collective-permute-start(bf16[16,16,128]{2,1,0:T(8,128)(2,1)S(1)} %get-tuple-element.56), channel_id=1, source_target_pairs={{0,6},{1,7},{2,4},{3,5},{4,2},{5,3},{6,0},{7,1},{8,14},{9,15},{10,... | collective-permute-start | bytes 196616 | tf_op jit(solution)/shard_map/ppermute | solution.py:331
  (4 other events, 2.8 us)

commit v6 on v5

--- a/solution.py
+++ b/solution.py
@@ -59,7 +59,7 @@
             ]
         return carry
 
-    lax.fori_loop(0, rows, one_row, 0, unroll=min(rows, 8))
+    lax.fori_loop(0, rows, one_row, 0, unroll=min(rows, 16))
 
 
 def read_rows(parts, h, size):
@@ -163,7 +163,7 @@
     homes = [(ref, i) for ref in pair_refs for i in range(ref.shape[0])]
     columns = [pl.multiple_of((me ^ unit) * width, width) for unit in order]
     for row in range(deep):
-        middle = triangle[pl.ds(row, hidden, stride=deep), :].T[: fold * span].astype(NARROW)
+        middle = triangle[pl.ds(row, hidden, stride=deep), :].astype(NARROW).T[: fold * span]
         projected = jnp.dot(middle, output_value_ref[...], preferred_element_type=WIDE_TYPE)
         base = jnp.concatenate(
             [
@@ -420,8 +420,8 @@
         last = early[0]
         for unit in list(both)[1:]:
             last = right[unit] = right_edges((last,), unit, 0, both[unit])
-        order = list(right)
-        rights = list(right.values())
+        order = [0] + list(right)[:0:-1]
+        rights = [right[unit] for unit in order]
         early_near = swap(second[0], near_bit)
         left_early = left_edges((last,), low_bit ^ near_bit, (0,), SHORT, [early_near])
         done = finish(

time: 79.1 us -> 77.8 us (0.984)
  waiting for transfers between devices: 19.7 us -> 18.9 us
    ppermute x15, waiting for transfers between devices: 19.7 us -> 18.9 us  [swap(): return lax.ppermute(values, 'wide', [(d, d ^ mask) for d in range(count)])]
where the time goes in v6:
time: 77.8 us; the launch traced here: 77.4 us
  Pallas kernels  34.5 us (44%)
  starting transfers between devices  20.2 us (26%)
  waiting for transfers between devices  18.9 us (24%)
  local copies, waits for them, and re-layouts  3.22 us (4%)
    ppermute x15, waiting for transfers between devices, swap(): return lax.ppermute(values, 'wide', [(d, d ^ mask) for d in range(count)])  18.9 us
    ppermute x15, starting transfers between devices, swap(): return lax.ppermute(values, 'wide', [(d, d ^ mask) for d in range(count)])  16 us
    pallas_call x8, Pallas kernels, left_call(): pl.pallas_call(behind(functools.partial(left_kernel, unit, base, span, of...  12.7 us
    pallas_call x2, Pallas kernels, triangle_call(): pl.pallas_call(behind(functools.partial(triangle_kernel, len(pairs), orde...  11.6 us
    pallas_call x4, Pallas kernels, edge_call(): pl.pallas_call(behind(functools.partial(edge_kernel, unit, offset, len(pa...  8.97 us
    ppermute x3, starting transfers between devices, cross(): return lax.ppermute(values, 'wide', pairs)  4.26 us
    unnamed x20, local copies, waits for them, and re-layouts  3.22 us
  transfers between devices with their start and end apart: 18, of which 6 were waited for; matrix products, arithmetic and copies ran while one was open for 0% of the time, Pallas kernels for 43%

profile of v6, /device:TPU:0, one launch (start us, length us, event | category | flops | bytes accessed | tf_op | source)
XLA Modules:
  0.0 77.4 jit_solution(2724223971671520943)
XLA Ops:
  0.0 1.9 %collective-permute-start.3 = (bf16[16,256,128]{2,1,0:T(8,128)(2,1)}, bf16[16,256,128]{2,1,0:T(8,128)(2,1)S(1)}, u32[]{:S(2)}, u32[]{:S(2)}) collective-permute-start(bf16[16,256,128]{2,1,0:T(8,128)(2,1)} %in_ref.1), channel_id=1, source_target_pairs={{0,0},{1,1},{2,2},{3,3},{4,8},{5,9},{6,10},{7,11},{8,4},{9,5},{10,... | collective-permute-start | bytes 3145736 | tf_op jit(solution)/shard_map/ppermute | solution.py:336
  3.2 4.7 %collective-permute-start = (bf16[8,256,128]{2,1,0:T(8,128)(2,1)S(1)}, bf16[8,256,128]{2,1,0:T(8,128)(2,1)S(1)}, u32[]{:S(2)}, u32[]{:S(2)}) collective-permute-start(bf16[8,256,128]{2,1,0:T(8,128)(2,1)S(1)} %get-tuple-element.31.refs_6_), channel_id=1, source_target_pairs={{0,4},{1,5},{2,6},{3,7},{4,0},{5,1},{6,2},{7,3},{8,12},{9,13},{10,... | collective-permute-start | bytes 1572872 | tf_op jit(solution)/shard_map/ppermute | solution.py:331
  7.9 1.5 %collective-permute-start.2 = (bf16[8,256,128]{2,1,0:T(8,128)(2,1)S(1)}, bf16[8,256,128]{2,1,0:T(8,128)(2,1)S(1)}, u32[]{:S(2)}, u32[]{:S(2)}) collective-permute-start(bf16[8,256,128]{2,1,0:T(8,128)(2,1)S(1)} %get-tuple-element.32.refs_7_), channel_id=1, source_target_pairs={{0,2},{1,3},{2,0},{3,1},{4,6},{5,7},{6,4},{7,5},{8,10},{9,11},{10,... | collective-permute-start | bytes 1572872 | tf_op jit(solution)/shard_map/ppermute | solution.py:331
  10.7 2.5 %edges.4.refs_1_.refs_0_.refs_5_ = bf16[128,16,256]{2,1,0:T(8,128)(2,1)S(1)} custom-call(s32[1]{0:T(128)} %bitcast.refs_0_.refs_1_.me_ref, s32[256]{0:T(256)S(1)} %copy-done.5, s32[1,256]{1,0:T(1,128)S(1)} %bitcast.3, f32[1,128]{1,0:T(1,128)S(1)} %bitcast.15, bf16[128,128]{1,0:T(8,128)(2,1)S(1)} %copy-done.3, bf16[128,128]{1,0:T(8,128)(2,1)S(1)} %copy-done.4, ...), custom_call_target="tpu_custom_call" | custom-call | flops 1048576 | bytes 1024 | tf_op jit(solution)/shard_map/edges/pallas_call | solution.py:221
  13.2 7.5 %collective-permute-done.refs_0_ = bf16[8,256,128]{2,1,0:T(8,128)(2,1)S(1)} collective-permute-done((bf16[8,256,128]{2,1,0:T(8,128)(2,1)S(1)}, bf16[8,256,128]{2,1,0:T(8,128)(2,1)S(1)}, u32[]{:S(2)}, u32[]{:S(2)}) %collective-permute-start) | collective-permute-done | bytes 524320 | tf_op jit(solution)/shard_map/ppermute | solution.py:331
  20.7 1.5 %collective-permute-start.7 = (bf16[8,256,128]{2,1,0:T(8,128)(2,1)S(1)}, bf16[8,256,128]{2,1,0:T(8,128)(2,1)S(1)}, u32[]{:S(2)}, u32[]{:S(2)}) collective-permute-start(bf16[8,256,128]{2,1,0:T(8,128)(2,1)S(1)} %hold.6.refs_7_), channel_id=1, source_target_pairs={{0,2},{1,3},{2,0},{3,1},{4,6},{5,7},{6,4},{7,5},{8,10},{9,11},{10,... | collective-permute-start | bytes 1572872 | tf_op jit(solution)/shard_map/ppermute | solution.py:331
  24.2 1.3 %left_edges.9 = (f32[1024,128]{1,0:T(8,128)S(1)}, f32[1024,128]{1,0:T(8,128)S(1)}) custom-call(f32[1024,128]{1,0:T(8,128)S(1)} %get-tuple-element.33.refs_0_.refs_8_, s32[1]{0:T(128)} %bitcast.refs_0_.refs_1_.me_ref, s32[256]{0:T(256)S(1)} %copy-done.5, s32[1,256]{1,0:T(1,128)S(1)} %bitcast.5, f32[1,128]{1,0:T(1,128)S(1)} %bitcast.17, ...), custom_call_target="tpu_custom_call" | custom-call | flops 1048576 | bytes 1024 | tf_op jit(solution)/shard_map/left_edges/pallas_call | solution.py:238
  26.4 2.4 %left_edges.10 = (f32[2048,128]{1,0:T(8,128)S(1)}, f32[2048,128]{1,0:T(8,128)S(1)}) custom-call(f32[1024,128]{1,0:T(8,128)S(1)} %get-tuple-element.34.refs_1_.refs_0_.refs_8_, s32[1]{0:T(128)} %bitcast.refs_0_.refs_1_.me_ref, s32[256]{0:T(256)S(1)} %copy-done.5, s32[1,256]{1,0:T(1,128)S(1)} %bitcast.6, f32[1,128]{1,0:T(1,128)S(1)} %bitcast.18, ...), custom_call_target="tpu_custom_call" | custom-call | flops 1048576 | bytes 1024 | tf_op jit(solution)/shard_map/left_edges/pallas_call | solution.py:238
  28.8 5.3 %collective-permute-done.4.refs_7_ = bf16[8,256,128]{2,1,0:T(8,128)(2,1)} collective-permute-done((bf16[8,256,128]{2,1,0:T(8,128)(2,1)S(1)}, bf16[8,256,128]{2,1,0:T(8,128)(2,1)}, u32[]{:S(2)}, u32[]{:S(2)}) %collective-permute-start.4) | collective-permute-done | bytes 524320 | tf_op jit(solution)/shard_map/ppermute | solution.py:331
  34.4 2.0 %edges.5.refs_1_.refs_0_.refs_8_ = bf16[128,16,256]{2,1,0:T(8,128)(2,1)S(1)} custom-call(f32[2048,128]{1,0:T(8,128)S(1)} %get-tuple-element.35.refs_0_.refs_13_, s32[1]{0:T(128)} %bitcast.refs_0_.refs_1_.me_ref, s32[256]{0:T(256)S(1)} %copy-done.5, s32[1,256]{1,0:T(1,128)S(1)} %bitcast.7, f32[1,128]{1,0:T(1,128)S(1)} %bitcast.19, ...), custom_call_target="tpu_custom_call" | custom-call | flops 1048576 | bytes 1024 | tf_op jit(solution)/shard_map/edges/pallas_call | solution.py:221
  36.4 2.0 %edges.6.refs_0_.refs_7_ = bf16[128,16,256]{2,1,0:T(8,128)(2,1)S(1)} custom-call(bf16[128,16,256]{2,1,0:T(8,128)(2,1)S(1)} %edges.5.refs_1_.refs_0_.refs_8_, s32[1]{0:T(128)} %bitcast.refs_0_.refs_1_.me_ref, s32[256]{0:T(256)S(1)} %copy-done.5, s32[1,256]{1,0:T(1,128)S(1)} %bitcast.8, f32[1,128]{1,0:T(1,128)S(1)} %bitcast.20, ...), custom_call_target="tpu_custom_call" | custom-call | flops 34359738368 | bytes 1024 | tf_op jit(solution)/shard_map/edges/pallas_call | solution.py:221
  38.4 2.4 %left_edges.11 = (f32[2048,128]{1,0:T(8,128)S(1)}, f32[2048,128]{1,0:T(8,128)S(1)}) custom-call(bf16[128,16,256]{2,1,0:T(8,128)(2,1)S(1)} %edges.6.refs_0_.refs_7_, s32[1]{0:T(128)} %bitcast.refs_0_.refs_1_.me_ref, s32[256]{0:T(256)S(1)} %copy-done.5, s32[1,256]{1,0:T(1,128)S(1)} %bitcast.9, f32[1,128]{1,0:T(1,128)S(1)} %bitcast.21, ...), custom_call_target="tpu_custom_call" | custom-call | flops 1048576 | bytes 1024 | tf_op jit(solution)/shard_map/left_edges/pallas_call | solution.py:238
  40.9 1.7 %collective-permute-start.13 = (bf16[8,256,128]{2,1,0:T(8,128)(2,1)}, bf16[8,256,128]{2,1,0:T(8,128)(2,1)S(1)}, u32[]{:S(2)}, u32[]{:S(2)}) collective-permute-start(bf16[8,256,128]{2,1,0:T(8,128)(2,1)} %hold.8.refs_7_), channel_id=1, source_target_pairs={{0,0},{1,1},{2,2},{3,3},{4,8},{5,9},{6,10},{7,11},{8,4},{9,5},{10,... | collective-permute-start | bytes 1572872 | tf_op jit(solution)/shard_map/ppermute | solution.py:336
  42.6 1.3 %left_edges.12 = (f32[1024,128]{1,0:T(8,128)S(1)}, f32[1024,128]{1,0:T(8,128)S(1)}) custom-call(s32[1]{0:T(128)} %bitcast.refs_0_.refs_1_.me_ref, s32[256]{0:T(256)S(1)} %copy-done.5, s32[1,256]{1,0:T(1,128)S(1)} %bitcast.10, f32[1,128]{1,0:T(1,128)S(1)} %bitcast.22, bf16[128,128]{1,0:T(8,128)(2,1)S(1)} %copy-done, bf16[128,128]{1,0:T(8,128)(2,1)S(1)} %copy-done.1, ...), custom_call_target="tpu_custom_call" | custom-call | flops 1048576 | bytes 1024 | tf_op jit(solution)/shard_map/left_edges/pallas_call | solution.py:238
  44.0 2.3 %collective-permute-done.8.refs_8_ = bf16[8,256,128]{2,1,0:T(8,128)(2,1)S(1)} collective-permute-done((bf16[8,256,128]{2,1,0:T(8,128)(2,1)S(1)}, bf16[8,256,128]{2,1,0:T(8,128)(2,1)S(1)}, u32[]{:S(2)}, u32[]{:S(2)}) %collective-permute-start.8) | collective-permute-done | bytes 524320 | tf_op jit(solution)/shard_map/ppermute | solution.py:331
  46.3 2.5 %edges.7.refs_0_.refs_6_ = bf16[128,16,256]{2,1,0:T(8,128)(2,1)S(1)} custom-call(f32[1024,128]{1,0:T(8,128)S(1)} %get-tuple-element.39.refs_0_.refs_17_, s32[1]{0:T(128)} %bitcast.refs_0_.refs_1_.me_ref, s32[256]{0:T(256)S(1)} %copy-done.5, s32[1,256]{1,0:T(1,128)S(1)} %bitcast.11, f32[1,128]{1,0:T(1,128)S(1)} %bitcast.23, bf16[128,128]{1,0:T(8,128)(2,1)S(1)} %copy-done.3, ...), custom_call_target="tpu_custom_call" | custom-call | flops 1048576 | bytes 1024 | tf_op jit(solution)/shard_map/edges/pallas_call | solution.py:221
  48.8 1.3 %left_edges.13 = (f32[1024,128]{1,0:T(8,128)S(1)}, f32[1024,128]{1,0:T(8,128)S(1)}) custom-call(bf16[128,16,256]{2,1,0:T(8,128)(2,1)S(1)} %edges.7.refs_0_.refs_6_, s32[1]{0:T(128)} %bitcast.refs_0_.refs_1_.me_ref, s32[256]{0:T(256)S(1)} %copy-done.5, s32[1,256]{1,0:T(1,128)S(1)} %bitcast.12, f32[1,128]{1,0:T(1,128)S(1)} %bitcast.24, ...), custom_call_target="tpu_custom_call" | custom-call | flops 1048576 | bytes 1024 | tf_op jit(solution)/shard_map/left_edges/pallas_call | solution.py:238
  50.8 7.4 %triangle.2 = (bf16[48,16,128]{2,1,0:T(8,128)(2,1)S(1)}, bf16[48,16,128]{2,1,0:T(8,128)(2,1)S(1)}, bf16[48,16,128]{2,1,0:T(8,128)(2,1)S(1)}, bf16[48,16,128]{2,1,0:T(8,128)(2,1)S(1)}) custom-call(s32[1]{0:T(128)} %bitcast.refs_0_.refs_1_.me_ref, f32[128]{0:T(128)S(1)} %copy-done.9, f32[1,128]{1,0:T(1,128)S(1)} %bitcast.25, bf16[128,128]{1,0:T(8,128)(2,1)S(1)} %copy-done.6, ...), custom_call_target="tpu_custom_call" | custom-call | flops 1048576 | bytes 1024 | tf_op jit(solution)/shard_map/triangle/pallas_call | solution.py:257
  58.4 2.8 %collective-permute-start.10 = (bf16[48,16,128]{2,1,0:T(8,128)(2,1)S(1)}, bf16[48,16,128]{2,1,0:T(8,128)(2,1)S(1)}, u32[]{:S(2)}, u32[]{:S(2)}) collective-permute-start(bf16[48,16,128]{2,1,0:T(8,128)(2,1)S(1)} %get-tuple-element.46), channel_id=1, source_target_pairs={{0,6},{1,7},{2,4},{3,5},{4,2},{5,3},{6,0},{7,1},{8,14},{9,15},{10,... | collective-permute-start | bytes 589832 | tf_op jit(solution)/shard_map/ppermute | solution.py:331
  61.9 1.3 %left_edges.14 = (f32[1024,128]{1,0:T(8,128)S(1)}, f32[1024,128]{1,0:T(8,128)S(1)}) custom-call(bf16[48,16,128]{2,1,0:T(8,128)(2,1)S(1)} %get-tuple-element.45.refs_1_.refs_0_.rest_0_, s32[1]{0:T(128)} %bitcast.refs_0_.refs_1_.me_ref, s32[256]{0:T(256)S(1)} %copy-done.5, s32[1,256]{1,0:T(1,128)S(1)} %bitcast.13, f32[1,128]{1,0:T(1,128)S(1)} %bitcast.26, ...), custom_call_target="tpu_custom_call" | custom-call | flops 1048576 | bytes 1024 | tf_op jit(solution)/shard_map/left_edges/pallas_call | solution.py:238
  63.3 1.3 %left_edges.15 = (f32[1024,128]{1,0:T(8,128)S(1)}, f32[1024,128]{1,0:T(8,128)S(1)}) custom-call(f32[1024,128]{1,0:T(8,128)S(1)} %get-tuple-element.49.refs_0_.refs_11_, s32[1]{0:T(128)} %bitcast.refs_0_.refs_1_.me_ref, s32[256]{0:T(256)S(1)} %copy-done.5, s32[1,256]{1,0:T(1,128)S(1)} %bitcast.14, f32[1,128]{1,0:T(1,128)S(1)} %bitcast.27, ...), custom_call_target="tpu_custom_call" | custom-call | flops 1048576 | bytes 1024 | tf_op jit(solution)/shard_map/left_edges/pallas_call | solution.py:238
  64.6 4.1 %triangle.3 = (bf16[16,16,128]{2,1,0:T(8,128)(2,1)S(1)}, bf16[16,16,128]{2,1,0:T(8,128)(2,1)S(1)}, bf16[16,16,128]{2,1,0:T(8,128)(2,1)S(1)}, bf16[16,16,128]{2,1,0:T(8,128)(2,1)S(1)}) custom-call(s32[1]{0:T(128)} %bitcast.refs_0_.refs_1_.me_ref, f32[128]{0:T(128)S(1)} %copy-done.9, f32[1,128]{1,0:T(1,128)S(1)} %bitcast.28, bf16[128,128]{1,0:T(8,128)(2,1)S(1)} %copy-done.6, ...), custom_call_target="tpu_custom_call" | custom-call | flops 1048576 | bytes 1024 | tf_op jit(solution)/shard_map/triangle/pallas_call | solution.py:257
  68.7 2.8 %collective-permute-start.15 = (bf16[16,16,128]{2,1,0:T(8,128)(2,1)S(1)}, bf16[16,16,128]{2,1,0:T(8,128)(2,1)S(1)}, u32[]{:S(2)}, u32[]{:S(2)}) collective-permute-start(bf16[16,16,128]{2,1,0:T(8,128)(2,1)S(1)} %get-tuple-element.54), channel_id=1, source_target_pairs={{0,6},{1,7},{2,4},{3,5},{4,2},{5,3},{6,0},{7,1},{8,14},{9,15},{10,... | collective-permute-start | bytes 196616 | tf_op jit(solution)/shard_map/ppermute | solution.py:331
  72.3 2.3 %collective-permute-done.15.rest_5_ = bf16[16,16,128]{2,1,0:T(8,128)(2,1)S(1)} collective-permute-done((bf16[16,16,128]{2,1,0:T(8,128)(2,1)S(1)}, bf16[16,16,128]{2,1,0:T(8,128)(2,1)S(1)}, u32[]{:S(2)}, u32[]{:S(2)}) %collective-permute-start.15) | collective-permute-done | bytes 65568 | tf_op jit(solution)/shard_map/ppermute | solution.py:331
  (54 shorter events, 10.7 us)
Async XLA Ops:
  0.0 25.6 %collective-permute-start.3 = (bf16[16,256,128]{2,1,0:T(8,128)(2,1)}, bf16[16,256,128]{2,1,0:T(8,128)(2,1)S(1)}, u32[]{:S(2)}, u32[]{:S(2)}) collective-permute-start(bf16[16,256,128]{2,1,0:T(8,128)(2,1)} %in_ref.1), channel_id=1, source_target_pairs={{0,0},{1,1},{2,2},{3,3},{4,8},{5,9},{6,10},{7,11},{8,4},{9,5},{10,... | collective-permute-start | bytes 3145736 | tf_op jit(solution)/shard_map/ppermute | solution.py:336
  1.9 1.2 %copy-start.2 = (bf16[16,256,128]{2,1,0:T(8,128)(2,1)S(1)}, bf16[16,256,128]{2,1,0:T(8,128)(2,1)}, u32[]{:S(2)}) copy-start(bf16[16,256,128]{2,1,0:T(8,128)(2,1)} %in_ref.1) | copy-start | bytes 3145732
  3.1 6.9 %copy-start.3 = (bf16[128,128]{1,0:T(8,128)(2,1)S(1)}, bf16[128,128]{1,0:T(8,128)(2,1)}, u32[]{:S(2)}) copy-start(bf16[128,128]{1,0:T(8,128)(2,1)} %refs_5_.20) | copy-start | bytes 98308
  3.1 6.9 %copy-start.4 = (bf16[128,128]{1,0:T(8,128)(2,1)S(1)}, bf16[128,128]{1,0:T(8,128)(2,1)}, u32[]{:S(2)}) copy-start(bf16[128,128]{1,0:T(8,128)(2,1)} %refs_6_.16) | copy-start | bytes 98308
  3.2 17.5 %collective-permute-start = (bf16[8,256,128]{2,1,0:T(8,128)(2,1)S(1)}, bf16[8,256,128]{2,1,0:T(8,128)(2,1)S(1)}, u32[]{:S(2)}, u32[]{:S(2)}) collective-permute-start(bf16[8,256,128]{2,1,0:T(8,128)(2,1)S(1)} %get-tuple-element.31.refs_6_), channel_id=1, source_target_pairs={{0,4},{1,5},{2,6},{3,7},{4,0},{5,1},{6,2},{7,3},{8,12},{9,13},{10,... | collective-permute-start | bytes 1572872 | tf_op jit(solution)/shard_map/ppermute | solution.py:331
  7.9 15.6 %collective-permute-start.2 = (bf16[8,256,128]{2,1,0:T(8,128)(2,1)S(1)}, bf16[8,256,128]{2,1,0:T(8,128)(2,1)S(1)}, u32[]{:S(2)}, u32[]{:S(2)}) collective-permute-start(bf16[8,256,128]{2,1,0:T(8,128)(2,1)S(1)} %get-tuple-element.32.refs_7_), channel_id=1, source_target_pairs={{0,2},{1,3},{2,0},{3,1},{4,6},{5,7},{6,4},{7,5},{8,10},{9,11},{10,... | collective-permute-start | bytes 1572872 | tf_op jit(solution)/shard_map/ppermute | solution.py:331
  9.4 24.7 %collective-permute-start.4 = (bf16[8,256,128]{2,1,0:T(8,128)(2,1)S(1)}, bf16[8,256,128]{2,1,0:T(8,128)(2,1)}, u32[]{:S(2)}, u32[]{:S(2)}) collective-permute-start(bf16[8,256,128]{2,1,0:T(8,128)(2,1)S(1)} %get-tuple-element.31.refs_6_), channel_id=1, source_target_pairs={{0,2},{1,3},{2,0},{3,1},{4,6},{5,7},{6,4},{7,5},{8,10},{9,11},{10,... | collective-permute-start | bytes 1572872 | tf_op jit(solution)/shard_map/ppermute | solution.py:331
  9.9 26.5 %collective-permute-start.5 = (bf16[8,256,128]{2,1,0:T(8,128)(2,1)S(1)}, bf16[8,256,128]{2,1,0:T(8,128)(2,1)}, u32[]{:S(2)}, u32[]{:S(2)}) collective-permute-start(bf16[8,256,128]{2,1,0:T(8,128)(2,1)S(1)} %get-tuple-element.32.refs_7_), channel_id=1, source_target_pairs={{0,4},{1,5},{2,6},{3,7},{4,0},{5,1},{6,2},{7,3},{8,12},{9,13},{10,... | collective-permute-start | bytes 1572872 | tf_op jit(solution)/shard_map/ppermute | solution.py:331
  20.7 23.3 %collective-permute-start.7 = (bf16[8,256,128]{2,1,0:T(8,128)(2,1)S(1)}, bf16[8,256,128]{2,1,0:T(8,128)(2,1)S(1)}, u32[]{:S(2)}, u32[]{:S(2)}) collective-permute-start(bf16[8,256,128]{2,1,0:T(8,128)(2,1)S(1)} %hold.6.refs_7_), channel_id=1, source_target_pairs={{0,2},{1,3},{2,0},{3,1},{4,6},{5,7},{6,4},{7,5},{8,10},{9,11},{10,... | collective-permute-start | bytes 1572872 | tf_op jit(solution)/shard_map/ppermute | solution.py:331
  23.5 17.3 %collective-permute-start.1 = (bf16[8,256,128]{2,1,0:T(8,128)(2,1)S(1)}, bf16[8,256,128]{2,1,0:T(8,128)(2,1)S(1)}, u32[]{:S(2)}, u32[]{:S(2)}) collective-permute-start(bf16[8,256,128]{2,1,0:T(8,128)(2,1)S(1)} %hold.6.refs_7_), channel_id=1, source_target_pairs={{0,0},{1,1},{2,2},{3,3},{4,8},{5,9},{6,10},{7,11},{8,4},{9,5},{10,... | collective-permute-start | bytes 1572872 | tf_op jit(solution)/shard_map/ppermute | solution.py:336
  25.6 0.8 copy-start.1
  25.6 12.8 %collective-permute-start.6 = (bf16[16,256,128]{2,1,0:T(8,128)(2,1)S(1)}, bf16[16,256,128]{2,1,0:T(8,128)(2,1)S(1)}, u32[]{:S(2)}, u32[]{:S(2)}) collective-permute-start(bf16[16,256,128]{2,1,0:T(8,128)(2,1)S(1)} %hold.7.refs_7_.refs_1_.refs_9_), channel_id=1, source_target_pairs={{0,1},{1,0},{2,3},{3,2},{4,5},{5,4},{6,7},{7,6},{8,9},{9,8},{10,11... | collective-permute-start | bytes 3145736 | tf_op jit(solution)/shard_map/ppermute | solution.py:331
  34.1 12.2 %collective-permute-start.8 = (bf16[8,256,128]{2,1,0:T(8,128)(2,1)S(1)}, bf16[8,256,128]{2,1,0:T(8,128)(2,1)S(1)}, u32[]{:S(2)}, u32[]{:S(2)}) collective-permute-start(bf16[8,256,128]{2,1,0:T(8,128)(2,1)S(1)} %hold.10), channel_id=1, source_target_pairs={{0,4},{1,5},{2,6},{3,7},{4,0},{5,1},{6,2},{7,3},{8,12},{9,13},{10,... | collective-permute-start | bytes 1572872 | tf_op jit(solution)/shard_map/ppermute | solution.py:331
  40.9 8.0 %collective-permute-start.9 = (bf16[8,256,128]{2,1,0:T(8,128)(2,1)S(1)}, bf16[8,256,128]{2,1,0:T(8,128)(2,1)S(1)}, u32[]{:S(2)}, u32[]{:S(2)}) collective-permute-start(bf16[8,256,128]{2,1,0:T(8,128)(2,1)S(1)} %hold.9.refs_6_.refs_11_), channel_id=1, source_target_pairs={{0,1},{1,0},{2,3},{3,2},{4,5},{5,4},{6,7},{7,6},{8,9},{9,8},{10,11... | collective-permute-start | bytes 1572872 | tf_op jit(solution)/shard_map/ppermute | solution.py:331
  40.9 17.3 %collective-permute-start.13 = (bf16[8,256,128]{2,1,0:T(8,128)(2,1)}, bf16[8,256,128]{2,1,0:T(8,128)(2,1)S(1)}, u32[]{:S(2)}, u32[]{:S(2)}) collective-permute-start(bf16[8,256,128]{2,1,0:T(8,128)(2,1)} %hold.8.refs_7_), channel_id=1, source_target_pairs={{0,0},{1,1},{2,2},{3,3},{4,8},{5,9},{6,10},{7,11},{8,4},{9,5},{10,... | collective-permute-start | bytes 1572872 | tf_op jit(solution)/shard_map/ppermute | solution.py:336
  48.8 1.4 %copy-start.6 = (bf16[128,128]{1,0:T(8,128)(2,1)S(1)}, bf16[128,128]{1,0:T(8,128)(2,1)}, u32[]{:S(2)}) copy-start(bf16[128,128]{1,0:T(8,128)(2,1)} %refs_3_.3) | copy-start | bytes 98308
  48.8 1.4 %copy-start.7 = (bf16[128,128]{1,0:T(8,128)(2,1)S(1)}, bf16[128,128]{1,0:T(8,128)(2,1)}, u32[]{:S(2)}) copy-start(bf16[128,128]{1,0:T(8,128)(2,1)} %refs_4_.7) | copy-start | bytes 98308
  58.3 5.0 %collective-permute-start.14 = (bf16[8,256,128]{2,1,0:T(8,128)(2,1)S(1)}, bf16[8,256,128]{2,1,0:T(8,128)(2,1)S(1)}, u32[]{:S(2)}, u32[]{:S(2)}) collective-permute-start(bf16[8,256,128]{2,1,0:T(8,128)(2,1)S(1)} %hold.11.refs_7_.refs_9_), channel_id=1, source_target_pairs={{0,1},{1,0},{2,3},{3,2},{4,5},{5,4},{6,7},{7,6},{8,9},{9,8},{10,11... | collective-permute-start | bytes 1572872 | tf_op jit(solution)/shard_map/ppermute | solution.py:331
  58.4 13.4 %collective-permute-start.10 = (bf16[48,16,128]{2,1,0:T(8,128)(2,1)S(1)}, bf16[48,16,128]{2,1,0:T(8,128)(2,1)S(1)}, u32[]{:S(2)}, u32[]{:S(2)}) collective-permute-start(bf16[48,16,128]{2,1,0:T(8,128)(2,1)S(1)} %get-tuple-element.46), channel_id=1, source_target_pairs={{0,6},{1,7},{2,4},{3,5},{4,2},{5,3},{6,0},{7,1},{8,14},{9,15},{10,... | collective-permute-start | bytes 589832 | tf_op jit(solution)/shard_map/ppermute | solution.py:331
  61.1 11.2 %collective-permute-start.11 = (bf16[48,16,128]{2,1,0:T(8,128)(2,1)S(1)}, bf16[48,16,128]{2,1,0:T(8,128)(2,1)S(1)}, u32[]{:S(2)}, u32[]{:S(2)}) collective-permute-start(bf16[48,16,128]{2,1,0:T(8,128)(2,1)S(1)} %get-tuple-element.47), channel_id=1, source_target_pairs={{0,4},{1,5},{2,6},{3,7},{4,0},{5,1},{6,2},{7,3},{8,12},{9,13},{10,... | collective-permute-start | bytes 589832 | tf_op jit(solution)/shard_map/ppermute | solution.py:331
  61.4 10.9 %collective-permute-start.12 = (bf16[48,16,128]{2,1,0:T(8,128)(2,1)S(1)}, bf16[48,16,128]{2,1,0:T(8,128)(2,1)S(1)}, u32[]{:S(2)}, u32[]{:S(2)}) collective-permute-start(bf16[48,16,128]{2,1,0:T(8,128)(2,1)S(1)} %get-tuple-element.48), channel_id=1, source_target_pairs={{0,2},{1,3},{2,0},{3,1},{4,6},{5,7},{6,4},{7,5},{8,10},{9,11},{10,... | collective-permute-start | bytes 589832 | tf_op jit(solution)/shard_map/ppermute | solution.py:331
  68.7 5.8 %collective-permute-start.15 = (bf16[16,16,128]{2,1,0:T(8,128)(2,1)S(1)}, bf16[16,16,128]{2,1,0:T(8,128)(2,1)S(1)}, u32[]{:S(2)}, u32[]{:S(2)}) collective-permute-start(bf16[16,16,128]{2,1,0:T(8,128)(2,1)S(1)} %get-tuple-element.54), channel_id=1, source_target_pairs={{0,6},{1,7},{2,4},{3,5},{4,2},{5,3},{6,0},{7,1},{8,14},{9,15},{10,... | collective-permute-start | bytes 196616 | tf_op jit(solution)/shard_map/ppermute | solution.py:331
  71.5 4.3 %collective-permute-start.16 = (bf16[16,16,128]{2,1,0:T(8,128)(2,1)S(1)}, bf16[16,16,128]{2,1,0:T(8,128)(2,1)S(1)}, u32[]{:S(2)}, u32[]{:S(2)}) collective-permute-start(bf16[16,16,128]{2,1,0:T(8,128)(2,1)S(1)} %get-tuple-element.55), channel_id=1, source_target_pairs={{0,4},{1,5},{2,6},{3,7},{4,0},{5,1},{6,2},{7,3},{8,12},{9,13},{10,... | collective-permute-start | bytes 196616 | tf_op jit(solution)/shard_map/ppermute | solution.py:331
  71.8 4.3 %collective-permute-start.17 = (bf16[16,16,128]{2,1,0:T(8,128)(2,1)S(1)}, bf16[16,16,128]{2,1,0:T(8,128)(2,1)S(1)}, u32[]{:S(2)}, u32[]{:S(2)}) collective-permute-start(bf16[16,16,128]{2,1,0:T(8,128)(2,1)S(1)} %get-tuple-element.56), channel_id=1, source_target_pairs={{0,2},{1,3},{2,0},{3,1},{4,6},{5,7},{6,4},{7,5},{8,10},{9,11},{10,... | collective-permute-start | bytes 196616 | tf_op jit(solution)/shard_map/ppermute | solution.py:331
  (4 other events, 2.8 us)

commit v7 on v6

--- a/solution.py
+++ b/solution.py
@@ -408,7 +408,7 @@
         both = {low_bit: side}
         for bit in side_bits:
             for unit in [unit ^ low_bit for unit in both]:
-                across = hold(plain[unit ^ bit][0], first)
+                across = hold(plain[unit ^ bit][0], plain_ready[unit ^ bit][0])
                 there = [swap(both[unit ^ low_bit][0], bit), swap(across, low_bit)]
                 both[unit ^ bit ^ low_bit] = there
         second = [cross(piece) for piece in side]

time: 77.8 us -> 75.9 us (0.976)
  waiting for transfers between devices: 18.9 us -> 11.7 us
  starting transfers between devices: 20.2 us -> 26.3 us
    ppermute x15, waiting for transfers between devices: 18.9 us -> 11.7 us  [swap(): return lax.ppermute(values, 'wide', [(d, d ^ mask) for d in range(count)])]
    ppermute x15, starting transfers between devices: 16 us -> 22 us  [swap(): return lax.ppermute(values, 'wide', [(d, d ^ mask) for d in range(count)])]
  transfers between devices with their start and end apart: 18 -> 18, of which waited for: 6 -> 4; matrix products, arithmetic and copies ran while one was open for 0% -> 0% of each run, Pallas kernels for 43% -> 44%
where the time goes in v7:
time: 75.9 us; the launch traced here: 75.5 us
  Pallas kernels  34.5 us (45%)
  starting transfers between devices  26.3 us (35%)
  waiting for transfers between devices  11.7 us (15%)
  local copies, waits for them, and re-layouts  2.56 us (3%)
    ppermute x15, starting transfers between devices, swap(): return lax.ppermute(values, 'wide', [(d, d ^ mask) for d in range(count)])  22 us
    pallas_call x8, Pallas kernels, left_call(): pl.pallas_call(behind(functools.partial(left_kernel, unit, base, span, of...  12.7 us
    ppermute x15, waiting for transfers between devices, swap(): return lax.ppermute(values, 'wide', [(d, d ^ mask) for d in range(count)])  11.7 us
    pallas_call x2, Pallas kernels, triangle_call(): pl.pallas_call(behind(functools.partial(triangle_kernel, len(pairs), orde...  11.6 us
    pallas_call x4, Pallas kernels, edge_call(): pl.pallas_call(behind(functools.partial(edge_kernel, unit, offset, len(pa...  8.98 us
    ppermute x3, starting transfers between devices, cross(): return lax.ppermute(values, 'wide', pairs)  4.25 us
    unnamed x20, local copies, waits for them, and re-layouts  2.56 us
  transfers between devices with their start and end apart: 18, of which 4 were waited for; matrix products, arithmetic and copies ran while one was open for 0% of the time, Pallas kernels for 44%

profile of v7, /device:TPU:0, one launch (start us, length us, event | category | flops | bytes accessed | tf_op | source)
XLA Modules:
  0.0 75.5 jit_solution(9543854135504817472)
XLA Ops:
  0.0 1.9 %collective-permute-start.3 = (bf16[16,256,128]{2,1,0:T(8,128)(2,1)}, bf16[16,256,128]{2,1,0:T(8,128)(2,1)S(1)}, u32[]{:S(2)}, u32[]{:S(2)}) collective-permute-start(bf16[16,256,128]{2,1,0:T(8,128)(2,1)} %in_ref.1), channel_id=1, source_target_pairs={{0,0},{1,1},{2,2},{3,3},{4,8},{5,9},{6,10},{7,11},{8,4},{9,5},{10,... | collective-permute-start | bytes 3145736 | tf_op jit(solution)/shard_map/ppermute | solution.py:336
  3.2 4.7 %collective-permute-start = (bf16[8,256,128]{2,1,0:T(8,128)(2,1)S(1)}, bf16[8,256,128]{2,1,0:T(8,128)(2,1)S(1)}, u32[]{:S(2)}, u32[]{:S(2)}) collective-permute-start(bf16[8,256,128]{2,1,0:T(8,128)(2,1)S(1)} %get-tuple-element.31.refs_6_), channel_id=1, source_target_pairs={{0,4},{1,5},{2,6},{3,7},{4,0},{5,1},{6,2},{7,3},{8,12},{9,13},{10,... | collective-permute-start | bytes 1572872 | tf_op jit(solution)/shard_map/ppermute | solution.py:331
  7.9 1.5 %collective-permute-start.2 = (bf16[8,256,128]{2,1,0:T(8,128)(2,1)S(1)}, bf16[8,256,128]{2,1,0:T(8,128)(2,1)S(1)}, u32[]{:S(2)}, u32[]{:S(2)}) collective-permute-start(bf16[8,256,128]{2,1,0:T(8,128)(2,1)S(1)} %get-tuple-element.32.refs_7_), channel_id=1, source_target_pairs={{0,2},{1,3},{2,0},{3,1},{4,6},{5,7},{6,4},{7,5},{8,10},{9,11},{10,... | collective-permute-start | bytes 1572872 | tf_op jit(solution)/shard_map/ppermute | solution.py:331
  10.7 2.5 %edges.4.refs_1_.refs_0_.refs_5_ = bf16[128,16,256]{2,1,0:T(8,128)(2,1)S(1)} custom-call(s32[1]{0:T(128)} %bitcast.refs_0_.refs_1_.me_ref, s32[256]{0:T(256)S(1)} %copy-done.5, s32[1,256]{1,0:T(1,128)S(1)} %bitcast.3, f32[1,128]{1,0:T(1,128)S(1)} %bitcast.15, bf16[128,128]{1,0:T(8,128)(2,1)S(1)} %copy-done.3, bf16[128,128]{1,0:T(8,128)(2,1)S(1)} %copy-done.4, ...), custom_call_target="tpu_custom_call" | custom-call | flops 1048576 | bytes 1024 | tf_op jit(solution)/shard_map/edges/pallas_call | solution.py:221
  13.2 7.5 %collective-permute-done.refs_0_ = bf16[8,256,128]{2,1,0:T(8,128)(2,1)S(1)} collective-permute-done((bf16[8,256,128]{2,1,0:T(8,128)(2,1)S(1)}, bf16[8,256,128]{2,1,0:T(8,128)(2,1)S(1)}, u32[]{:S(2)}, u32[]{:S(2)}) %collective-permute-start) | collective-permute-done | bytes 524320 | tf_op jit(solution)/shard_map/ppermute | solution.py:331
  20.7 1.5 %collective-permute-start.7 = (bf16[8,256,128]{2,1,0:T(8,128)(2,1)S(1)}, bf16[8,256,128]{2,1,0:T(8,128)(2,1)S(1)}, u32[]{:S(2)}, u32[]{:S(2)}) collective-permute-start(bf16[8,256,128]{2,1,0:T(8,128)(2,1)S(1)} %hold.6.refs_7_), channel_id=1, source_target_pairs={{0,2},{1,3},{2,0},{3,1},{4,6},{5,7},{6,4},{7,5},{8,10},{9,11},{10,... | collective-permute-start | bytes 1572872 | tf_op jit(solution)/shard_map/ppermute | solution.py:331
  24.2 1.3 %left_edges.9 = (f32[1024,128]{1,0:T(8,128)S(1)}, f32[1024,128]{1,0:T(8,128)S(1)}) custom-call(f32[1024,128]{1,0:T(8,128)S(1)} %get-tuple-element.33.refs_0_.refs_8_, s32[1]{0:T(128)} %bitcast.refs_0_.refs_1_.me_ref, s32[256]{0:T(256)S(1)} %copy-done.5, s32[1,256]{1,0:T(1,128)S(1)} %bitcast.5, f32[1,128]{1,0:T(1,128)S(1)} %bitcast.17, ...), custom_call_target="tpu_custom_call" | custom-call | flops 1048576 | bytes 1024 | tf_op jit(solution)/shard_map/left_edges/pallas_call | solution.py:238
  25.6 5.5 %collective-permute-start.8 = (bf16[8,256,128]{2,1,0:T(8,128)(2,1)S(1)}, bf16[8,256,128]{2,1,0:T(8,128)(2,1)S(1)}, u32[]{:S(2)}, u32[]{:S(2)}) collective-permute-start(bf16[8,256,128]{2,1,0:T(8,128)(2,1)S(1)} %hold.10), channel_id=1, source_target_pairs={{0,4},{1,5},{2,6},{3,7},{4,0},{5,1},{6,2},{7,3},{8,12},{9,13},{10,... | collective-permute-start | bytes 1572872 | tf_op jit(solution)/shard_map/ppermute | solution.py:331
  31.2 2.4 %left_edges.10 = (f32[2048,128]{1,0:T(8,128)S(1)}, f32[2048,128]{1,0:T(8,128)S(1)}) custom-call(f32[1024,128]{1,0:T(8,128)S(1)} %get-tuple-element.34.refs_1_.refs_0_.refs_8_, s32[1]{0:T(128)} %bitcast.refs_0_.refs_1_.me_ref, s32[256]{0:T(256)S(1)} %copy-done.5, s32[1,256]{1,0:T(1,128)S(1)} %bitcast.6, f32[1,128]{1,0:T(1,128)S(1)} %bitcast.18, ...), custom_call_target="tpu_custom_call" | custom-call | flops 1048576 | bytes 1024 | tf_op jit(solution)/shard_map/left_edges/pallas_call | solution.py:238
  34.1 1.9 %edges.5.refs_1_.refs_0_.refs_8_ = bf16[128,16,256]{2,1,0:T(8,128)(2,1)S(1)} custom-call(f32[2048,128]{1,0:T(8,128)S(1)} %get-tuple-element.35.refs_0_.refs_13_, s32[1]{0:T(128)} %bitcast.refs_0_.refs_1_.me_ref, s32[256]{0:T(256)S(1)} %copy-done.5, s32[1,256]{1,0:T(1,128)S(1)} %bitcast.7, f32[1,128]{1,0:T(1,128)S(1)} %bitcast.19, ...), custom_call_target="tpu_custom_call" | custom-call | flops 1048576 | bytes 1024 | tf_op jit(solution)/shard_map/edges/pallas_call | solution.py:221
  36.1 2.0 %edges.6.refs_0_.refs_7_ = bf16[128,16,256]{2,1,0:T(8,128)(2,1)S(1)} custom-call(bf16[128,16,256]{2,1,0:T(8,128)(2,1)S(1)} %edges.5.refs_1_.refs_0_.refs_8_, s32[1]{0:T(128)} %bitcast.refs_0_.refs_1_.me_ref, s32[256]{0:T(256)S(1)} %copy-done.5, s32[1,256]{1,0:T(1,128)S(1)} %bitcast.8, f32[1,128]{1,0:T(1,128)S(1)} %bitcast.20, ...), custom_call_target="tpu_custom_call" | custom-call | flops 34359738368 | bytes 1024 | tf_op jit(solution)/shard_map/edges/pallas_call | solution.py:221
  38.1 2.4 %left_edges.11 = (f32[2048,128]{1,0:T(8,128)S(1)}, f32[2048,128]{1,0:T(8,128)S(1)}) custom-call(bf16[128,16,256]{2,1,0:T(8,128)(2,1)S(1)} %edges.6.refs_0_.refs_7_, s32[1]{0:T(128)} %bitcast.refs_0_.refs_1_.me_ref, s32[256]{0:T(256)S(1)} %copy-done.5, s32[1,256]{1,0:T(1,128)S(1)} %bitcast.9, f32[1,128]{1,0:T(1,128)S(1)} %bitcast.21, ...), custom_call_target="tpu_custom_call" | custom-call | flops 1048576 | bytes 1024 | tf_op jit(solution)/shard_map/left_edges/pallas_call | solution.py:238
  41.1 1.7 %collective-permute-start.13 = (bf16[8,256,128]{2,1,0:T(8,128)(2,1)}, bf16[8,256,128]{2,1,0:T(8,128)(2,1)S(1)}, u32[]{:S(2)}, u32[]{:S(2)}) collective-permute-start(bf16[8,256,128]{2,1,0:T(8,128)(2,1)} %hold.8.refs_7_), channel_id=1, source_target_pairs={{0,0},{1,1},{2,2},{3,3},{4,8},{5,9},{6,10},{7,11},{8,4},{9,5},{10,... | collective-permute-start | bytes 1572872 | tf_op jit(solution)/shard_map/ppermute | solution.py:336
  42.8 1.3 %left_edges.12 = (f32[1024,128]{1,0:T(8,128)S(1)}, f32[1024,128]{1,0:T(8,128)S(1)}) custom-call(s32[1]{0:T(128)} %bitcast.refs_0_.refs_1_.me_ref, s32[256]{0:T(256)S(1)} %copy-done.5, s32[1,256]{1,0:T(1,128)S(1)} %bitcast.10, f32[1,128]{1,0:T(1,128)S(1)} %bitcast.22, bf16[128,128]{1,0:T(8,128)(2,1)S(1)} %copy-done, bf16[128,128]{1,0:T(8,128)(2,1)S(1)} %copy-done.1, ...), custom_call_target="tpu_custom_call" | custom-call | flops 1048576 | bytes 1024 | tf_op jit(solution)/shard_map/left_edges/pallas_call | solution.py:238
  44.2 2.5 %edges.7.refs_0_.refs_6_ = bf16[128,16,256]{2,1,0:T(8,128)(2,1)S(1)} custom-call(f32[1024,128]{1,0:T(8,128)S(1)} %get-tuple-element.39.refs_0_.refs_17_, s32[1]{0:T(128)} %bitcast.refs_0_.refs_1_.me_ref, s32[256]{0:T(256)S(1)} %copy-done.5, s32[1,256]{1,0:T(1,128)S(1)} %bitcast.11, f32[1,128]{1,0:T(1,128)S(1)} %bitcast.23, bf16[128,128]{1,0:T(8,128)(2,1)S(1)} %copy-done.3, ...), custom_call_target="tpu_custom_call" | custom-call | flops 1048576 | bytes 1024 | tf_op jit(solution)/shard_map/edges/pallas_call | solution.py:221
  46.7 1.3 %left_edges.13 = (f32[1024,128]{1,0:T(8,128)S(1)}, f32[1024,128]{1,0:T(8,128)S(1)}) custom-call(bf16[128,16,256]{2,1,0:T(8,128)(2,1)S(1)} %edges.7.refs_0_.refs_6_, s32[1]{0:T(128)} %bitcast.refs_0_.refs_1_.me_ref, s32[256]{0:T(256)S(1)} %copy-done.5, s32[1,256]{1,0:T(1,128)S(1)} %bitcast.12, f32[1,128]{1,0:T(1,128)S(1)} %bitcast.24, ...), custom_call_target="tpu_custom_call" | custom-call | flops 1048576 | bytes 1024 | tf_op jit(solution)/shard_map/left_edges/pallas_call | solution.py:238
  48.7 7.4 %triangle.2 = (bf16[48,16,128]{2,1,0:T(8,128)(2,1)S(1)}, bf16[48,16,128]{2,1,0:T(8,128)(2,1)S(1)}, bf16[48,16,128]{2,1,0:T(8,128)(2,1)S(1)}, bf16[48,16,128]{2,1,0:T(8,128)(2,1)S(1)}) custom-call(s32[1]{0:T(128)} %bitcast.refs_0_.refs_1_.me_ref, f32[128]{0:T(128)S(1)} %copy-done.9, f32[1,128]{1,0:T(1,128)S(1)} %bitcast.25, bf16[128,128]{1,0:T(8,128)(2,1)S(1)} %copy-done.6, ...), custom_call_target="tpu_custom_call" | custom-call | flops 1048576 | bytes 1024 | tf_op jit(solution)/shard_map/triangle/pallas_call | solution.py:257
  56.3 3.2 %collective-permute-start.10 = (bf16[48,16,128]{2,1,0:T(8,128)(2,1)S(1)}, bf16[48,16,128]{2,1,0:T(8,128)(2,1)S(1)}, u32[]{:S(2)}, u32[]{:S(2)}) collective-permute-start(bf16[48,16,128]{2,1,0:T(8,128)(2,1)S(1)} %get-tuple-element.46), channel_id=1, source_target_pairs={{0,6},{1,7},{2,4},{3,5},{4,2},{5,3},{6,0},{7,1},{8,14},{9,15},{10,... | collective-permute-start | bytes 589832 | tf_op jit(solution)/shard_map/ppermute | solution.py:331
  60.1 1.3 %left_edges.14 = (f32[1024,128]{1,0:T(8,128)S(1)}, f32[1024,128]{1,0:T(8,128)S(1)}) custom-call(bf16[48,16,128]{2,1,0:T(8,128)(2,1)S(1)} %get-tuple-element.45.refs_1_.refs_0_.rest_0_, s32[1]{0:T(128)} %bitcast.refs_0_.refs_1_.me_ref, s32[256]{0:T(256)S(1)} %copy-done.5, s32[1,256]{1,0:T(1,128)S(1)} %bitcast.13, f32[1,128]{1,0:T(1,128)S(1)} %bitcast.26, ...), custom_call_target="tpu_custom_call" | custom-call | flops 1048576 | bytes 1024 | tf_op jit(solution)/shard_map/left_edges/pallas_call | solution.py:238
  61.4 1.3 %left_edges.15 = (f32[1024,128]{1,0:T(8,128)S(1)}, f32[1024,128]{1,0:T(8,128)S(1)}) custom-call(f32[1024,128]{1,0:T(8,128)S(1)} %get-tuple-element.49.refs_0_.refs_11_, s32[1]{0:T(128)} %bitcast.refs_0_.refs_1_.me_ref, s32[256]{0:T(256)S(1)} %copy-done.5, s32[1,256]{1,0:T(1,128)S(1)} %bitcast.14, f32[1,128]{1,0:T(1,128)S(1)} %bitcast.27, ...), custom_call_target="tpu_custom_call" | custom-call | flops 1048576 | bytes 1024 | tf_op jit(solution)/shard_map/left_edges/pallas_call | solution.py:238
  62.8 4.1 %triangle.3 = (bf16[16,16,128]{2,1,0:T(8,128)(2,1)S(1)}, bf16[16,16,128]{2,1,0:T(8,128)(2,1)S(1)}, bf16[16,16,128]{2,1,0:T(8,128)(2,1)S(1)}, bf16[16,16,128]{2,1,0:T(8,128)(2,1)S(1)}) custom-call(s32[1]{0:T(128)} %bitcast.refs_0_.refs_1_.me_ref, f32[128]{0:T(128)S(1)} %copy-done.9, f32[1,128]{1,0:T(1,128)S(1)} %bitcast.28, bf16[128,128]{1,0:T(8,128)(2,1)S(1)} %copy-done.6, ...), custom_call_target="tpu_custom_call" | custom-call | flops 1048576 | bytes 1024 | tf_op jit(solution)/shard_map/triangle/pallas_call | solution.py:257
  66.9 3.0 %collective-permute-start.15 = (bf16[16,16,128]{2,1,0:T(8,128)(2,1)S(1)}, bf16[16,16,128]{2,1,0:T(8,128)(2,1)S(1)}, u32[]{:S(2)}, u32[]{:S(2)}) collective-permute-start(bf16[16,16,128]{2,1,0:T(8,128)(2,1)S(1)} %get-tuple-element.54), channel_id=1, source_target_pairs={{0,6},{1,7},{2,4},{3,5},{4,2},{5,3},{6,0},{7,1},{8,14},{9,15},{10,... | collective-permute-start | bytes 196616 | tf_op jit(solution)/shard_map/ppermute | solution.py:331
  70.5 2.1 %collective-permute-done.15.rest_5_ = bf16[16,16,128]{2,1,0:T(8,128)(2,1)S(1)} collective-permute-done((bf16[16,16,128]{2,1,0:T(8,128)(2,1)S(1)}, bf16[16,16,128]{2,1,0:T(8,128)(2,1)S(1)}, u32[]{:S(2)}, u32[]{:S(2)}) %collective-permute-start.15) | collective-permute-done | bytes 65568 | tf_op jit(solution)/shard_map/ppermute | solution.py:331
  72.7 1.5 %collective-permute-done.16.rest_6_ = bf16[16,16,128]{2,1,0:T(8,128)(2,1)S(1)} collective-permute-done((bf16[16,16,128]{2,1,0:T(8,128)(2,1)S(1)}, bf16[16,16,128]{2,1,0:T(8,128)(2,1)S(1)}, u32[]{:S(2)}, u32[]{:S(2)}) %collective-permute-start.16) | collective-permute-done | bytes 65568 | tf_op jit(solution)/shard_map/ppermute | solution.py:331
  (54 shorter events, 8.9 us)
Async XLA Ops:
  0.0 25.6 %collective-permute-start.3 = (bf16[16,256,128]{2,1,0:T(8,128)(2,1)}, bf16[16,256,128]{2,1,0:T(8,128)(2,1)S(1)}, u32[]{:S(2)}, u32[]{:S(2)}) collective-permute-start(bf16[16,256,128]{2,1,0:T(8,128)(2,1)} %in_ref.1), channel_id=1, source_target_pairs={{0,0},{1,1},{2,2},{3,3},{4,8},{5,9},{6,10},{7,11},{8,4},{9,5},{10,... | collective-permute-start | bytes 3145736 | tf_op jit(solution)/shard_map/ppermute | solution.py:336
  3.1 6.9 %copy-start.3 = (bf16[128,128]{1,0:T(8,128)(2,1)S(1)}, bf16[128,128]{1,0:T(8,128)(2,1)}, u32[]{:S(2)}) copy-start(bf16[128,128]{1,0:T(8,128)(2,1)} %refs_5_.20) | copy-start | bytes 98308
  3.1 6.9 %copy-start.4 = (bf16[128,128]{1,0:T(8,128)(2,1)S(1)}, bf16[128,128]{1,0:T(8,128)(2,1)}, u32[]{:S(2)}) copy-start(bf16[128,128]{1,0:T(8,128)(2,1)} %refs_6_.16) | copy-start | bytes 98308
  3.2 17.5 %collective-permute-start = (bf16[8,256,128]{2,1,0:T(8,128)(2,1)S(1)}, bf16[8,256,128]{2,1,0:T(8,128)(2,1)S(1)}, u32[]{:S(2)}, u32[]{:S(2)}) collective-permute-start(bf16[8,256,128]{2,1,0:T(8,128)(2,1)S(1)} %get-tuple-element.31.refs_6_), channel_id=1, source_target_pairs={{0,4},{1,5},{2,6},{3,7},{4,0},{5,1},{6,2},{7,3},{8,12},{9,13},{10,... | collective-permute-start | bytes 1572872 | tf_op jit(solution)/shard_map/ppermute | solution.py:331
  7.9 15.6 %collective-permute-start.2 = (bf16[8,256,128]{2,1,0:T(8,128)(2,1)S(1)}, bf16[8,256,128]{2,1,0:T(8,128)(2,1)S(1)}, u32[]{:S(2)}, u32[]{:S(2)}) collective-permute-start(bf16[8,256,128]{2,1,0:T(8,128)(2,1)S(1)} %get-tuple-element.32.refs_7_), channel_id=1, source_target_pairs={{0,2},{1,3},{2,0},{3,1},{4,6},{5,7},{6,4},{7,5},{8,10},{9,11},{10,... | collective-permute-start | bytes 1572872 | tf_op jit(solution)/shard_map/ppermute | solution.py:331
  9.4 24.7 %collective-permute-start.4 = (bf16[8,256,128]{2,1,0:T(8,128)(2,1)S(1)}, bf16[8,256,128]{2,1,0:T(8,128)(2,1)}, u32[]{:S(2)}, u32[]{:S(2)}) collective-permute-start(bf16[8,256,128]{2,1,0:T(8,128)(2,1)S(1)} %get-tuple-element.31.refs_6_), channel_id=1, source_target_pairs={{0,2},{1,3},{2,0},{3,1},{4,6},{5,7},{6,4},{7,5},{8,10},{9,11},{10,... | collective-permute-start | bytes 1572872 | tf_op jit(solution)/shard_map/ppermute | solution.py:331
  9.9 26.1 %collective-permute-start.5 = (bf16[8,256,128]{2,1,0:T(8,128)(2,1)S(1)}, bf16[8,256,128]{2,1,0:T(8,128)(2,1)}, u32[]{:S(2)}, u32[]{:S(2)}) collective-permute-start(bf16[8,256,128]{2,1,0:T(8,128)(2,1)S(1)} %get-tuple-element.32.refs_7_), channel_id=1, source_target_pairs={{0,4},{1,5},{2,6},{3,7},{4,0},{5,1},{6,2},{7,3},{8,12},{9,13},{10,... | collective-permute-start | bytes 1572872 | tf_op jit(solution)/shard_map/ppermute | solution.py:331
  20.7 23.4 %collective-permute-start.7 = (bf16[8,256,128]{2,1,0:T(8,128)(2,1)S(1)}, bf16[8,256,128]{2,1,0:T(8,128)(2,1)S(1)}, u32[]{:S(2)}, u32[]{:S(2)}) collective-permute-start(bf16[8,256,128]{2,1,0:T(8,128)(2,1)S(1)} %hold.6.refs_7_), channel_id=1, source_target_pairs={{0,2},{1,3},{2,0},{3,1},{4,6},{5,7},{6,4},{7,5},{8,10},{9,11},{10,... | collective-permute-start | bytes 1572872 | tf_op jit(solution)/shard_map/ppermute | solution.py:331
  23.5 17.0 %collective-permute-start.1 = (bf16[8,256,128]{2,1,0:T(8,128)(2,1)S(1)}, bf16[8,256,128]{2,1,0:T(8,128)(2,1)S(1)}, u32[]{:S(2)}, u32[]{:S(2)}) collective-permute-start(bf16[8,256,128]{2,1,0:T(8,128)(2,1)S(1)} %hold.6.refs_7_), channel_id=1, source_target_pairs={{0,0},{1,1},{2,2},{3,3},{4,8},{5,9},{6,10},{7,11},{8,4},{9,5},{10,... | collective-permute-start | bytes 1572872 | tf_op jit(solution)/shard_map/ppermute | solution.py:336
  25.6 5.6 %copy-start = (bf16[128,128]{1,0:T(8,128)(2,1)S(1)}, bf16[128,128]{1,0:T(8,128)(2,1)}, u32[]{:S(2)}) copy-start(bf16[128,128]{1,0:T(8,128)(2,1)} %refs_5_.23) | copy-start | bytes 98308
  25.6 5.6 %copy-start.1 = (bf16[128,128]{1,0:T(8,128)(2,1)S(1)}, bf16[128,128]{1,0:T(8,128)(2,1)}, u32[]{:S(2)}) copy-start(bf16[128,128]{1,0:T(8,128)(2,1)} %refs_6_.19) | copy-start | bytes 98308
  25.6 18.5 %collective-permute-start.8 = (bf16[8,256,128]{2,1,0:T(8,128)(2,1)S(1)}, bf16[8,256,128]{2,1,0:T(8,128)(2,1)S(1)}, u32[]{:S(2)}, u32[]{:S(2)}) collective-permute-start(bf16[8,256,128]{2,1,0:T(8,128)(2,1)S(1)} %hold.10), channel_id=1, source_target_pairs={{0,4},{1,5},{2,6},{3,7},{4,0},{5,1},{6,2},{7,3},{8,12},{9,13},{10,... | collective-permute-start | bytes 1572872 | tf_op jit(solution)/shard_map/ppermute | solution.py:331
  34.1 4.0 %collective-permute-start.6 = (bf16[16,256,128]{2,1,0:T(8,128)(2,1)S(1)}, bf16[16,256,128]{2,1,0:T(8,128)(2,1)S(1)}, u32[]{:S(2)}, u32[]{:S(2)}) collective-permute-start(bf16[16,256,128]{2,1,0:T(8,128)(2,1)S(1)} %hold.7.refs_7_.refs_9_), channel_id=1, source_target_pairs={{0,1},{1,0},{2,3},{3,2},{4,5},{5,4},{6,7},{7,6},{8,9},{9,8},{10,11... | collective-permute-start | bytes 3145736 | tf_op jit(solution)/shard_map/ppermute | solution.py:331
  40.5 6.2 %collective-permute-start.9 = (bf16[8,256,128]{2,1,0:T(8,128)(2,1)S(1)}, bf16[8,256,128]{2,1,0:T(8,128)(2,1)S(1)}, u32[]{:S(2)}, u32[]{:S(2)}) collective-permute-start(bf16[8,256,128]{2,1,0:T(8,128)(2,1)S(1)} %hold.9.refs_6_.refs_11_), channel_id=1, source_target_pairs={{0,1},{1,0},{2,3},{3,2},{4,5},{5,4},{6,7},{7,6},{8,9},{9,8},{10,11... | collective-permute-start | bytes 1572872 | tf_op jit(solution)/shard_map/ppermute | solution.py:331
  41.1 15.0 %collective-permute-start.13 = (bf16[8,256,128]{2,1,0:T(8,128)(2,1)}, bf16[8,256,128]{2,1,0:T(8,128)(2,1)S(1)}, u32[]{:S(2)}, u32[]{:S(2)}) collective-permute-start(bf16[8,256,128]{2,1,0:T(8,128)(2,1)} %hold.8.refs_7_), channel_id=1, source_target_pairs={{0,0},{1,1},{2,2},{3,3},{4,8},{5,9},{6,10},{7,11},{8,4},{9,5},{10,... | collective-permute-start | bytes 1572872 | tf_op jit(solution)/shard_map/ppermute | solution.py:336
  46.7 1.4 %copy-start.6 = (bf16[128,128]{1,0:T(8,128)(2,1)S(1)}, bf16[128,128]{1,0:T(8,128)(2,1)}, u32[]{:S(2)}) copy-start(bf16[128,128]{1,0:T(8,128)(2,1)} %refs_3_.3) | copy-start | bytes 98308
  46.7 1.4 %copy-start.7 = (bf16[128,128]{1,0:T(8,128)(2,1)S(1)}, bf16[128,128]{1,0:T(8,128)(2,1)}, u32[]{:S(2)}) copy-start(bf16[128,128]{1,0:T(8,128)(2,1)} %refs_4_.7) | copy-start | bytes 98308
  56.2 5.2 %collective-permute-start.14 = (bf16[8,256,128]{2,1,0:T(8,128)(2,1)S(1)}, bf16[8,256,128]{2,1,0:T(8,128)(2,1)S(1)}, u32[]{:S(2)}, u32[]{:S(2)}) collective-permute-start(bf16[8,256,128]{2,1,0:T(8,128)(2,1)S(1)} %hold.11.refs_7_.refs_9_), channel_id=1, source_target_pairs={{0,1},{1,0},{2,3},{3,2},{4,5},{5,4},{6,7},{7,6},{8,9},{9,8},{10,11... | collective-permute-start | bytes 1572872 | tf_op jit(solution)/shard_map/ppermute | solution.py:331
  56.3 13.6 %collective-permute-start.10 = (bf16[48,16,128]{2,1,0:T(8,128)(2,1)S(1)}, bf16[48,16,128]{2,1,0:T(8,128)(2,1)S(1)}, u32[]{:S(2)}, u32[]{:S(2)}) collective-permute-start(bf16[48,16,128]{2,1,0:T(8,128)(2,1)S(1)} %get-tuple-element.46), channel_id=1, source_target_pairs={{0,6},{1,7},{2,4},{3,5},{4,2},{5,3},{6,0},{7,1},{8,14},{9,15},{10,... | collective-permute-start | bytes 589832 | tf_op jit(solution)/shard_map/ppermute | solution.py:331
  59.5 11.0 %collective-permute-start.11 = (bf16[48,16,128]{2,1,0:T(8,128)(2,1)S(1)}, bf16[48,16,128]{2,1,0:T(8,128)(2,1)S(1)}, u32[]{:S(2)}, u32[]{:S(2)}) collective-permute-start(bf16[48,16,128]{2,1,0:T(8,128)(2,1)S(1)} %get-tuple-element.47), channel_id=1, source_target_pairs={{0,4},{1,5},{2,6},{3,7},{4,0},{5,1},{6,2},{7,3},{8,12},{9,13},{10,... | collective-permute-start | bytes 589832 | tf_op jit(solution)/shard_map/ppermute | solution.py:331
  59.5 11.0 %collective-permute-start.12 = (bf16[48,16,128]{2,1,0:T(8,128)(2,1)S(1)}, bf16[48,16,128]{2,1,0:T(8,128)(2,1)S(1)}, u32[]{:S(2)}, u32[]{:S(2)}) collective-permute-start(bf16[48,16,128]{2,1,0:T(8,128)(2,1)S(1)} %get-tuple-element.48), channel_id=1, source_target_pairs={{0,2},{1,3},{2,0},{3,1},{4,6},{5,7},{6,4},{7,5},{8,10},{9,11},{10,... | collective-permute-start | bytes 589832 | tf_op jit(solution)/shard_map/ppermute | solution.py:331
  66.9 5.8 %collective-permute-start.15 = (bf16[16,16,128]{2,1,0:T(8,128)(2,1)S(1)}, bf16[16,16,128]{2,1,0:T(8,128)(2,1)S(1)}, u32[]{:S(2)}, u32[]{:S(2)}) collective-permute-start(bf16[16,16,128]{2,1,0:T(8,128)(2,1)S(1)} %get-tuple-element.54), channel_id=1, source_target_pairs={{0,6},{1,7},{2,4},{3,5},{4,2},{5,3},{6,0},{7,1},{8,14},{9,15},{10,... | collective-permute-start | bytes 196616 | tf_op jit(solution)/shard_map/ppermute | solution.py:331
  69.9 4.3 %collective-permute-start.16 = (bf16[16,16,128]{2,1,0:T(8,128)(2,1)S(1)}, bf16[16,16,128]{2,1,0:T(8,128)(2,1)S(1)}, u32[]{:S(2)}, u32[]{:S(2)}) collective-permute-start(bf16[16,16,128]{2,1,0:T(8,128)(2,1)S(1)} %get-tuple-element.55), channel_id=1, source_target_pairs={{0,4},{1,5},{2,6},{3,7},{4,0},{5,1},{6,2},{7,3},{8,12},{9,13},{10,... | collective-permute-start | bytes 196616 | tf_op jit(solution)/shard_map/ppermute | solution.py:331
  69.9 4.3 %collective-permute-start.17 = (bf16[16,16,128]{2,1,0:T(8,128)(2,1)S(1)}, bf16[16,16,128]{2,1,0:T(8,128)(2,1)S(1)}, u32[]{:S(2)}, u32[]{:S(2)}) collective-permute-start(bf16[16,16,128]{2,1,0:T(8,128)(2,1)S(1)} %get-tuple-element.56), channel_id=1, source_target_pairs={{0,2},{1,3},{2,0},{3,1},{4,6},{5,7},{6,4},{7,5},{8,10},{9,11},{10,... | collective-permute-start | bytes 196616 | tf_op jit(solution)/shard_map/ppermute | solution.py:331
  (4 other events, 3.2 us)

commit v8 on v7

--- a/solution.py
+++ b/solution.py
@@ -142,7 +142,7 @@
         return total + product
 
     zeros = jnp.zeros((deep, fold * span), WIDE_TYPE)
-    mean_value = lax.fori_loop(0, hidden, multiply, zeros, unroll=16) * (1.0 / hidden)
+    mean_value = lax.fori_loop(0, hidden, multiply, zeros, unroll=64) * (1.0 / hidden)
 
     def spread(h, total):
         at = pl.multiple_of(h * deep, deep)

time: 75.9 us -> 74.5 us (0.982)
  Pallas kernels: 34.5 us -> 33.1 us
    pallas_call x2, Pallas kernels: 11.6 us -> 10.2 us  [triangle_call(): pl.pallas_call(behind(functools.partial(triangle_kernel, len(pairs), orde...]
  transfers between devices with their start and end apart: 18 -> 18, of which waited for: 4 -> 4; matrix products, arithmetic and copies ran while one was open for 0% -> 0% of each run, Pallas kernels for 44% -> 43%
where the time goes in v8:
time: 74.5 us; the launch traced here: 74.1 us
  Pallas kernels  33.1 us (44%)
  starting transfers between devices  26.3 us (35%)
  waiting for transfers between devices  11.7 us (16%)
  local copies, waits for them, and re-layouts  2.56 us (3%)
    ppermute x15, starting transfers between devices, swap(): return lax.ppermute(values, 'wide', [(d, d ^ mask) for d in range(count)])  22 us
    pallas_call x8, Pallas kernels, left_call(): pl.pallas_call(behind(functools.partial(left_kernel, unit, base, span, of...  12.7 us
    ppermute x15, waiting for transfers between devices, swap(): return lax.ppermute(values, 'wide', [(d, d ^ mask) for d in range(count)])  11.7 us
    pallas_call x2, Pallas kernels, triangle_call(): pl.pallas_call(behind(functools.partial(triangle_kernel, len(pairs), orde...  10.2 us
    pallas_call x4, Pallas kernels, edge_call(): pl.pallas_call(behind(functools.partial(edge_kernel, unit, offset, len(pa...  8.98 us
    ppermute x3, starting transfers between devices, cross(): return lax.ppermute(values, 'wide', pairs)  4.25 us
    unnamed x20, local copies, waits for them, and re-layouts  2.56 us
  transfers between devices with their start and end apart: 18, of which 4 were waited for; matrix products, arithmetic and copies ran while one was open for 0% of the time, Pallas kernels for 43%

profile of v8, /device:TPU:0, one launch (start us, length us, event | category | flops | bytes accessed | tf_op | source)
XLA Modules:
  0.0 74.1 jit_solution(15891850846347575265)
XLA Ops:
  0.0 1.9 %collective-permute-start.3 = (bf16[16,256,128]{2,1,0:T(8,128)(2,1)}, bf16[16,256,128]{2,1,0:T(8,128)(2,1)S(1)}, u32[]{:S(2)}, u32[]{:S(2)}) collective-permute-start(bf16[16,256,128]{2,1,0:T(8,128)(2,1)} %in_ref.1), channel_id=1, source_target_pairs={{0,0},{1,1},{2,2},{3,3},{4,8},{5,9},{6,10},{7,11},{8,4},{9,5},{10,... | collective-permute-start | bytes 3145736 | tf_op jit(solution)/shard_map/ppermute | solution.py:336
  3.2 4.7 %collective-permute-start = (bf16[8,256,128]{2,1,0:T(8,128)(2,1)S(1)}, bf16[8,256,128]{2,1,0:T(8,128)(2,1)S(1)}, u32[]{:S(2)}, u32[]{:S(2)}) collective-permute-start(bf16[8,256,128]{2,1,0:T(8,128)(2,1)S(1)} %get-tuple-element.31.refs_6_), channel_id=1, source_target_pairs={{0,4},{1,5},{2,6},{3,7},{4,0},{5,1},{6,2},{7,3},{8,12},{9,13},{10,... | collective-permute-start | bytes 1572872 | tf_op jit(solution)/shard_map/ppermute | solution.py:331
  7.9 1.5 %collective-permute-start.2 = (bf16[8,256,128]{2,1,0:T(8,128)(2,1)S(1)}, bf16[8,256,128]{2,1,0:T(8,128)(2,1)S(1)}, u32[]{:S(2)}, u32[]{:S(2)}) collective-permute-start(bf16[8,256,128]{2,1,0:T(8,128)(2,1)S(1)} %get-tuple-element.32.refs_7_), channel_id=1, source_target_pairs={{0,2},{1,3},{2,0},{3,1},{4,6},{5,7},{6,4},{7,5},{8,10},{9,11},{10,... | collective-permute-start | bytes 1572872 | tf_op jit(solution)/shard_map/ppermute | solution.py:331
  10.7 2.5 %edges.4.refs_1_.refs_0_.refs_5_ = bf16[128,16,256]{2,1,0:T(8,128)(2,1)S(1)} custom-call(s32[1]{0:T(128)} %bitcast.refs_0_.refs_1_.me_ref, s32[256]{0:T(256)S(1)} %copy-done.5, s32[1,256]{1,0:T(1,128)S(1)} %bitcast.3, f32[1,128]{1,0:T(1,128)S(1)} %bitcast.15, bf16[128,128]{1,0:T(8,128)(2,1)S(1)} %copy-done.3, bf16[128,128]{1,0:T(8,128)(2,1)S(1)} %copy-done.4, ...), custom_call_target="tpu_custom_call" | custom-call | flops 1048576 | bytes 1024 | tf_op jit(solution)/shard_map/edges/pallas_call | solution.py:221
  13.2 7.5 %collective-permute-done.refs_0_ = bf16[8,256,128]{2,1,0:T(8,128)(2,1)S(1)} collective-permute-done((bf16[8,256,128]{2,1,0:T(8,128)(2,1)S(1)}, bf16[8,256,128]{2,1,0:T(8,128)(2,1)S(1)}, u32[]{:S(2)}, u32[]{:S(2)}) %collective-permute-start) | collective-permute-done | bytes 524320 | tf_op jit(solution)/shard_map/ppermute | solution.py:331
  20.7 1.5 %collective-permute-start.7 = (bf16[8,256,128]{2,1,0:T(8,128)(2,1)S(1)}, bf16[8,256,128]{2,1,0:T(8,128)(2,1)S(1)}, u32[]{:S(2)}, u32[]{:S(2)}) collective-permute-start(bf16[8,256,128]{2,1,0:T(8,128)(2,1)S(1)} %hold.6.refs_7_), channel_id=1, source_target_pairs={{0,2},{1,3},{2,0},{3,1},{4,6},{5,7},{6,4},{7,5},{8,10},{9,11},{10,... | collective-permute-start | bytes 1572872 | tf_op jit(solution)/shard_map/ppermute | solution.py:331
  24.2 1.3 %left_edges.9 = (f32[1024,128]{1,0:T(8,128)S(1)}, f32[1024,128]{1,0:T(8,128)S(1)}) custom-call(f32[1024,128]{1,0:T(8,128)S(1)} %get-tuple-element.33.refs_0_.refs_8_, s32[1]{0:T(128)} %bitcast.refs_0_.refs_1_.me_ref, s32[256]{0:T(256)S(1)} %copy-done.5, s32[1,256]{1,0:T(1,128)S(1)} %bitcast.5, f32[1,128]{1,0:T(1,128)S(1)} %bitcast.17, ...), custom_call_target="tpu_custom_call" | custom-call | flops 1048576 | bytes 1024 | tf_op jit(solution)/shard_map/left_edges/pallas_call | solution.py:238
  25.6 5.5 %collective-permute-start.8 = (bf16[8,256,128]{2,1,0:T(8,128)(2,1)S(1)}, bf16[8,256,128]{2,1,0:T(8,128)(2,1)S(1)}, u32[]{:S(2)}, u32[]{:S(2)}) collective-permute-start(bf16[8,256,128]{2,1,0:T(8,128)(2,1)S(1)} %hold.10), channel_id=1, source_target_pairs={{0,4},{1,5},{2,6},{3,7},{4,0},{5,1},{6,2},{7,3},{8,12},{9,13},{10,... | collective-permute-start | bytes 1572872 | tf_op jit(solution)/shard_map/ppermute | solution.py:331
  31.2 2.4 %left_edges.10 = (f32[2048,128]{1,0:T(8,128)S(1)}, f32[2048,128]{1,0:T(8,128)S(1)}) custom-call(f32[1024,128]{1,0:T(8,128)S(1)} %get-tuple-element.34.refs_1_.refs_0_.refs_8_, s32[1]{0:T(128)} %bitcast.refs_0_.refs_1_.me_ref, s32[256]{0:T(256)S(1)} %copy-done.5, s32[1,256]{1,0:T(1,128)S(1)} %bitcast.6, f32[1,128]{1,0:T(1,128)S(1)} %bitcast.18, ...), custom_call_target="tpu_custom_call" | custom-call | flops 1048576 | bytes 1024 | tf_op jit(solution)/shard_map/left_edges/pallas_call | solution.py:238
  34.1 1.9 %edges.5.refs_1_.refs_0_.refs_8_ = bf16[128,16,256]{2,1,0:T(8,128)(2,1)S(1)} custom-call(f32[2048,128]{1,0:T(8,128)S(1)} %get-tuple-element.35.refs_0_.refs_13_, s32[1]{0:T(128)} %bitcast.refs_0_.refs_1_.me_ref, s32[256]{0:T(256)S(1)} %copy-done.5, s32[1,256]{1,0:T(1,128)S(1)} %bitcast.7, f32[1,128]{1,0:T(1,128)S(1)} %bitcast.19, ...), custom_call_target="tpu_custom_call" | custom-call | flops 1048576 | bytes 1024 | tf_op jit(solution)/shard_map/edges/pallas_call | solution.py:221
  36.1 2.0 %edges.6.refs_0_.refs_7_ = bf16[128,16,256]{2,1,0:T(8,128)(2,1)S(1)} custom-call(bf16[128,16,256]{2,1,0:T(8,128)(2,1)S(1)} %edges.5.refs_1_.refs_0_.refs_8_, s32[1]{0:T(128)} %bitcast.refs_0_.refs_1_.me_ref, s32[256]{0:T(256)S(1)} %copy-done.5, s32[1,256]{1,0:T(1,128)S(1)} %bitcast.8, f32[1,128]{1,0:T(1,128)S(1)} %bitcast.20, ...), custom_call_target="tpu_custom_call" | custom-call | flops 34359738368 | bytes 1024 | tf_op jit(solution)/shard_map/edges/pallas_call | solution.py:221
  38.1 2.4 %left_edges.11 = (f32[2048,128]{1,0:T(8,128)S(1)}, f32[2048,128]{1,0:T(8,128)S(1)}) custom-call(bf16[128,16,256]{2,1,0:T(8,128)(2,1)S(1)} %edges.6.refs_0_.refs_7_, s32[1]{0:T(128)} %bitcast.refs_0_.refs_1_.me_ref, s32[256]{0:T(256)S(1)} %copy-done.5, s32[1,256]{1,0:T(1,128)S(1)} %bitcast.9, f32[1,128]{1,0:T(1,128)S(1)} %bitcast.21, ...), custom_call_target="tpu_custom_call" | custom-call | flops 1048576 | bytes 1024 | tf_op jit(solution)/shard_map/left_edges/pallas_call | solution.py:238
  41.1 1.7 %collective-permute-start.13 = (bf16[8,256,128]{2,1,0:T(8,128)(2,1)}, bf16[8,256,128]{2,1,0:T(8,128)(2,1)S(1)}, u32[]{:S(2)}, u32[]{:S(2)}) collective-permute-start(bf16[8,256,128]{2,1,0:T(8,128)(2,1)} %hold.8.refs_7_), channel_id=1, source_target_pairs={{0,0},{1,1},{2,2},{3,3},{4,8},{5,9},{6,10},{7,11},{8,4},{9,5},{10,... | collective-permute-start | bytes 1572872 | tf_op jit(solution)/shard_map/ppermute | solution.py:336
  42.8 1.3 %left_edges.12 = (f32[1024,128]{1,0:T(8,128)S(1)}, f32[1024,128]{1,0:T(8,128)S(1)}) custom-call(s32[1]{0:T(128)} %bitcast.refs_0_.refs_1_.me_ref, s32[256]{0:T(256)S(1)} %copy-done.5, s32[1,256]{1,0:T(1,128)S(1)} %bitcast.10, f32[1,128]{1,0:T(1,128)S(1)} %bitcast.22, bf16[128,128]{1,0:T(8,128)(2,1)S(1)} %copy-done, bf16[128,128]{1,0:T(8,128)(2,1)S(1)} %copy-done.1, ...), custom_call_target="tpu_custom_call" | custom-call | flops 1048576 | bytes 1024 | tf_op jit(solution)/shard_map/left_edges/pallas_call | solution.py:238
  44.2 2.5 %edges.7.refs_0_.refs_6_ = bf16[128,16,256]{2,1,0:T(8,128)(2,1)S(1)} custom-call(f32[1024,128]{1,0:T(8,128)S(1)} %get-tuple-element.39.refs_0_.refs_17_, s32[1]{0:T(128)} %bitcast.refs_0_.refs_1_.me_ref, s32[256]{0:T(256)S(1)} %copy-done.5, s32[1,256]{1,0:T(1,128)S(1)} %bitcast.11, f32[1,128]{1,0:T(1,128)S(1)} %bitcast.23, bf16[128,128]{1,0:T(8,128)(2,1)S(1)} %copy-done.3, ...), custom_call_target="tpu_custom_call" | custom-call | flops 1048576 | bytes 1024 | tf_op jit(solution)/shard_map/edges/pallas_call | solution.py:221
  46.7 1.3 %left_edges.13 = (f32[1024,128]{1,0:T(8,128)S(1)}, f32[1024,128]{1,0:T(8,128)S(1)}) custom-call(bf16[128,16,256]{2,1,0:T(8,128)(2,1)S(1)} %edges.7.refs_0_.refs_6_, s32[1]{0:T(128)} %bitcast.refs_0_.refs_1_.me_ref, s32[256]{0:T(256)S(1)} %copy-done.5, s32[1,256]{1,0:T(1,128)S(1)} %bitcast.12, f32[1,128]{1,0:T(1,128)S(1)} %bitcast.24, ...), custom_call_target="tpu_custom_call" | custom-call | flops 1048576 | bytes 1024 | tf_op jit(solution)/shard_map/left_edges/pallas_call | solution.py:238
  48.7 6.8 %triangle.2 = (bf16[48,16,128]{2,1,0:T(8,128)(2,1)S(1)}, bf16[48,16,128]{2,1,0:T(8,128)(2,1)S(1)}, bf16[48,16,128]{2,1,0:T(8,128)(2,1)S(1)}, bf16[48,16,128]{2,1,0:T(8,128)(2,1)S(1)}) custom-call(s32[1]{0:T(128)} %bitcast.refs_0_.refs_1_.me_ref, f32[128]{0:T(128)S(1)} %copy-done.9, f32[1,128]{1,0:T(1,128)S(1)} %bitcast.25, bf16[128,128]{1,0:T(8,128)(2,1)S(1)} %copy-done.6, ...), custom_call_target="tpu_custom_call" | custom-call | flops 1048576 | bytes 1024 | tf_op jit(solution)/shard_map/triangle/pallas_call | solution.py:257
  55.6 3.3 %collective-permute-start.10 = (bf16[48,16,128]{2,1,0:T(8,128)(2,1)S(1)}, bf16[48,16,128]{2,1,0:T(8,128)(2,1)S(1)}, u32[]{:S(2)}, u32[]{:S(2)}) collective-permute-start(bf16[48,16,128]{2,1,0:T(8,128)(2,1)S(1)} %get-tuple-element.46), channel_id=1, source_target_pairs={{0,6},{1,7},{2,4},{3,5},{4,2},{5,3},{6,0},{7,1},{8,14},{9,15},{10,... | collective-permute-start | bytes 589832 | tf_op jit(solution)/shard_map/ppermute | solution.py:331
  59.5 1.3 %left_edges.14 = (f32[1024,128]{1,0:T(8,128)S(1)}, f32[1024,128]{1,0:T(8,128)S(1)}) custom-call(bf16[48,16,128]{2,1,0:T(8,128)(2,1)S(1)} %get-tuple-element.45.refs_1_.refs_0_.rest_0_, s32[1]{0:T(128)} %bitcast.refs_0_.refs_1_.me_ref, s32[256]{0:T(256)S(1)} %copy-done.5, s32[1,256]{1,0:T(1,128)S(1)} %bitcast.13, f32[1,128]{1,0:T(1,128)S(1)} %bitcast.26, ...), custom_call_target="tpu_custom_call" | custom-call | flops 1048576 | bytes 1024 | tf_op jit(solution)/shard_map/left_edges/pallas_call | solution.py:238
  60.8 1.3 %left_edges.15 = (f32[1024,128]{1,0:T(8,128)S(1)}, f32[1024,128]{1,0:T(8,128)S(1)}) custom-call(f32[1024,128]{1,0:T(8,128)S(1)} %get-tuple-element.49.refs_0_.refs_11_, s32[1]{0:T(128)} %bitcast.refs_0_.refs_1_.me_ref, s32[256]{0:T(256)S(1)} %copy-done.5, s32[1,256]{1,0:T(1,128)S(1)} %bitcast.14, f32[1,128]{1,0:T(1,128)S(1)} %bitcast.27, ...), custom_call_target="tpu_custom_call" | custom-call | flops 1048576 | bytes 1024 | tf_op jit(solution)/shard_map/left_edges/pallas_call | solution.py:238
  62.1 3.4 %triangle.3 = (bf16[16,16,128]{2,1,0:T(8,128)(2,1)S(1)}, bf16[16,16,128]{2,1,0:T(8,128)(2,1)S(1)}, bf16[16,16,128]{2,1,0:T(8,128)(2,1)S(1)}, bf16[16,16,128]{2,1,0:T(8,128)(2,1)S(1)}) custom-call(s32[1]{0:T(128)} %bitcast.refs_0_.refs_1_.me_ref, f32[128]{0:T(128)S(1)} %copy-done.9, f32[1,128]{1,0:T(1,128)S(1)} %bitcast.28, bf16[128,128]{1,0:T(8,128)(2,1)S(1)} %copy-done.6, ...), custom_call_target="tpu_custom_call" | custom-call | flops 1048576 | bytes 1024 | tf_op jit(solution)/shard_map/triangle/pallas_call | solution.py:257
  65.5 3.0 %collective-permute-start.15 = (bf16[16,16,128]{2,1,0:T(8,128)(2,1)S(1)}, bf16[16,16,128]{2,1,0:T(8,128)(2,1)S(1)}, u32[]{:S(2)}, u32[]{:S(2)}) collective-permute-start(bf16[16,16,128]{2,1,0:T(8,128)(2,1)S(1)} %get-tuple-element.54), channel_id=1, source_target_pairs={{0,6},{1,7},{2,4},{3,5},{4,2},{5,3},{6,0},{7,1},{8,14},{9,15},{10,... | collective-permute-start | bytes 196616 | tf_op jit(solution)/shard_map/ppermute | solution.py:331
  69.2 2.2 %collective-permute-done.15.rest_5_ = bf16[16,16,128]{2,1,0:T(8,128)(2,1)S(1)} collective-permute-done((bf16[16,16,128]{2,1,0:T(8,128)(2,1)S(1)}, bf16[16,16,128]{2,1,0:T(8,128)(2,1)S(1)}, u32[]{:S(2)}, u32[]{:S(2)}) %collective-permute-start.15) | collective-permute-done | bytes 65568 | tf_op jit(solution)/shard_map/ppermute | solution.py:331
  71.3 1.5 %collective-permute-done.16.rest_6_ = bf16[16,16,128]{2,1,0:T(8,128)(2,1)S(1)} collective-permute-done((bf16[16,16,128]{2,1,0:T(8,128)(2,1)S(1)}, bf16[16,16,128]{2,1,0:T(8,128)(2,1)S(1)}, u32[]{:S(2)}, u32[]{:S(2)}) %collective-permute-start.16) | collective-permute-done | bytes 65568 | tf_op jit(solution)/shard_map/ppermute | solution.py:331
  (54 shorter events, 8.9 us)
Async XLA Ops:
  0.0 25.6 %collective-permute-start.3 = (bf16[16,256,128]{2,1,0:T(8,128)(2,1)}, bf16[16,256,128]{2,1,0:T(8,128)(2,1)S(1)}, u32[]{:S(2)}, u32[]{:S(2)}) collective-permute-start(bf16[16,256,128]{2,1,0:T(8,128)(2,1)} %in_ref.1), channel_id=1, source_target_pairs={{0,0},{1,1},{2,2},{3,3},{4,8},{5,9},{6,10},{7,11},{8,4},{9,5},{10,... | collective-permute-start | bytes 3145736 | tf_op jit(solution)/shard_map/ppermute | solution.py:336
  3.1 6.9 %copy-start.3 = (bf16[128,128]{1,0:T(8,128)(2,1)S(1)}, bf16[128,128]{1,0:T(8,128)(2,1)}, u32[]{:S(2)}) copy-start(bf16[128,128]{1,0:T(8,128)(2,1)} %refs_5_.20) | copy-start | bytes 98308
  3.1 6.9 %copy-start.4 = (bf16[128,128]{1,0:T(8,128)(2,1)S(1)}, bf16[128,128]{1,0:T(8,128)(2,1)}, u32[]{:S(2)}) copy-start(bf16[128,128]{1,0:T(8,128)(2,1)} %refs_6_.16) | copy-start | bytes 98308
  3.2 17.5 %collective-permute-start = (bf16[8,256,128]{2,1,0:T(8,128)(2,1)S(1)}, bf16[8,256,128]{2,1,0:T(8,128)(2,1)S(1)}, u32[]{:S(2)}, u32[]{:S(2)}) collective-permute-start(bf16[8,256,128]{2,1,0:T(8,128)(2,1)S(1)} %get-tuple-element.31.refs_6_), channel_id=1, source_target_pairs={{0,4},{1,5},{2,6},{3,7},{4,0},{5,1},{6,2},{7,3},{8,12},{9,13},{10,... | collective-permute-start | bytes 1572872 | tf_op jit(solution)/shard_map/ppermute | solution.py:331
  7.9 15.6 %collective-permute-start.2 = (bf16[8,256,128]{2,1,0:T(8,128)(2,1)S(1)}, bf16[8,256,128]{2,1,0:T(8,128)(2,1)S(1)}, u32[]{:S(2)}, u32[]{:S(2)}) collective-permute-start(bf16[8,256,128]{2,1,0:T(8,128)(2,1)S(1)} %get-tuple-element.32.refs_7_), channel_id=1, source_target_pairs={{0,2},{1,3},{2,0},{3,1},{4,6},{5,7},{6,4},{7,5},{8,10},{9,11},{10,... | collective-permute-start | bytes 1572872 | tf_op jit(solution)/shard_map/ppermute | solution.py:331
  9.4 24.7 %collective-permute-start.4 = (bf16[8,256,128]{2,1,0:T(8,128)(2,1)S(1)}, bf16[8,256,128]{2,1,0:T(8,128)(2,1)}, u32[]{:S(2)}, u32[]{:S(2)}) collective-permute-start(bf16[8,256,128]{2,1,0:T(8,128)(2,1)S(1)} %get-tuple-element.31.refs_6_), channel_id=1, source_target_pairs={{0,2},{1,3},{2,0},{3,1},{4,6},{5,7},{6,4},{7,5},{8,10},{9,11},{10,... | collective-permute-start | bytes 1572872 | tf_op jit(solution)/shard_map/ppermute | solution.py:331
  9.9 26.1 %collective-permute-start.5 = (bf16[8,256,128]{2,1,0:T(8,128)(2,1)S(1)}, bf16[8,256,128]{2,1,0:T(8,128)(2,1)}, u32[]{:S(2)}, u32[]{:S(2)}) collective-permute-start(bf16[8,256,128]{2,1,0:T(8,128)(2,1)S(1)} %get-tuple-element.32.refs_7_), channel_id=1, source_target_pairs={{0,4},{1,5},{2,6},{3,7},{4,0},{5,1},{6,2},{7,3},{8,12},{9,13},{10,... | collective-permute-start | bytes 1572872 | tf_op jit(solution)/shard_map/ppermute | solution.py:331
  20.7 23.4 %collective-permute-start.7 = (bf16[8,256,128]{2,1,0:T(8,128)(2,1)S(1)}, bf16[8,256,128]{2,1,0:T(8,128)(2,1)S(1)}, u32[]{:S(2)}, u32[]{:S(2)}) collective-permute-start(bf16[8,256,128]{2,1,0:T(8,128)(2,1)S(1)} %hold.6.refs_7_), channel_id=1, source_target_pairs={{0,2},{1,3},{2,0},{3,1},{4,6},{5,7},{6,4},{7,5},{8,10},{9,11},{10,... | collective-permute-start | bytes 1572872 | tf_op jit(solution)/shard_map/ppermute | solution.py:331
  23.5 17.0 %collective-permute-start.1 = (bf16[8,256,128]{2,1,0:T(8,128)(2,1)S(1)}, bf16[8,256,128]{2,1,0:T(8,128)(2,1)S(1)}, u32[]{:S(2)}, u32[]{:S(2)}) collective-permute-start(bf16[8,256,128]{2,1,0:T(8,128)(2,1)S(1)} %hold.6.refs_7_), channel_id=1, source_target_pairs={{0,0},{1,1},{2,2},{3,3},{4,8},{5,9},{6,10},{7,11},{8,4},{9,5},{10,... | collective-permute-start | bytes 1572872 | tf_op jit(solution)/shard_map/ppermute | solution.py:336
  25.6 5.6 %copy-start = (bf16[128,128]{1,0:T(8,128)(2,1)S(1)}, bf16[128,128]{1,0:T(8,128)(2,1)}, u32[]{:S(2)}) copy-start(bf16[128,128]{1,0:T(8,128)(2,1)} %refs_5_.23) | copy-start | bytes 98308
  25.6 5.6 %copy-start.1 = (bf16[128,128]{1,0:T(8,128)(2,1)S(1)}, bf16[128,128]{1,0:T(8,128)(2,1)}, u32[]{:S(2)}) copy-start(bf16[128,128]{1,0:T(8,128)(2,1)} %refs_6_.19) | copy-start | bytes 98308
  25.6 18.5 %collective-permute-start.8 = (bf16[8,256,128]{2,1,0:T(8,128)(2,1)S(1)}, bf16[8,256,128]{2,1,0:T(8,128)(2,1)S(1)}, u32[]{:S(2)}, u32[]{:S(2)}) collective-permute-start(bf16[8,256,128]{2,1,0:T(8,128)(2,1)S(1)} %hold.10), channel_id=1, source_target_pairs={{0,4},{1,5},{2,6},{3,7},{4,0},{5,1},{6,2},{7,3},{8,12},{9,13},{10,... | collective-permute-start | bytes 1572872 | tf_op jit(solution)/shard_map/ppermute | solution.py:331
  34.1 4.0 %collective-permute-start.6 = (bf16[16,256,128]{2,1,0:T(8,128)(2,1)S(1)}, bf16[16,256,128]{2,1,0:T(8,128)(2,1)S(1)}, u32[]{:S(2)}, u32[]{:S(2)}) collective-permute-start(bf16[16,256,128]{2,1,0:T(8,128)(2,1)S(1)} %hold.7.refs_7_.refs_9_), channel_id=1, source_target_pairs={{0,1},{1,0},{2,3},{3,2},{4,5},{5,4},{6,7},{7,6},{8,9},{9,8},{10,11... | collective-permute-start | bytes 3145736 | tf_op jit(solution)/shard_map/ppermute | solution.py:331
  40.5 6.2 %collective-permute-start.9 = (bf16[8,256,128]{2,1,0:T(8,128)(2,1)S(1)}, bf16[8,256,128]{2,1,0:T(8,128)(2,1)S(1)}, u32[]{:S(2)}, u32[]{:S(2)}) collective-permute-start(bf16[8,256,128]{2,1,0:T(8,128)(2,1)S(1)} %hold.9.refs_6_.refs_11_), channel_id=1, source_target_pairs={{0,1},{1,0},{2,3},{3,2},{4,5},{5,4},{6,7},{7,6},{8,9},{9,8},{10,11... | collective-permute-start | bytes 1572872 | tf_op jit(solution)/shard_map/ppermute | solution.py:331
  41.1 14.4 %collective-permute-start.13 = (bf16[8,256,128]{2,1,0:T(8,128)(2,1)}, bf16[8,256,128]{2,1,0:T(8,128)(2,1)S(1)}, u32[]{:S(2)}, u32[]{:S(2)}) collective-permute-start(bf16[8,256,128]{2,1,0:T(8,128)(2,1)} %hold.8.refs_7_), channel_id=1, source_target_pairs={{0,0},{1,1},{2,2},{3,3},{4,8},{5,9},{6,10},{7,11},{8,4},{9,5},{10,... | collective-permute-start | bytes 1572872 | tf_op jit(solution)/shard_map/ppermute | solution.py:336
  46.7 1.4 %copy-start.6 = (bf16[128,128]{1,0:T(8,128)(2,1)S(1)}, bf16[128,128]{1,0:T(8,128)(2,1)}, u32[]{:S(2)}) copy-start(bf16[128,128]{1,0:T(8,128)(2,1)} %refs_3_.3) | copy-start | bytes 98308
  46.7 1.4 %copy-start.7 = (bf16[128,128]{1,0:T(8,128)(2,1)S(1)}, bf16[128,128]{1,0:T(8,128)(2,1)}, u32[]{:S(2)}) copy-start(bf16[128,128]{1,0:T(8,128)(2,1)} %refs_4_.7) | copy-start | bytes 98308
  55.5 5.2 %collective-permute-start.14 = (bf16[8,256,128]{2,1,0:T(8,128)(2,1)S(1)}, bf16[8,256,128]{2,1,0:T(8,128)(2,1)S(1)}, u32[]{:S(2)}, u32[]{:S(2)}) collective-permute-start(bf16[8,256,128]{2,1,0:T(8,128)(2,1)S(1)} %hold.11.refs_7_.refs_9_), channel_id=1, source_target_pairs={{0,1},{1,0},{2,3},{3,2},{4,5},{5,4},{6,7},{7,6},{8,9},{9,8},{10,11... | collective-permute-start | bytes 1572872 | tf_op jit(solution)/shard_map/ppermute | solution.py:331
  55.6 12.9 %collective-permute-start.10 = (bf16[48,16,128]{2,1,0:T(8,128)(2,1)S(1)}, bf16[48,16,128]{2,1,0:T(8,128)(2,1)S(1)}, u32[]{:S(2)}, u32[]{:S(2)}) collective-permute-start(bf16[48,16,128]{2,1,0:T(8,128)(2,1)S(1)} %get-tuple-element.46), channel_id=1, source_target_pairs={{0,6},{1,7},{2,4},{3,5},{4,2},{5,3},{6,0},{7,1},{8,14},{9,15},{10,... | collective-permute-start | bytes 589832 | tf_op jit(solution)/shard_map/ppermute | solution.py:331
  58.9 10.3 %collective-permute-start.11 = (bf16[48,16,128]{2,1,0:T(8,128)(2,1)S(1)}, bf16[48,16,128]{2,1,0:T(8,128)(2,1)S(1)}, u32[]{:S(2)}, u32[]{:S(2)}) collective-permute-start(bf16[48,16,128]{2,1,0:T(8,128)(2,1)S(1)} %get-tuple-element.47), channel_id=1, source_target_pairs={{0,4},{1,5},{2,6},{3,7},{4,0},{5,1},{6,2},{7,3},{8,12},{9,13},{10,... | collective-permute-start | bytes 589832 | tf_op jit(solution)/shard_map/ppermute | solution.py:331
  58.9 10.3 %collective-permute-start.12 = (bf16[48,16,128]{2,1,0:T(8,128)(2,1)S(1)}, bf16[48,16,128]{2,1,0:T(8,128)(2,1)S(1)}, u32[]{:S(2)}, u32[]{:S(2)}) collective-permute-start(bf16[48,16,128]{2,1,0:T(8,128)(2,1)S(1)} %get-tuple-element.48), channel_id=1, source_target_pairs={{0,2},{1,3},{2,0},{3,1},{4,6},{5,7},{6,4},{7,5},{8,10},{9,11},{10,... | collective-permute-start | bytes 589832 | tf_op jit(solution)/shard_map/ppermute | solution.py:331
  65.5 5.8 %collective-permute-start.15 = (bf16[16,16,128]{2,1,0:T(8,128)(2,1)S(1)}, bf16[16,16,128]{2,1,0:T(8,128)(2,1)S(1)}, u32[]{:S(2)}, u32[]{:S(2)}) collective-permute-start(bf16[16,16,128]{2,1,0:T(8,128)(2,1)S(1)} %get-tuple-element.54), channel_id=1, source_target_pairs={{0,6},{1,7},{2,4},{3,5},{4,2},{5,3},{6,0},{7,1},{8,14},{9,15},{10,... | collective-permute-start | bytes 196616 | tf_op jit(solution)/shard_map/ppermute | solution.py:331
  68.5 4.3 %collective-permute-start.16 = (bf16[16,16,128]{2,1,0:T(8,128)(2,1)S(1)}, bf16[16,16,128]{2,1,0:T(8,128)(2,1)S(1)}, u32[]{:S(2)}, u32[]{:S(2)}) collective-permute-start(bf16[16,16,128]{2,1,0:T(8,128)(2,1)S(1)} %get-tuple-element.55), channel_id=1, source_target_pairs={{0,4},{1,5},{2,6},{3,7},{4,0},{5,1},{6,2},{7,3},{8,12},{9,13},{10,... | collective-permute-start | bytes 196616 | tf_op jit(solution)/shard_map/ppermute | solution.py:331
  68.5 4.3 %collective-permute-start.17 = (bf16[16,16,128]{2,1,0:T(8,128)(2,1)S(1)}, bf16[16,16,128]{2,1,0:T(8,128)(2,1)S(1)}, u32[]{:S(2)}, u32[]{:S(2)}) collective-permute-start(bf16[16,16,128]{2,1,0:T(8,128)(2,1)S(1)} %get-tuple-element.56), channel_id=1, source_target_pairs={{0,2},{1,3},{2,0},{3,1},{4,6},{5,7},{6,4},{7,5},{8,10},{9,11},{10,... | collective-permute-start | bytes 196616 | tf_op jit(solution)/shard_map/ppermute | solution.py:331
  (4 other events, 3.2 us)
